TPU v7x, 32 devices: a whole 2x2x4 slice. The times are simulated.
32 devices in a mesh: dp: 16 (over z, y, core), mp: 2 (over x).
Axes of the slice: x: 2, y: 2, z: 4, core: 2. Of those that a mesh axis runs over, the one named last changes fastest.
Arguments:
- byte_ids: int32 [2, 16384, 8], P(None, ('dp', 'mp')), may hold values from 0 to 255
- segment_ids: int32 [2, 16384], P(None, ('dp', 'mp')), may hold values from 0 to 1023, as said below
- embed_table: bfloat16 [256, 1024], P('dp'), may hold values from -6 to 6
- patch_weight: bfloat16 [8192, 1024], P('mp', 'dp'), may hold values from -0.0625 to 0.0625
- norm1_gain: float32 [1024], replicated, may hold values from 0.5 to 1.5
- mamba_in: bfloat16 [1024, 2, 2048], P('dp', None, 'mp'), may hold values from -0.1875 to 0.1875
- mamba_dt: bfloat16 [1024, 32], P('dp', 'mp'), may hold values from -0.1875 to 0.1875
- mamba_bc: bfloat16 [1024, 256], P('dp'), may hold values from -0.1875 to 0.1875
- conv_x: float32 [4, 2048], P(None, 'mp'), may hold values from -3 to 3
- conv_bc: float32 [4, 256], replicated, may hold values from -3 to 3
- dt_bias: float32 [32], P('mp'), may hold values from -4 to -1
- a_log: float32 [32], P('mp'), may hold values from -3 to 1
- d_skip: float32 [32], P('mp'), may hold values from 0.5 to 1.5
- gate_gain: float32 [2048], P('mp'), may hold values from 0.5 to 1.5
- mamba_out: bfloat16 [2048, 1024], P('mp', 'dp'), may hold values from -0.125 to 0.125
- norm2_gain: float32 [1024], replicated, may hold values from 0.5 to 1.5
- attn_qkv: bfloat16 [1024, 3, 1024], P('dp', None, 'mp'), may hold values from -0.1875 to 0.1875
- attn_out: bfloat16 [1024, 1024], P('mp', 'dp'), may hold values from -0.5 to 0.5
- norm3_gain: float32 [1024], replicated, may hold values from 0.5 to 1.5
- ffn_in: bfloat16 [1024, 2, 4096], P('dp', None, 'mp'), may hold values from -0.1875 to 0.1875
- ffn_out: bfloat16 [4096, 1024], P('mp', 'dp'), may hold values from -0.09375 to 0.09375
- d_out: float32 [2, 16384, 1024], P(None, ('dp', 'mp')), may hold values from -6 to 6
Outputs:
- mixed: float32 [2, 16384, 1024], P(None, ('dp', 'mp'))
- grad_embed_table: float32 [256, 1024], replicated
- grad_patch_weight: float32 [8192, 1024], P('mp')
- grad_norm1_gain: float32 [1024], replicated
- grad_mamba_in: float32 [1024, 2, 2048], P(None, None, 'mp')
- grad_mamba_dt: float32 [1024, 32], P(None, 'mp')
- grad_mamba_bc: float32 [1024, 256], replicated
- grad_conv_x: float32 [4, 2048], P(None, 'mp')
- grad_conv_bc: float32 [4, 256], replicated
- grad_dt_bias: float32 [32], P('mp')
- grad_a_log: float32 [32], P('mp')
- grad_d_skip: float32 [32], P('mp')
- grad_gate_gain: float32 [2048], P('mp')
- grad_mamba_out: float32 [2048, 1024], P('mp')
- grad_norm2_gain: float32 [1024], replicated
- grad_attn_qkv: float32 [1024, 3, 1024], P(None, None, 'mp')
- grad_attn_out: float32 [1024, 1024], P('mp')
- grad_norm3_gain: float32 [1024], replicated
- grad_ffn_in: float32 [1024, 2, 4096], P(None, None, 'mp')
- grad_ffn_out: float32 [4096, 1024], P('mp')
Inputs may be any that keep to these rules, and one draw needn't show every extreme that they name: `segment_ids`: within each packed row of 1024 patches the ids never fall, start at 0 on the row's first patch and are 1023 on its last; in every row one segment starts within the row's first 512 patches and ends within its last 512.
All inputs are finite; a program needn't handle non-finite values.
Results may differ from a plain program's by a relative error of at most 0.028.
Values may be sent and summed in bfloat16 or wider, within the bound.
No kernel may reach another device: no remote copies, remote signals or barrier semaphores. Data moves between devices by JAX's collectives and lax.ppermute only.
A program may use at most 640 MiB of HBM per device.

v0:
```python
import jax
import jax.numpy as jnp
from jax import lax
from jax.sharding import PartitionSpec as P

PATCH = 8
VOCAB = 256
HD = 64
MB = 2
DIN = 2048


def product(left, right):
    return jnp.dot(left, right, preferred_element_type=jnp.float32)


def product_left(left, right):
    return lax.dot_general(
        left, right, (((0,), (0,)), ((), ())), preferred_element_type=jnp.float32
    )


def product_right(left, right):
    return lax.dot_general(
        left, right, (((1,), (1,)), ((), ())), preferred_element_type=jnp.float32
    )


def rms_apply(hidden, gain):
    return hidden * lax.rsqrt(jnp.mean(hidden * hidden, axis=-1, keepdims=True) + 1e-05) * gain


def conv_rows(signal, weights, seg):
    taps = weights.shape[0]
    total = weights[taps - 1] * signal
    for lag in range(1, taps):
        moved = jnp.concatenate(
            [jnp.zeros((lag, signal.shape[1]), signal.dtype), signal[:-lag]], axis=0
        )
        same = jnp.concatenate([jnp.zeros((lag,), dtype=bool), seg[lag:] == seg[:-lag]], axis=0)
        total = total + weights[taps - 1 - lag] * moved * same[:, None]
    return total


def mixer_local(packed, seg, conv_x, conv_bc, dt_bias, a_log, d_skip):
    length = packed.shape[0]
    width = conv_x.shape[1]
    state = conv_bc.shape[1] // 2
    heads = dt_bias.shape[0]
    gate_part = packed[:, :width]
    xin = packed[:, width : 2 * width]
    bc = packed[:, 2 * width : 2 * width + 2 * state]
    dtr = packed[:, 2 * width + 2 * state :]
    xs = jax.nn.silu(conv_rows(xin, conv_x, seg))
    bcs = jax.nn.silu(conv_rows(bc, conv_bc, seg)).astype(jnp.bfloat16)
    inner = product_right(bcs[:, state:], bcs[:, :state])
    steps = jax.nn.softplus(dtr + dt_bias)
    cumul = jnp.cumsum(-jnp.exp(a_log) * steps, axis=0).T
    spots = jnp.arange(length)
    keep = ((spots[:, None] >= spots[None, :]) & (seg[:, None] == seg[None, :]))[None]
    spread = cumul[:, :, None] - cumul[:, None, :]
    mixing = (jnp.where(keep, jnp.exp(jnp.where(keep, spread, 0.0)), 0.0) * inner[None]).astype(
        jnp.bfloat16
    )
    channels = xs.reshape(length, heads, -1)
    driven = (steps[:, :, None] * channels).astype(jnp.bfloat16)
    moved = jnp.einsum("hts,shp->thp", mixing, driven, preferred_element_type=jnp.float32)
    result = moved + d_skip[None, :, None] * channels
    return result.reshape(length, width) * jax.nn.silu(gate_part)


def attend_local(packed, seg):
    length = packed.shape[0]
    width = packed.shape[1] // 3
    heads = width // HD
    rounded = packed.astype(jnp.bfloat16)
    query = rounded[:, :width].reshape(length, heads, HD)
    keys = rounded[:, width : 2 * width].reshape(length, heads, HD)
    vals = rounded[:, 2 * width :].reshape(length, heads, HD)
    spots = jnp.arange(length)
    keep = ((spots[:, None] >= spots[None, :]) & (seg[:, None] == seg[None, :]))[None]
    scores = jnp.einsum("thd,shd->hts", query, keys, preferred_element_type=jnp.float32) * HD ** (
        -0.5
    )
    scores = jnp.where(keep, scores, -1e30)
    top = jnp.max(scores, axis=-1, keepdims=True)
    weights = jnp.exp(scores - top)
    weights = (weights / jnp.sum(weights, axis=-1, keepdims=True)).astype(jnp.bfloat16)
    result = jnp.einsum("hts,shd->thd", weights, vals, preferred_element_type=jnp.float32)
    return result.reshape(length, width)


def swiglu_local(packed):
    half = packed.shape[1] // 2
    return jax.nn.silu(packed[:, :half]) * packed[:, half:]


def widen(block):
    return lax.all_gather(block, "mp", axis=0, tiled=True)


def narrow(term, count):
    return lax.psum_scatter(
        term(jnp.int32(0), count * lax.axis_size("mp")), "mp", scatter_dimension=0, tiled=True
    )


def widen_grad(block):
    return lax.all_gather(block, "mp", axis=0, tiled=True)


def narrow_grad(term, count):
    return lax.psum_scatter(
        term(jnp.int32(0), count * lax.axis_size("mp")), "mp", scatter_dimension=0, tiled=True
    )


def arrange(full):
    table, patch_rows, w_mix, w_dt, w_bc, w_mout, w_qkv, w_aout, w_ffin, w_ffout = full
    width = w_mix.shape[0]
    w_proj = jnp.concatenate([w_mix.reshape(width, -1), w_bc, w_dt], axis=1)
    return (
        table,
        patch_rows,
        w_proj,
        w_mout,
        w_qkv.reshape(width, -1),
        w_aout,
        w_ffin.reshape(width, -1),
        w_ffout,
    )


def table_terms(onehot, d_embed):
    upper = d_embed.astype(jnp.bfloat16)
    lower = (d_embed - upper.astype(jnp.float32)).astype(jnp.bfloat16)
    first = jnp.einsum("lpv,lpd->vd", onehot, upper, preferred_element_type=jnp.float32)
    return first + jnp.einsum("lpv,lpd->vd", onehot, lower, preferred_element_type=jnp.float32)


def on_device(
    byte_ids,
    segment_ids,
    embed_table,
    patch_weight,
    norm1_gain,
    mamba_in,
    mamba_dt,
    mamba_bc,
    conv_x,
    conv_bc,
    dt_bias,
    a_log,
    d_skip,
    gate_gain,
    mamba_out,
    norm2_gain,
    attn_qkv,
    attn_out,
    norm3_gain,
    ffn_in,
    ffn_out,
    d_out,
):
    parts = lax.axis_size("mp")
    index = lax.axis_index("mp")
    piece = byte_ids.shape[1]
    length = piece * parts
    per_pos = PATCH // parts
    inner_width = mamba_in.shape[2]
    state = mamba_bc.shape[1] // 2
    sharded = (
        embed_table,
        patch_weight,
        mamba_in,
        mamba_dt,
        mamba_bc,
        mamba_out,
        attn_qkv,
        attn_out,
        ffn_in,
        ffn_out,
    )
    fetched = (
        lax.all_gather(sharded[0], "dp", axis=0, tiled=True),
        lax.all_gather(sharded[1], "dp", axis=1, tiled=True),
        lax.all_gather(sharded[2], "dp", axis=0, tiled=True),
        lax.all_gather(sharded[3], "dp", axis=0, tiled=True),
        lax.all_gather(sharded[4], "dp", axis=0, tiled=True),
        lax.all_gather(sharded[5], "dp", axis=1, tiled=True),
        lax.all_gather(sharded[6], "dp", axis=0, tiled=True),
        lax.all_gather(sharded[7], "dp", axis=1, tiled=True),
        lax.all_gather(sharded[8], "dp", axis=0, tiled=True),
        lax.all_gather(sharded[9], "dp", axis=1, tiled=True),
    )
    table, patch_rows, w_proj, w_mout, w_qkv, w_aout, w_ffin, w_ffout = arrange(fetched)
    kept = []
    outputs = []
    for batch in range(MB):
        ids_all, seg_all = (
            lax.all_gather(byte_ids[batch], "mp", axis=0, tiled=True),
            lax.all_gather(segment_ids[batch], "mp", axis=0, tiled=True),
        )
        local_ids = lax.dynamic_slice_in_dim(ids_all, index * per_pos, per_pos, 1)
        onehot = (
            local_ids[:, :, None] == jnp.arange(VOCAB, dtype=jnp.int32)[None, None, :]
        ).astype(jnp.bfloat16)
        embedded = jnp.einsum("lpv,vd->lpd", onehot, table, preferred_element_type=jnp.float32)
        embedded = embedded.astype(jnp.bfloat16).reshape(length, -1)
        resid0 = narrow(lambda start, count: product(embedded, patch_rows), piece)
        wide1 = widen(rms_apply(resid0, norm1_gain).astype(jnp.bfloat16))
        proj = product(wide1, w_proj)
        gated = mixer_local(proj, seg_all, conv_x, conv_bc, dt_bias, a_log, d_skip)
        total = lax.psum(jnp.sum(gated * gated, axis=1), "mp")
        factor = lax.rsqrt(total / DIN + 1e-05)[:, None]
        gnormed = (gated * factor * gate_gain).astype(jnp.bfloat16)
        resid1 = resid0 + narrow(lambda start, count: product(gnormed, w_mout), piece)
        wide2 = widen(rms_apply(resid1, norm2_gain).astype(jnp.bfloat16))
        qkv = product(wide2, w_qkv)
        attended = attend_local(qkv, seg_all).astype(jnp.bfloat16)
        resid2 = resid1 + narrow(lambda start, count: product(attended, w_aout), piece)
        wide3 = widen(rms_apply(resid2, norm3_gain).astype(jnp.bfloat16))
        gate_up = product(wide3, w_ffin)
        hidden = swiglu_local(gate_up).astype(jnp.bfloat16)
        outputs.append(resid2 + narrow(lambda start, count: product(hidden, w_ffout), piece))
        kept.append(
            (
                seg_all,
                onehot,
                embedded,
                resid0,
                resid1,
                resid2,
                wide1,
                proj,
                gated,
                factor,
                gnormed,
                wide2,
                qkv,
                attended,
                wide3,
                gate_up,
                hidden,
            )
        )
    mixed = jnp.stack(outputs, axis=0)
    grad_resid = [d_out[batch] for batch in range(MB)]
    acc_ffin = jnp.zeros(w_ffin.shape, jnp.float32)
    acc_ffout = jnp.zeros(w_ffout.shape, jnp.float32)
    acc_gain3 = jnp.zeros(norm3_gain.shape, jnp.float32)
    for batch in range(MB):
        saved = kept[batch]
        wide_grad = widen_grad(grad_resid[batch].astype(jnp.bfloat16))
        acc_ffout = acc_ffout + product_left(saved[16], wide_grad)
        d_hidden = product_right(wide_grad, w_ffout)
        d_gate_up = jax.vjp(swiglu_local, saved[15])[1](d_hidden)[0].astype(jnp.bfloat16)
        acc_ffin = acc_ffin + product_left(saved[14], d_gate_up)
        d_norm = narrow_grad(lambda start, count: product_right(d_gate_up, w_ffin), piece)
        d_back, d_gain = jax.vjp(rms_apply, saved[5], norm3_gain)[1](d_norm)
        grad_resid[batch] = grad_resid[batch] + d_back
        acc_gain3 = acc_gain3 + d_gain
    acc_qkv = jnp.zeros(w_qkv.shape, jnp.float32)
    acc_aout = jnp.zeros(w_aout.shape, jnp.float32)
    acc_gain2 = jnp.zeros(norm2_gain.shape, jnp.float32)
    for batch in range(MB):
        saved = kept[batch]
        seg_all = saved[0]
        wide_grad = widen_grad(grad_resid[batch].astype(jnp.bfloat16))
        acc_aout = acc_aout + product_left(saved[13], wide_grad)
        d_att = product_right(wide_grad, w_aout)
        d_qkv = jax.vjp(lambda packed: attend_local(packed, seg_all), saved[12])[1](d_att)[0]
        d_qkv = d_qkv.astype(jnp.bfloat16)
        acc_qkv = acc_qkv + product_left(saved[11], d_qkv)
        d_norm = narrow_grad(lambda start, count: product_right(d_qkv, w_qkv), piece)
        d_back, d_gain = jax.vjp(rms_apply, saved[4], norm2_gain)[1](d_norm)
        grad_resid[batch] = grad_resid[batch] + d_back
        acc_gain2 = acc_gain2 + d_gain
    acc_proj = jnp.zeros(w_proj.shape, jnp.float32)
    acc_mout = jnp.zeros(w_mout.shape, jnp.float32)
    acc_ggain = jnp.zeros(gate_gain.shape, jnp.float32)
    acc_convx = jnp.zeros(conv_x.shape, jnp.float32)
    acc_convbc = jnp.zeros(conv_bc.shape, jnp.float32)
    acc_bias = jnp.zeros(dt_bias.shape, jnp.float32)
    acc_alog = jnp.zeros(a_log.shape, jnp.float32)
    acc_skip = jnp.zeros(d_skip.shape, jnp.float32)
    acc_gain1 = jnp.zeros(norm1_gain.shape, jnp.float32)
    for batch in range(MB):
        saved = kept[batch]
        seg_all = saved[0]
        gated = saved[8]
        factor = saved[9]
        wide_grad = widen_grad(grad_resid[batch].astype(jnp.bfloat16))
        acc_mout = acc_mout + product_left(saved[10], wide_grad)
        d_gn = product_right(wide_grad, w_mout)
        weighted = d_gn * gate_gain
        acc_ggain = acc_ggain + jnp.sum(gated * factor * d_gn, axis=0)
        cross = lax.psum(jnp.sum(gated * weighted, axis=1), "mp")
        d_gated = weighted * factor - gated * factor**3 * (cross / DIN)[:, None]
        pull = jax.vjp(
            lambda packed, taps_x, taps_bc, bias, decay, skip: mixer_local(
                packed, seg_all, taps_x, taps_bc, bias, decay, skip
            ),
            saved[7],
            conv_x,
            conv_bc,
            dt_bias,
            a_log,
            d_skip,
        )[1]
        d_proj, d_convx, d_convbc, d_bias, d_alog, d_skipped = pull(d_gated)
        d_proj = d_proj.astype(jnp.bfloat16)
        acc_convx = acc_convx + d_convx
        acc_convbc = acc_convbc + d_convbc
        acc_bias = acc_bias + d_bias
        acc_alog = acc_alog + d_alog
        acc_skip = acc_skip + d_skipped
        acc_proj = acc_proj + product_left(saved[6], d_proj)
        d_norm = narrow_grad(lambda start, count: product_right(d_proj, w_proj), piece)
        d_back, d_gain = jax.vjp(rms_apply, saved[3], norm1_gain)[1](d_norm)
        grad_resid[batch] = grad_resid[batch] + d_back
        acc_gain1 = acc_gain1 + d_gain
    acc_patch = jnp.zeros(patch_rows.shape, jnp.float32)
    acc_table = jnp.zeros(table.shape, jnp.float32)
    for batch in range(MB):
        saved = kept[batch]
        wide_grad = widen_grad(grad_resid[batch].astype(jnp.bfloat16))
        acc_patch = acc_patch + product_left(saved[2], wide_grad)
        d_embed = product_right(wide_grad, patch_rows).reshape(length, per_pos, -1)
        acc_table = acc_table + table_terms(saved[1], d_embed)
    model_width = w_proj.shape[0]
    grad_mix = acc_proj[:, : 2 * inner_width].reshape(model_width, 2, inner_width)
    grad_bc = acc_proj[:, 2 * inner_width : 2 * inner_width + 2 * state]
    grad_dt = acc_proj[:, 2 * inner_width + 2 * state :]
    (
        acc_patch,
        grad_mix,
        grad_dt,
        acc_mout,
        acc_convx,
        acc_bias,
        acc_alog,
        acc_skip,
        acc_ggain,
        acc_qkv,
        acc_aout,
        acc_ffin,
        acc_ffout,
    ) = lax.psum(
        (
            acc_patch,
            grad_mix,
            grad_dt,
            acc_mout,
            acc_convx,
            acc_bias,
            acc_alog,
            acc_skip,
            acc_ggain,
            acc_qkv,
            acc_aout,
            acc_ffin,
            acc_ffout,
        ),
        "dp",
    )
    acc_table, grad_bc, acc_convbc, acc_gain1, acc_gain2, acc_gain3 = lax.psum(
        (acc_table, grad_bc, acc_convbc, acc_gain1, acc_gain2, acc_gain3), ("dp", "mp")
    )
    grad_qkv = acc_qkv.reshape(model_width, 3, -1)
    grad_ffin = acc_ffin.reshape(model_width, 2, -1)
    return (
        mixed,
        acc_table,
        acc_patch,
        acc_gain1,
        grad_mix,
        grad_dt,
        grad_bc,
        acc_convx,
        acc_convbc,
        acc_bias,
        acc_alog,
        acc_skip,
        acc_ggain,
        acc_mout,
        acc_gain2,
        grad_qkv,
        acc_aout,
        acc_gain3,
        grad_ffin,
        acc_ffout,
    )


def solution(mesh):
    return jax.shard_map(
        on_device,
        mesh=mesh,
        in_specs=(
            P(None, ("dp", "mp"), None),
            P(None, ("dp", "mp")),
            P("dp", None),
            P("mp", "dp"),
            P(),
            P("dp", None, "mp"),
            P("dp", "mp"),
            P("dp", None),
            P(None, "mp"),
            P(),
            P("mp"),
            P("mp"),
            P("mp"),
            P("mp"),
            P("mp", "dp"),
            P(),
            P("dp", None, "mp"),
            P("mp", "dp"),
            P(),
            P("dp", None, "mp"),
            P("mp", "dp"),
            P(None, ("dp", "mp"), None),
        ),
        out_specs=(
            P(None, ("dp", "mp"), None),
            P(),
            P("mp", None),
            P(),
            P(None, None, "mp"),
            P(None, "mp"),
            P(),
            P(None, "mp"),
            P(),
            P("mp"),
            P("mp"),
            P("mp"),
            P("mp"),
            P("mp", None),
            P(),
            P(None, None, "mp"),
            P("mp", None),
            P(),
            P(None, None, "mp"),
            P("mp", None),
        ),
        check_vma=False,
    )
```

profile of v0, /device:TPU:0, one launch (start us, length us, event | category | flops | bytes accessed | tf_op | source)
XLA Modules:
  0.0 3573.3 jit_solution(4505380268738454526)
XLA Ops:
  14.0 25.9 all_gather.85
  46.0 43.6 %all-gather.27.cloned.1.call-done = bf16[4096,1024]{0,1:T(8,128)(2,1)} async-done(((bf16[4096,64]{0,1:T(8,128)(2,1)}), bf16[4096,1024]{0,1:T(8,128)(2,1)}) %all-gather.27.cloned.1.call-update) | async-done | bytes 8388624 | tf_op jit(solution)/shard_map/all_gather | solution.py:186
  126.6 30.7 reduce-scatter.23.cloned.1.call-done
  159.3 55.3 %reduce-scatter.15.cloned.1.call-done = f32[512,1024]{1,0:T(8,128)} async-done(((f32[1024,1024]{1,0:T(8,128)}), f32[512,1024]{1,0:T(8,128)}) %reduce-scatter.15.cloned.1.call-update) | async-done | bytes 2097168 | tf_op jit(solution)/shard_map/reduce_scatter | solution.py:103
  399.6 23.6 bitcast_add_fusion.1
  479.2 45.4 %reduce-scatter.17.cloned.1.call-done = f32[512,1024]{1,0:T(8,128)} async-done(((f32[1024,1024]{1,0:T(8,128)}), f32[512,1024]{1,0:T(8,128)}) %reduce-scatter.17.cloned.1.call-update) | async-done | bytes 2097168 | tf_op jit(solution)/shard_map/reduce_scatter | solution.py:103
  527.1 54.7 %reduce-scatter.25.cloned.1.call-done = f32[512,1024]{1,0:T(8,128)} async-done(((f32[1024,1024]{1,0:T(8,128)}), f32[512,1024]{1,0:T(8,128)}) %reduce-scatter.25.cloned.1.call-update) | async-done | bytes 2097168 | tf_op jit(solution)/shard_map/reduce_scatter | solution.py:103
  588.9 40.3 %all-gather.37.cloned.1.call-done = bf16[1024,3,512]{2,0,1:T(8,128)(2,1)} async-done(((bf16[64,3,512]{2,0,1:T(8,128)(2,1)}), bf16[1024,3,512]{2,0,1:T(8,128)(2,1)}) %all-gather.37.cloned.1.call-update) | async-done | bytes 3145744 | tf_op jit(solution)/shard_map/all_gather | solution.py:191
  634.0 29.2 all-gather.35.cloned.1.call-done
  825.9 50.3 %reduce-scatter.27.cloned.1.call-done = f32[512,1024]{1,0:T(8,128)} async-done(((f32[1024,1024]{1,0:T(8,128)}), f32[512,1024]{1,0:T(8,128)}) %reduce-scatter.27.cloned.1.call-update) | async-done | bytes 2097168 | tf_op jit(solution)/shard_map/reduce_scatter | solution.py:103
  887.4 65.8 %all-gather.43.cloned.1.call-done = bf16[1024,2,2048]{2,1,0:T(2,128)(2,1)} async-done(((bf16[64,2,2048]{2,1,0:T(2,128)(2,1)}), bf16[1024,2,2048]{2,1,0:T(2,128)(2,1)}) %all-gather.43.cloned.1.call-update) | async-done | bytes 8388624 | tf_op jit(solution)/shard_map/all_gather | solution.py:193
  1021.1 52.9 %all-gather.45.cloned.1.call-done = bf16[2048,1024]{0,1:T(8,128)(2,1)} async-done(((bf16[2048,64]{0,1:T(8,128)(2,1)}), bf16[2048,1024]{0,1:T(8,128)(2,1)}) %all-gather.45.cloned.1.call-update) | async-done | bytes 4194320 | tf_op jit(solution)/shard_map/all_gather | solution.py:194
  1198.4 57.3 %reduce-scatter.31.cloned.1.call-done = f32[512,1024]{1,0:T(8,128)} async-done(((f32[1024,1024]{1,0:T(8,128)}), f32[512,1024]{1,0:T(8,128)}) %reduce-scatter.31.cloned.1.call-update) | async-done | bytes 2097168 | tf_op jit(solution)/shard_map/reduce_scatter | solution.py:113
  1260.3 51.9 %reduce-scatter.29.cloned.1.call-done = f32[512,1024]{1,0:T(8,128)} async-done(((f32[1024,1024]{1,0:T(8,128)}), f32[512,1024]{1,0:T(8,128)}) %reduce-scatter.29.cloned.1.call-update) | async-done | bytes 2097168 | tf_op jit(solution)/shard_map/reduce_scatter | solution.py:103
  1312.2 56.7 %reduce-scatter.21.cloned.1.call-done = f32[512,1024]{1,0:T(8,128)} async-done(((f32[1024,1024]{1,0:T(8,128)}), f32[512,1024]{1,0:T(8,128)}) %reduce-scatter.21.cloned.1.call-update) | async-done | bytes 2097168 | tf_op jit(solution)/shard_map/reduce_scatter | solution.py:103
  1379.3 32.4 all-gather.55.cloned.1.call-done
  1436.0 29.9 fusion.210
  1523.4 21.8 fusion.21
  1545.2 30.2 fusion.203
  1626.7 54.3 %reduce-scatter.39.cloned.1.call-done = f32[512,1024]{1,0:T(8,128)} async-done(((f32[1024,1024]{1,0:T(8,128)}), f32[512,1024]{1,0:T(8,128)}) %reduce-scatter.39.cloned.1.call-update) | async-done | bytes 2097168 | tf_op jit(solution)/shard_map/reduce_scatter | solution.py:113
  1691.6 32.4 all-gather.57.cloned.1.call-done
  1730.6 28.7 all-gather.65.cloned.1.call-done
  1796.6 40.5 %fusion.11 = (f32[16,1024]{1,0:T(8,128)S(1)}, f32[16,1024]{1,0:T(8,128)S(1)}, bf16[1024,1024]{1,0:T(8,128)(2,1)S(1)}) fusion(f32[1024,1024]{1,0:T(8,128)} %fusion.132, f32[16,1024]{1,0:T(8,128)S(1)} %bitcast.461, pred[1024,1024]{1,0:T(8,128)(4,1)S(1)} %copy-done.96, f32[16,64,1024]{2,1,0:T(8,128)} %bitcast.413, f32[1024,16,64]{0,2,1:T(8,128)} %bitcast.387, ...), kind=kOutput, calls=%fused_computation.19 | convolution fusion | flops 2349826048 | bytes 15990784 | tf_op jit(solution)/shard_map/transpose(jvp(hts,shp->thp))/dot_general | solution.py:67
  1839.6 40.7 %fusion.13 = (f32[16,1024]{1,0:T(8,128)}, f32[16,1024]{1,0:T(8,128)}, bf16[1024,1024]{1,0:T(8,128)(2,1)S(1)}) fusion(f32[1024,1024]{1,0:T(8,128)S(1)} %copy-done.66, f32[16,1024]{1,0:T(8,128)S(1)} %bitcast.458, pred[1024,1024]{1,0:T(8,128)(4,1)S(1)} %copy-done.94, f32[16,64,1024]{2,1,0:T(8,128)S(1)} %bitcast.412, f32[1024,16,64]{0,2,1:T(8,128)S(1)} %bitcast.386, ...), kind=kOutput, calls=%fused_computation.21 | convolution fusion | flops 2349826048 | bytes 15990784 | tf_op jit(solution)/shard_map/transpose(jvp(hts,shp->thp))/dot_general | solution.py:67
  1881.6 26.5 fusion.74
  1948.8 25.9 fusion.76
  2133.1 46.9 %reduce-scatter.41.cloned.1.call-done = f32[512,1024]{1,0:T(8,128)} async-done(((f32[1024,1024]{1,0:T(8,128)}), f32[512,1024]{1,0:T(8,128)}) %reduce-scatter.41.cloned.1.call-update) | async-done | bytes 2097168 | tf_op jit(solution)/shard_map/reduce_scatter | solution.py:113
  2384.4 22.0 reshape.771
  2413.1 62.4 %all-reduce.68 = (f32[4,1024]{1,0:T(4,128)}, f32[16]{0:T(128)}, f32[16]{0:T(128)}, f32[16]{0:T(128)}, f32[1024]{0:T(1024)}) all-reduce(f32[4,1024]{1,0:T(4,128)S(1)} %add_add_fusion.6, f32[16]{0:T(128)S(1)} %add.555, f32[16]{0:T(128)S(1)} %add_multiply_fusion, f32[16]{0:T(128)S(1)} %add.557, ...), channel_id=1, replica_groups=mesh['dp'=16,'mp'=2] {'dp'}, use_global_device_ids=true, to_apply=%region_80.82 | all-reduce | flops 5168 | bytes 41344 | tf_op jit(solution)/shard_map/psum | solution.py:349
  2475.6 39.1 %all-reduce.66 = (f32[1024]{0:T(1024)}, f32[4,256]{1,0:T(4,128)}, f32[1024]{0:T(1024)}, f32[1024]{0:T(1024)}) all-reduce(f32[1024]{0:T(1024)S(1)} %add.551, f32[4,256]{1,0:T(4,128)S(1)} %add_add_fusion.7, f32[1024]{0:T(1024)S(1)} %add.560, f32[1024]{0:T(1024)S(1)} %add.563), channel_id=1, replica_groups=mesh['dp'=16,'mp'=2] {'dp','mp'}, use_global_device_ids=true, to_apply=%region_68.70 | all-reduce | flops 4096 | bytes 32768 | tf_op jit(solution)/shard_map/psum | solution.py:367
  2517.3 705.9 %all-reduce.80.cloned.1.call-done = (f32[4096,1024]{1,0:T(8,128)}, f32[1024,2,1024]{2,1,0:T(2,128)}, f32[1024,16]{0,1:T(8,128)}, f32[1024,1024]{1,0:T(8,128)}, f...) async-done(((f32[4096,1024]{1,0:T(8,128)}, f32[1024,2,1024]{2,1,0:T(2,128)}, f32[1024,16]{0,1:T(8,128)}, f32[1024,1024]{1,0:T(8,128)}, ...) | async-done | bytes 46202896 | tf_op jit(solution)/shard_map/psum | solution.py:349
  3229.9 295.2 %all-reduce.76.cloned.1.call-done = f32[1024,2,2048]{2,1,0:T(2,128)} async-done(((f32[1024,2,2048]{2,1,0:T(2,128)}), f32[1024,2,2048]{2,1,0:T(2,128)}) %all-reduce.76.cloned.1.call-update) | async-done | bytes 16777232 | tf_op jit(solution)/shard_map/psum | solution.py:349
  (911 shorter events, 1336.8 us)
Async XLA Ops:
  7.9 149.5 %reduce-scatter.23.cloned.1.call-start = ((), (), s32[]{:S(2)}) async-start(), calls=%async_computation.28 | async-start | bytes 6291456 | tf_op jit(solution)/shard_map/reduce_scatter | solution.py:103
  126.0 154.3 %all-gather.31.cloned.1.call-start = ((), (), s32[]{:S(2)}) async-start(), calls=%async_computation.17 | async-start | bytes 4456448 | tf_op jit(solution)/shard_map/all_gather | solution.py:187
  126.6 178.2 %all-gather.47.cloned.1.call-start = ((), (), s32[]{:S(2)}) async-start(), calls=%async_computation.29 | async-start | bytes 3145728 | tf_op jit(solution)/shard_map/all_gather | solution.py:99
  220.5 119.4 %all-gather.29.cloned.1.call-start = ((), (), s32[]{:S(2)}) async-start(), calls=%async_computation.16 | async-start | bytes 3145728 | tf_op jit(solution)/shard_map/all_gather | solution.py:99
  221.1 241.4 %all-gather.33.cloned.1.call-start = ((), (), s32[]{:S(2)}) async-start(), calls=%async_computation.18 | async-start | bytes 2228224 | tf_op jit(solution)/shard_map/all_gather | solution.py:190
  221.9 302.7 %reduce-scatter.17.cloned.1.call-start = ((), (), s32[]{:S(2)}) async-start(), calls=%async_computation.19 | async-start | bytes 6291456 | tf_op jit(solution)/shard_map/reduce_scatter | solution.py:103
  470.1 111.8 %reduce-scatter.25.cloned.1.call-start = ((), (), s32[]{:S(2)}) async-start(), calls=%async_computation.30 | async-start | bytes 6291456 | tf_op jit(solution)/shard_map/reduce_scatter | solution.py:103
  478.6 150.6 %all-gather.37.cloned.1.call-start = ((), (), s32[]{:S(2)}) async-start(), calls=%async_computation.21 | async-start | bytes 3342336 | tf_op jit(solution)/shard_map/all_gather | solution.py:191
  479.1 184.1 %all-gather.35.cloned.1.call-start = ((), (), s32[]{:S(2)}) async-start(), calls=%async_computation.20 | async-start | bytes 3145728 | tf_op jit(solution)/shard_map/all_gather | solution.py:99
  587.5 140.8 %all-gather.49.cloned.1.call-start = ((), (), s32[]{:S(2)}) async-start(), calls=%async_computation.31 | async-start | bytes 3145728 | tf_op jit(solution)/shard_map/all_gather | solution.py:99
  588.1 163.0 %all-gather.39.cloned.1.call-start = ((), (), s32[]{:S(2)}) async-start(), calls=%async_computation.22 | async-start | bytes 1114112 | tf_op jit(solution)/shard_map/all_gather | solution.py:192
  588.9 233.2 %reduce-scatter.19.cloned.1.call-start = ((), (), s32[]{:S(2)}) async-start(), calls=%async_computation.23 | async-start | bytes 6291456 | tf_op jit(solution)/shard_map/reduce_scatter | solution.py:103
  756.1 120.2 %reduce-scatter.27.cloned.1.call-start = ((), (), s32[]{:S(2)}) async-start(), calls=%async_computation.32 | async-start | bytes 6291456 | tf_op jit(solution)/shard_map/reduce_scatter | solution.py:103
  821.4 131.8 %all-gather.43.cloned.1.call-start = ((), (), s32[]{:S(2)}) async-start(), calls=%async_computation.25 | async-start | bytes 8912896 | tf_op jit(solution)/shard_map/all_gather | solution.py:193
  822.0 164.6 %all-gather.51.cloned.1.call-start = ((), (), s32[]{:S(2)}) async-start(), calls=%async_computation.33 | async-start | bytes 3145728 | tf_op jit(solution)/shard_map/all_gather | solution.py:99
  881.2 139.9 %all-gather.61.cloned.1.call-start = ((), (), s32[]{:S(2)}) async-start(), calls=%async_computation.42 | async-start | bytes 3145728 | tf_op jit(solution)/shard_map/all_gather | solution.py:109
  885.2 188.9 %all-gather.45.cloned.1.call-start = ((), (), s32[]{:S(2)}) async-start(), calls=%async_computation.26 | async-start | bytes 4456448 | tf_op jit(solution)/shard_map/all_gather | solution.py:194
  885.9 221.9 %all-gather.41.cloned.1.call-start = ((), (), s32[]{:S(2)}) async-start(), calls=%async_computation.24 | async-start | bytes 3145728 | tf_op jit(solution)/shard_map/all_gather | solution.py:99
  886.5 255.3 %all-gather.53.cloned.1.call-start = ((), (), s32[]{:S(2)}) async-start(), calls=%async_computation.35 | async-start | bytes 3145728 | tf_op jit(solution)/shard_map/all_gather | solution.py:109
  887.2 311.2 %reduce-scatter.37.cloned.1.call-start = ((), (), s32[]{:S(2)}) async-start(), calls=%async_computation.43 | async-start | bytes 6291456 | tf_op jit(solution)/shard_map/reduce_scatter | solution.py:113
  1107.7 148.0 %reduce-scatter.31.cloned.1.call-start = ((), (), s32[]{:S(2)}) async-start(), calls=%async_computation.36 | async-start | bytes 6291456 | tf_op jit(solution)/shard_map/reduce_scatter | solution.py:113
  1175.4 136.8 %reduce-scatter.29.cloned.1.call-start = ((), (), s32[]{:S(2)}) async-start(), calls=%async_computation.34 | async-start | bytes 6291456 | tf_op jit(solution)/shard_map/reduce_scatter | solution.py:103
  1186.0 183.0 %reduce-scatter.21.cloned.1.call-start = ((), (), s32[]{:S(2)}) async-start(), calls=%async_computation.27 | async-start | bytes 6291456 | tf_op jit(solution)/shard_map/reduce_scatter | solution.py:103
  1196.3 215.4 %all-gather.55.cloned.1.call-start = ((), (), s32[]{:S(2)}) async-start(), calls=%async_computation.37 | async-start | bytes 3145728 | tf_op jit(solution)/shard_map/all_gather | solution.py:109
  1378.5 141.6 %all-gather.63.cloned.1.call-start = ((), (), s32[]{:S(2)}) async-start(), calls=%async_computation.44 | async-start | bytes 3145728 | tf_op jit(solution)/shard_map/all_gather | solution.py:109
  1379.1 247.6 %reduce-scatter.33.cloned.1.call-start = ((), (), s32[]{:S(2)}) async-start(), calls=%async_computation.38 | async-start | bytes 6291456 | tf_op jit(solution)/shard_map/reduce_scatter | solution.py:113
  1520.0 161.0 %reduce-scatter.39.cloned.1.call-start = ((), (), s32[]{:S(2)}) async-start(), calls=%async_computation.45 | async-start | bytes 6291456 | tf_op jit(solution)/shard_map/reduce_scatter | solution.py:113
  1691.5 441.5 %reduce-scatter.35.cloned.1.call-start = ((), (), s32[]{:S(2)}) async-start(), calls=%async_computation.40 | async-start | bytes 6291456 | tf_op jit(solution)/shard_map/reduce_scatter | solution.py:113
  2082.0 158.1 %all-gather.67.cloned.1.call-start = ((), (), s32[]{:S(2)}) async-start(), calls=%async_computation.48 | async-start | bytes 3145728 | tf_op jit(solution)/shard_map/all_gather | solution.py:109
  2239.8 274.9 %all-reduce.78.cloned.1.call-start = ((), (), s32[]{:S(2)}) async-start(), calls=%async_computation.50 | async-start | bytes 4194304 | tf_op jit(solution)/shard_map/psum | solution.py:367
  2309.3 914.0 %all-reduce.80.cloned.1.call-start = ((), (), s32[]{:S(2)}) async-start(), calls=%async_computation.51 | async-start | bytes 92405760 | tf_op jit(solution)/shard_map/psum | solution.py:349
  2344.1 1181.0 %all-reduce.76.cloned.1.call-start = ((), (), s32[]{:S(2)}) async-start(), calls=%async_computation.49 | async-start | bytes 33554432 | tf_op jit(solution)/shard_map/psum | solution.py:349
  (288 other events, 8703.2 us)
Sparse Core Ops, SparseCore 0:
  10.2 79.3 all-gather.26
  104.8 52.5 reduce-scatter.22
  160.4 54.2 reduce-scatter.14
  216.7 53.4 all-gather.30
  306.8 33.1 all-gather.28
  342.1 41.3 all-gather.32
  470.2 54.2 reduce-scatter.16
  527.5 54.3 reduce-scatter.24
  583.9 45.2 all-gather.36
  665.2 33.1 all-gather.48
  700.5 37.9 all-gather.38
  756.2 54.3 reduce-scatter.18
  821.6 54.6 reduce-scatter.26
  878.3 74.8 all-gather.42
  988.0 33.1 all-gather.60
  1023.3 50.7 all-gather.44
  1108.6 33.1 all-gather.52
  1144.1 54.2 reduce-scatter.36
  1201.4 54.3 reduce-scatter.30
  1257.9 54.2 reduce-scatter.28
  1314.6 54.3 reduce-scatter.20
  1378.6 33.1 all-gather.54
  1413.1 33.1 all-gather.62
  1520.0 54.3 reduce-scatter.32
  1626.7 54.2 reduce-scatter.38
  1690.9 33.1 all-gather.56
  2068.4 54.2 reduce-scatter.34
  2125.6 54.3 reduce-scatter.40
  2188.7 33.1 all-gather.66
  2309.4 133.9 all-reduce.77
  2451.7 771.5 all-reduce.79
  3227.1 297.9 all-reduce.75
  (6 shorter events, 193.3 us)
where the time goes:
time: 3580 us; the launch traced here: 3570 us
  waiting for transfers between devices  1940 us (54%)
  matrix products  824 us (23%)
  other arithmetic  378 us (11%)
  local copies, waits for them, and re-layouts  208 us (6%)
  blocking collectives  198 us (6%)
    psum x2, waiting for transfers between devices, on_device(): lax.psum((acc_patch, grad_mix, grad_dt, acc_mout, acc_convx, acc_bias, ac...  1000 us
    reduce_scatter x8, waiting for transfers between devices, narrow(): lax.psum_scatter(term(jnp.int32(0), count * lax.axis_size('mp')), 'mp', s...  345 us
    dot_general x6, matrix products, mixer_local(): jnp.einsum('hts,shp->thp', mixing, driven, preferred_element_type=jnp.flo...  178 us
    dot_general x20, matrix products, product_right(): lax.dot_general(left, right, (((1,), (1,)), ((), ())), preferred_element_...  162 us
    reduce_scatter x6, waiting for transfers between devices, narrow_grad(): lax.psum_scatter(term(jnp.int32(0), count * lax.axis_size('mp')), 'mp', s...  161 us
    dot_general x14, matrix products, product_left(): lax.dot_general(left, right, (((0,), (0,)), ((), ())), preferred_element_...  144 us
    all_gather x8, waiting for transfers between devices, widen_grad(): return lax.all_gather(block, 'mp', axis=0, tiled=True)  142 us
    dot_general x14, matrix products, product(): return jnp.dot(left, right, preferred_element_type=jnp.float32)  130 us
  transfers between devices with their start and end apart: 38, of which 27 were waited for; matrix products, arithmetic and copies ran while one was open for 26% of the time, Pallas kernels for 0%

commit v1 on v0

--- a/solution.py
+++ b/solution.py
@@ -1,6 +1,8 @@
 import jax
 import jax.numpy as jnp
 from jax import lax
+from jax.experimental import pallas as pl
+from jax.experimental.pallas import tpu as pltpu
 from jax.sharding import PartitionSpec as P
 
 PATCH = 8
@@ -8,6 +10,1348 @@
 HD = 64
 MB = 2
 DIN = 2048
+PM = 64
+TAPS = 4
+VMEM_LIMIT = 56 * 1024 * 1024
+LOG2E = 1.4426950408889634
+BLK = 256
+
+
+def dot_nn(a, b):
+    return lax.dot_general(a, b, (((1,), (0,)), ((), ())), preferred_element_type=jnp.float32)
+
+
+def dot_nt(a, b):
+    return lax.dot_general(a, b, (((1,), (1,)), ((), ())), preferred_element_type=jnp.float32)
+
+
+def dot_tn(a, b):
+    return lax.dot_general(a, b, (((0,), (0,)), ((), ())), preferred_element_type=jnp.float32)
+
+
+def sigmoid(v):
+    return 0.5 * jnp.tanh(0.5 * v) + 0.5
+
+
+def head_masks(width, size):
+    lane = lax.broadcasted_iota(jnp.int32, (1, width), 1) // size
+    return [lane == h for h in range(width // size)]
+
+
+def spread_heads(cols, first, masks, width):
+    rows = cols.shape[0]
+    out = jnp.broadcast_to(cols[:, first : first + 1], (rows, width))
+    for h in range(1, len(masks)):
+        piece = jnp.broadcast_to(cols[:, first + h : first + h + 1], (rows, width))
+        out = jnp.where(masks[h], piece, out)
+    return out
+
+
+def two_parts(v):
+    upper = v.astype(jnp.bfloat16)
+    return upper, (v - upper.astype(jnp.float32)).astype(jnp.bfloat16)
+
+
+def attn_fwd_kernel(q_ref, k_ref, v_ref, pos_ref, o_ref, lse_ref, bias_ref):
+    length = pos_ref.shape[0]
+    width = q_ref.shape[2]
+
+    @pl.when(pl.program_id(0) == 0)
+    def _():
+        for i in range(length // BLK):
+            rows = pl.ds(i * BLK, BLK)
+            n = (i + 1) * BLK
+            spot = i * BLK + lax.broadcasted_iota(jnp.int32, (BLK, n), 0)
+            other = lax.broadcasted_iota(jnp.int32, (BLK, n), 1)
+            gap = (spot - other).astype(jnp.float32)
+            keep = (gap >= 0.0) & (gap <= pos_ref[rows, 0:1])
+            bias_ref[rows, 0:n] = jnp.where(keep, 0.0, -1e30)
+
+    masks = head_masks(width, HD)
+    spots = lax.broadcasted_iota(jnp.int32, (1, 128), 1)
+    for i in range(length // BLK):
+        rows = pl.ds(i * BLK, BLK)
+        n = (i + 1) * BLK
+        query = q_ref[0, rows, :] * jnp.bfloat16(HD**-0.5)
+        keys = k_ref[0, 0:n, :]
+        vals = v_ref[0, 0:n, :]
+        bias = bias_ref[rows, 0:n]
+        total = jnp.zeros((BLK, width), jnp.float32)
+        logs = jnp.zeros((BLK, 128), jnp.float32)
+        for h, mask in enumerate(masks):
+            scores = dot_nt(jnp.where(mask, query, jnp.bfloat16(0)), keys) + bias
+            top = jnp.max(scores, axis=1, keepdims=True)
+            weights = jnp.exp(scores - top)
+            norm = jnp.sum(weights, axis=1, keepdims=True)
+            probs = (weights * (1.0 / norm)).astype(jnp.bfloat16)
+            total = jnp.where(mask, dot_nn(probs, vals), total)
+            logs = jnp.where(spots == h, top + jnp.log(norm), logs)
+        o_ref[0, rows, :] = total.astype(jnp.bfloat16)
+        lse_ref[0, rows, :] = logs
+
+
+def attn_forward(qkv, posb):
+    parts, length, width3 = qkv.shape
+    width = width3 // 3
+    lanes = min(256, width)
+    per = width // lanes
+    groups = parts * per
+    block = (1, length, lanes)
+    return pl.pallas_call(
+        attn_fwd_kernel,
+        grid=(groups,),
+        in_specs=[
+            pl.BlockSpec(block, lambda g: (g // per, 0, g % per)),
+            pl.BlockSpec(block, lambda g: (g // per, 0, per + g % per)),
+            pl.BlockSpec(block, lambda g: (g // per, 0, 2 * per + g % per)),
+            pl.BlockSpec((length, 128), lambda g: (0, 0)),
+        ],
+        out_specs=[
+            pl.BlockSpec(block, lambda g: (g // per, 0, g % per)),
+            pl.BlockSpec((1, length, 128), lambda g: (g, 0, 0)),
+        ],
+        out_shape=[
+            jax.ShapeDtypeStruct((parts, length, width), jnp.bfloat16),
+            jax.ShapeDtypeStruct((groups, length, 128), jnp.float32),
+        ],
+        scratch_shapes=[pltpu.VMEM((length, length), jnp.float32)],
+        compiler_params=pltpu.CompilerParams(vmem_limit_bytes=VMEM_LIMIT),
+        cost_estimate=pl.CostEstimate(
+            flops=30_000_000_000, bytes_accessed=10_000_000, transcendentals=0
+        ),
+        name="attn_fwd",
+    )(qkv, qkv, qkv, posb)
+
+
+def attn_bwd_kernel(
+    q_ref, k_ref, v_ref, o_ref, do_ref, lse_ref, rem_ref, *others
+):
+    out_ref, bias_ref, dk_ref, dv_ref = others[-4:]
+    length = rem_ref.shape[0]
+    width = q_ref.shape[2]
+    per = out_ref.shape[2] // (3 * width)
+    step = pl.program_id(0)
+
+    @pl.when(step == 0)
+    def _():
+        for i in range(length // BLK):
+            cols = pl.ds(i * BLK, BLK)
+            n = (i + 1) * BLK
+            other = lax.broadcasted_iota(jnp.int32, (n, BLK), 0)
+            spot = i * BLK + lax.broadcasted_iota(jnp.int32, (n, BLK), 1)
+            gap = (spot - other).astype(jnp.float32)
+            keep = (gap >= 0.0) & (gap <= rem_ref[0:n, 0:1])
+            bias_ref[0:n, cols] = jnp.where(keep, 0.0, -1e30)
+
+    masks = head_masks(width, HD)
+    heads = len(masks)
+    rows8 = lax.broadcasted_iota(jnp.int32, (8, width), 0)
+    lane8 = lax.broadcasted_iota(jnp.int32, (8, width), 1) // HD
+    picks = jnp.where(rows8 == lane8, 1.0, 0.0).astype(jnp.bfloat16)
+    scale = jnp.bfloat16(HD**-0.5)
+    zero = jnp.bfloat16(0)
+    offset = pl.multiple_of((step % per) * width, width)
+    nblocks = length // BLK
+    for i in reversed(range(nblocks)):
+        rows = pl.ds(i * BLK, BLK)
+        n = (i + 1) * BLK
+        query = q_ref[0, rows, :] * scale
+        grad = do_ref[0, rows, :]
+        prod = grad.astype(jnp.float32) * o_ref[0, rows, :].astype(jnp.float32)
+        upper, lower = two_parts(prod)
+        delta = dot_nt(picks, upper) + dot_nt(picks, lower)
+        keys = k_ref[0, 0:n, :]
+        vals = v_ref[0, 0:n, :]
+        bias = bias_ref[0:n, rows]
+        d_query = jnp.zeros((BLK, width), jnp.float32)
+        d_keys = jnp.zeros((n, width), jnp.float32)
+        d_vals = jnp.zeros((n, width), jnp.float32)
+        for h, mask in enumerate(masks):
+            q_head = jnp.where(mask, query, zero)
+            g_head = jnp.where(mask, grad, zero)
+            probs = jnp.exp(dot_nt(keys, q_head) + bias - lse_ref[0, h : h + 1, rows])
+            d_probs = dot_nt(vals, g_head)
+            d_scores = (probs * (d_probs - delta[h : h + 1, :])).astype(jnp.bfloat16)
+            d_vals = d_vals + dot_nn(probs.astype(jnp.bfloat16), g_head)
+            d_keys = d_keys + dot_nn(d_scores, q_head)
+            d_query = jnp.where(mask, dot_tn(d_scores, keys), d_query)
+        out_ref[0, rows, pl.ds(offset, width)] = (d_query * (HD**-0.5)).astype(jnp.bfloat16)
+        if i == nblocks - 1:
+            dk_ref[...] = d_keys
+            dv_ref[...] = d_vals
+        else:
+            dk_ref[0:n, :] += d_keys
+            dv_ref[0:n, :] += d_vals
+    out_ref[0, :, pl.ds(per * width + offset, width)] = dk_ref[...].astype(jnp.bfloat16)
+    out_ref[0, :, pl.ds(2 * per * width + offset, width)] = dv_ref[...].astype(jnp.bfloat16)
+
+
+def attn_backward(qkv, attended, d_att, lse_rows, remb, deps):
+    parts, length, width3 = qkv.shape
+    width = width3 // 3
+    lanes = min(256, width)
+    per = width // lanes
+    groups = parts * per
+    block = (1, length, lanes)
+    return pl.pallas_call(
+        attn_bwd_kernel,
+        grid=(groups,),
+        in_specs=[
+            pl.BlockSpec(block, lambda g: (g // per, 0, g % per)),
+            pl.BlockSpec(block, lambda g: (g // per, 0, per + g % per)),
+            pl.BlockSpec(block, lambda g: (g // per, 0, 2 * per + g % per)),
+            pl.BlockSpec(block, lambda g: (g // per, 0, g % per)),
+            pl.BlockSpec(block, lambda g: (g // per, 0, g % per)),
+            pl.BlockSpec((1, 8, length), lambda g: (g, 0, 0)),
+            pl.BlockSpec((length, 128), lambda g: (0, 0)),
+        ]
+        + [pl.BlockSpec(memory_space=pl.ANY)] * len(deps),
+        out_specs=pl.BlockSpec((1, length, width3), lambda g: (g // per, 0, 0)),
+        out_shape=jax.ShapeDtypeStruct(qkv.shape, jnp.bfloat16),
+        scratch_shapes=[
+            pltpu.VMEM((length, length), jnp.float32),
+            pltpu.VMEM((length, lanes), jnp.float32),
+            pltpu.VMEM((length, lanes), jnp.float32),
+        ],
+        compiler_params=pltpu.CompilerParams(vmem_limit_bytes=VMEM_LIMIT),
+        cost_estimate=pl.CostEstimate(
+            flops=70_000_000_000, bytes_accessed=20_000_000, transcendentals=0
+        ),
+        name="attn_bwd",
+    )(qkv, qkv, qkv, attended, d_att, lse_rows, remb, *deps)
+
+
+def conv_moved(ref, part, rows, first, pos):
+    width = ref.shape[2]
+    if first == 0:
+        before = jnp.zeros((8, width), jnp.float32)
+    else:
+        before = ref[part, pl.ds(first - 8, 8), :]
+    signal = jnp.concatenate([before, ref[part, pl.ds(first, rows), :]], axis=0)
+    moved = [signal[8:]]
+    for lag in range(1, TAPS):
+        shifted = pltpu.roll(signal, lag, 0)[8:]
+        moved.append(jnp.where(pos >= lag, shifted, 0.0))
+    return moved
+
+
+def wide_rows(ref, first, rows, width):
+    block = ref[pl.ds(first, rows), :]
+    return jnp.concatenate([block] * (width // block.shape[1]), axis=1)
+
+
+def mix_fwd_kernel(
+    z_ref, x_ref, cols_ref, cumt_ref, conv_ref, skip_ref, pos_ref, bs_ref, cs_ref, bst_ref,
+    ssm_ref, state_ref, ssq_ref, inner_ref,
+):
+    length = pos_ref.shape[0]
+    width = x_ref.shape[2]
+    step = pl.program_id(0)
+    chunks = length // BLK
+
+    @pl.when(step == 0)
+    def _():
+        for k in range(chunks):
+            rows = pl.ds(k * BLK, BLK)
+            spot = lax.broadcasted_iota(jnp.int32, (BLK, BLK), 0)
+            other = lax.broadcasted_iota(jnp.int32, (BLK, BLK), 1)
+            gap = (spot - other).astype(jnp.float32)
+            keep = (gap >= 0.0) & (gap <= pos_ref[rows, 0:1])
+            inner_ref[k] = jnp.where(keep, dot_nt(cs_ref[rows, :], bs_ref[rows, :]), 0.0)
+
+    masks = head_masks(width, PM)
+    heads = len(masks)
+    span = cols_ref.shape[1] // 4
+    turn = lax.rem(4 * span - step * heads, 4 * span)
+    state = jnp.zeros((bs_ref.shape[1], width), jnp.float32)
+    for k in range(chunks):
+        first = k * BLK
+        rows = pl.ds(first, BLK)
+        pos = wide_rows(pos_ref, first, BLK, width)
+        moved = conv_moved(x_ref, 0, BLK, first, pos)
+        pre = conv_ref[TAPS - 1 : TAPS, :] * moved[0]
+        for lag in range(1, TAPS):
+            pre = pre + conv_ref[TAPS - 1 - lag : TAPS - lag, :] * moved[lag]
+        xs = pre * sigmoid(pre)
+        cols = pltpu.roll(cols_ref[rows, :], turn, 1)
+        driven = (spread_heads(cols, 0, masks, width) * xs).astype(jnp.bfloat16)
+        out = skip_ref[...] * xs
+        inner = inner_ref[k]
+        for h, mask in enumerate(masks):
+            gap = cols[:, span + h : span + h + 1] - cumt_ref[0, h : h + 1, rows]
+            mixing = (jnp.exp2(jnp.minimum(gap, 0.0)) * inner).astype(jnp.bfloat16)
+            out = out + dot_nn(mixing, jnp.where(mask, driven, jnp.bfloat16(0)))
+        state_bf, state_rest = two_parts(state)
+        state_ref[k] = state_bf
+        if k > 0:
+            carry = spread_heads(cols, 2 * span, masks, width)
+            recalled = dot_nn(cs_ref[rows, :], state_bf) + dot_nn(cs_ref[rows, :], state_rest)
+            out = out + carry * recalled
+        if k < chunks - 1:
+            last = spread_heads(cols, 3 * span, masks, width)
+            fed, fed_rest = two_parts(last * driven.astype(jnp.float32))
+            fresh = dot_nn(bst_ref[:, rows], fed) + dot_nn(bst_ref[:, rows], fed_rest)
+            if k > 0:
+                fresh = fresh + carry[BLK - 1 : BLK, :] * state
+            state = fresh
+        ssm_ref[0, rows, :] = out
+        gate = z_ref[0, rows, :]
+        gated = out * gate * sigmoid(gate)
+        square = gated * gated
+        total = square[:, 0:128]
+        for lane in range(128, width, 128):
+            total = total + square[:, lane : lane + 128]
+
+        @pl.when(step == 0)
+        def _():
+            ssq_ref[rows, :] = total
+
+        @pl.when(step > 0)
+        def _():
+            ssq_ref[rows, :] += total
+
+
+def mix_forward(z, x, cols, cumt, conv, skip, posb, bs, cs, bst):
+    parts, length, inner_width = z.shape
+    state = bs.shape[1]
+    lanes = 256
+    per = inner_width // lanes
+    groups = parts * per
+    block = (1, length, lanes)
+    whole = lambda g: (0, 0)
+    return pl.pallas_call(
+        mix_fwd_kernel,
+        grid=(groups,),
+        in_specs=[
+            pl.BlockSpec(block, lambda g: (g // per, 0, g % per)),
+            pl.BlockSpec(block, lambda g: (g // per, 0, g % per)),
+            pl.BlockSpec(cols.shape, whole),
+            pl.BlockSpec((1,) + cumt.shape[1:], lambda g: (g, 0, 0)),
+            pl.BlockSpec((TAPS, lanes), lambda g: (0, g)),
+            pl.BlockSpec((1, lanes), lambda g: (0, g)),
+            pl.BlockSpec((length, 128), whole),
+            pl.BlockSpec((length, state), whole),
+            pl.BlockSpec((length, state), whole),
+            pl.BlockSpec((state, length), whole),
+        ],
+        out_specs=[
+            pl.BlockSpec(block, lambda g: (g // per, 0, g % per)),
+            pl.BlockSpec((length // BLK, state, lanes), lambda g: (0, 0, g)),
+            pl.BlockSpec((length, 128), whole),
+        ],
+        out_shape=[
+            jax.ShapeDtypeStruct((parts, length, inner_width), jnp.float32),
+            jax.ShapeDtypeStruct((length // BLK, state, parts * inner_width), jnp.bfloat16),
+            jax.ShapeDtypeStruct((length, 128), jnp.float32),
+        ],
+        scratch_shapes=[pltpu.VMEM((length // BLK, BLK, BLK), jnp.float32)],
+        compiler_params=pltpu.CompilerParams(vmem_limit_bytes=VMEM_LIMIT),
+        cost_estimate=pl.CostEstimate(
+            flops=20_000_000_000, bytes_accessed=30_000_000, transcendentals=0
+        ),
+        name="mix_fwd",
+    )(z, x, cols, cumt, conv, skip, posb, bs, cs, bst)
+
+
+def mix_bwd_kernel(
+    z_ref, x_ref, ssm_ref, dgn_ref, cols_ref, cumt_ref, conv_ref, skip_ref, gain_ref,
+    pos_ref, rem_ref, rg_ref, cross_ref, bs_ref, cs_ref, cst_ref, state_ref, *others,
+):
+    dz_ref, dx_ref, dcols_ref, sums_ref, dbs_ref, dcs_ref = others[-9:-3]
+    inner_ref, dinner_ref, dpre_ref = others[-3:]
+    length = pos_ref.shape[0]
+    width = x_ref.shape[2]
+    step = pl.program_id(0)
+    chunks = length // BLK
+    spot = lax.broadcasted_iota(jnp.int32, (BLK, BLK), 1)
+    other = lax.broadcasted_iota(jnp.int32, (BLK, BLK), 0)
+    gap = (spot - other).astype(jnp.float32)
+
+    @pl.when(step == 0)
+    def _():
+        for k in range(chunks):
+            rows = pl.ds(k * BLK, BLK)
+            keep = (gap >= 0.0) & (gap <= rem_ref[rows, 0:1])
+            inner_ref[k] = jnp.where(keep, dot_nt(bs_ref[rows, :], cs_ref[rows, :]), 0.0)
+        dinner_ref[...] = jnp.zeros(dinner_ref.shape, jnp.float32)
+        dbs_ref[...] = jnp.zeros(dbs_ref.shape, jnp.float32)
+        dcs_ref[...] = jnp.zeros(dcs_ref.shape, jnp.float32)
+        dcols_ref[...] = jnp.zeros(dcols_ref.shape, jnp.float32)
+
+    masks = head_masks(width, PM)
+    heads = len(masks)
+    zero = jnp.bfloat16(0)
+    head_of = lax.broadcasted_iota(jnp.int32, (width, 128), 0) // PM
+    lane_of = lax.broadcasted_iota(jnp.int32, (width, 128), 1)
+    span = cols_ref.shape[1] // 4
+    turn = lax.rem(4 * span - step * heads, 4 * span)
+    lane_of = lane_of - step * heads
+    pick_cum = jnp.where(head_of == lane_of, 1.0, 0.0).astype(jnp.bfloat16)
+    pick_step = jnp.where(head_of + span == lane_of, 1.0, 0.0).astype(jnp.bfloat16)
+    dpre_ref[pl.ds(length, 8), :] = jnp.zeros((8, width), jnp.float32)
+    sums_ref[...] = jnp.zeros(sums_ref.shape, jnp.float32)
+    d_state = jnp.zeros((bs_ref.shape[1], width), jnp.float32)
+    skip = skip_ref[...]
+    gain = gain_ref[...]
+    for k in reversed(range(chunks)):
+        first = k * BLK
+        rows = pl.ds(first, BLK)
+        pos = wide_rows(pos_ref, first, BLK, width)
+        moved = conv_moved(x_ref, 0, BLK, first, pos)
+        pre = conv_ref[TAPS - 1 : TAPS, :] * moved[0]
+        for lag in range(1, TAPS):
+            pre = pre + conv_ref[TAPS - 1 - lag : TAPS - lag, :] * moved[lag]
+        sig = sigmoid(pre)
+        xs = pre * sig
+        cols = pltpu.roll(cols_ref[rows, :], turn, 1)
+        step_wide = spread_heads(cols, 0, masks, width)
+        driven = (step_wide * xs).astype(jnp.bfloat16)
+        gate = z_ref[0, rows, :]
+        sig_z = sigmoid(gate)
+        silu_z = gate * sig_z
+        ssm = ssm_ref[0, rows, :]
+        gated = ssm * silu_z
+        d_gn = dgn_ref[0, rows, :]
+        rg = wide_rows(rg_ref, first, BLK, width)
+        cross = wide_rows(cross_ref, first, BLK, width)
+        scaled = rg * d_gn
+        d_gated = gain * scaled - gated * cross
+        sums_ref[5:6, :] += jnp.sum(gated * scaled, axis=0, keepdims=True)
+        dz_ref[0, rows, :] = (d_gated * ssm * (sig_z + silu_z * (1.0 - sig_z))).astype(jnp.bfloat16)
+        d_out = d_gated * silu_z
+        d_low = d_out.astype(jnp.bfloat16)
+        sums_ref[4:5, :] += jnp.sum(d_out * xs, axis=0, keepdims=True)
+        inner = inner_ref[k]
+        d_inner = dinner_ref[k]
+        d_driven = jnp.zeros((BLK, width), jnp.float32)
+        for h, mask in enumerate(masks):
+            gap_h = cumt_ref[0, h : h + 1, rows] - cols[:, span + h : span + h + 1]
+            decay = jnp.exp2(jnp.minimum(gap_h, 0.0))
+            mixing = (decay * inner).astype(jnp.bfloat16)
+            d_driven = d_driven + dot_nn(mixing, jnp.where(mask, d_low, zero))
+            d_inner = d_inner + decay * dot_nt(jnp.where(mask, driven, zero), d_low)
+        dinner_ref[k] = d_inner
+        if k > 0:
+            carry = spread_heads(cols, 2 * span, masks, width)
+            carried, carried_rest = two_parts(carry * d_low.astype(jnp.float32))
+            dcs_ref[rows, :] += dot_nt(carried, state_ref[k])
+        if k < chunks - 1:
+            last = spread_heads(cols, 3 * span, masks, width)
+            fed = (last * driven.astype(jnp.float32)).astype(jnp.bfloat16)
+            d_state_bf, d_state_rest = two_parts(d_state)
+            dbs_ref[rows, :] += dot_nt(fed, d_state_bf)
+            recalled = dot_nn(bs_ref[rows, :], d_state_bf) + dot_nn(bs_ref[rows, :], d_state_rest)
+            d_driven = d_driven + last * recalled
+        if k > 0:
+            fresh = dot_nn(cst_ref[:, rows], carried) + dot_nn(cst_ref[:, rows], carried_rest)
+            if k < chunks - 1:
+                fresh = fresh + carry[BLK - 1 : BLK, :] * d_state
+            d_state = fresh
+        moved_out = ssm - skip * xs
+        balance = d_low.astype(jnp.float32) * moved_out - driven.astype(jnp.float32) * d_driven
+        upper, lower = two_parts(balance)
+        d_cum = dot_nn(upper, pick_cum) + dot_nn(lower, pick_cum)
+        d_driven = d_driven.astype(jnp.bfloat16).astype(jnp.float32)
+        upper, lower = two_parts(d_driven * xs)
+        dcols_ref[rows, :] += d_cum + dot_nn(upper, pick_step) + dot_nn(lower, pick_step)
+        d_xs = skip * d_out + step_wide * d_driven
+        d_pre = d_xs * (sig + xs * (1.0 - sig))
+        dpre_ref[rows, :] = d_pre
+        for lag in range(TAPS):
+            sums_ref[TAPS - 1 - lag : TAPS - lag, :] += jnp.sum(
+                d_pre * moved[lag], axis=0, keepdims=True
+            )
+        after = jnp.concatenate([d_pre, dpre_ref[pl.ds(first + BLK, 8), :]], axis=0)
+        rem = wide_rows(rem_ref, first, BLK, width)
+        d_x = conv_ref[TAPS - 1 : TAPS, :] * d_pre
+        for lag in range(1, TAPS):
+            shifted = pltpu.roll(after, BLK + 8 - lag, 0)[0:BLK]
+            d_x = d_x + conv_ref[TAPS - 1 - lag : TAPS - lag, :] * jnp.where(
+                rem >= lag, shifted, 0.0
+            )
+        dx_ref[0, rows, :] = d_x.astype(jnp.bfloat16)
+
+    @pl.when(step == pl.num_programs(0) - 1)
+    def _():
+        for k in range(chunks):
+            rows = pl.ds(k * BLK, BLK)
+            keep = (gap >= 0.0) & (gap <= rem_ref[rows, 0:1])
+            d_inner = jnp.where(keep, dinner_ref[k], 0.0)
+            dbs_ref[rows, :] += dot_nn(d_inner.astype(jnp.bfloat16), cs_ref[rows, :])
+            dcs_ref[rows, :] += dot_nn(d_inner.T.astype(jnp.bfloat16), bs_ref[rows, :])
+
+
+def mix_backward(
+    z, x, ssm, d_gn, cols, cumt, conv, skip, gain, posb, remb, rgb, crossb, bs, cs, cst, states, deps
+):
+    parts, length, inner_width = ssm.shape
+    state = bs.shape[1]
+    lanes = 256
+    per = inner_width // lanes
+    groups = parts * per
+    block = (1, length, lanes)
+    whole = lambda g: (0, 0)
+    own = lambda g: (g // per, 0, g % per)
+    return pl.pallas_call(
+        mix_bwd_kernel,
+        grid=(groups,),
+        in_specs=[
+            pl.BlockSpec(block, own),
+            pl.BlockSpec(block, own),
+            pl.BlockSpec(block, own),
+            pl.BlockSpec(block, own),
+            pl.BlockSpec(cols.shape, whole),
+            pl.BlockSpec((1,) + cumt.shape[1:], lambda g: (g, 0, 0)),
+            pl.BlockSpec((TAPS, lanes), lambda g: (0, g)),
+            pl.BlockSpec((1, lanes), lambda g: (0, g)),
+            pl.BlockSpec((1, lanes), lambda g: (0, g)),
+            pl.BlockSpec((length, 128), whole),
+            pl.BlockSpec((length, 128), whole),
+            pl.BlockSpec((length, 128), whole),
+            pl.BlockSpec((length, 128), whole),
+            pl.BlockSpec((length, state), whole),
+            pl.BlockSpec((length, state), whole),
+            pl.BlockSpec((state, length), whole),
+            pl.BlockSpec((length // BLK, state, lanes), lambda g: (0, 0, g)),
+        ]
+        + [pl.BlockSpec(memory_space=pl.ANY)] * len(deps),
+        out_specs=[
+            pl.BlockSpec(block, own),
+            pl.BlockSpec(block, own),
+            pl.BlockSpec((length, 128), whole),
+            pl.BlockSpec((8, lanes), lambda g: (0, g)),
+            pl.BlockSpec((length, state), whole),
+            pl.BlockSpec((length, state), whole),
+        ],
+        out_shape=[
+            jax.ShapeDtypeStruct((parts, length, inner_width), jnp.bfloat16),
+            jax.ShapeDtypeStruct(x.shape, jnp.bfloat16),
+            jax.ShapeDtypeStruct((length, 128), jnp.float32),
+            jax.ShapeDtypeStruct((8, parts * inner_width), jnp.float32),
+            jax.ShapeDtypeStruct((length, state), jnp.float32),
+            jax.ShapeDtypeStruct((length, state), jnp.float32),
+        ],
+        scratch_shapes=[
+            pltpu.VMEM((length // BLK, BLK, BLK), jnp.float32),
+            pltpu.VMEM((length // BLK, BLK, BLK), jnp.float32),
+            pltpu.VMEM((length + 8, lanes), jnp.float32),
+        ],
+        compiler_params=pltpu.CompilerParams(vmem_limit_bytes=VMEM_LIMIT),
+        cost_estimate=pl.CostEstimate(
+            flops=50_000_000_000, bytes_accessed=50_000_000, transcendentals=0
+        ),
+        name="mix_bwd",
+    )(
+        z, x, ssm, d_gn, cols, cumt, conv, skip, gain, posb, remb, rgb, crossb, bs, cs, cst,
+        states, *deps,
+    )
+
+
+def tile_of(columns, limit=512):
+    size = limit
+    while columns % size:
+        size -= 128
+    return size
+
+
+def part_product(
+    left, right, dtype, first=0, columns=None, extra=None, deps=(), fold=1, into=None, place=0, room=None
+):
+    parts, depth, whole = right.shape
+    rows = left.shape[0]
+    columns = whole - first if columns is None else columns
+    tile = tile_of(columns)
+    while first % tile or place % tile:
+        tile = tile_of(columns, tile - 128)
+    begin = first // tile
+    count = columns // tile
+    block = (1, rows, tile)
+    shift = place // tile
+    room = fold * columns if room is None else room
+    in_specs = [
+        pl.BlockSpec((rows, depth), lambda m, n: (0, 0)),
+        pl.BlockSpec((1, depth, tile), lambda m, n: (m, 0, begin + n)),
+    ]
+    operands = [left, right]
+    if extra is not None:
+        in_specs.append(pl.BlockSpec(block, lambda m, n: (m, 0, n)))
+        operands.append(extra)
+    aliases = {}
+    if into is not None:
+        aliases = {len(operands): 0}
+        deps = (into,) + tuple(deps)
+        room = into.shape[2]
+    in_specs += [pl.BlockSpec(memory_space=pl.ANY)] * len(deps)
+
+    def body(left_ref, right_ref, *others):
+        total = dot_nn(left_ref[...], right_ref[0])
+        if extra is not None:
+            total = total + others[0][0].astype(jnp.float32)
+        others[-1][0] = total.astype(dtype)
+
+    return pl.pallas_call(
+        body,
+        grid=(parts, count),
+        in_specs=in_specs,
+        out_specs=pl.BlockSpec(
+            block, lambda m, n: (m // fold, 0, shift + (m % fold) * count + n)
+        ),
+        out_shape=jax.ShapeDtypeStruct((parts // fold, rows, room), dtype),
+        input_output_aliases=aliases,
+        compiler_params=pltpu.CompilerParams(vmem_limit_bytes=VMEM_LIMIT),
+        cost_estimate=pl.CostEstimate(
+            flops=2 * parts * rows * depth * columns,
+            bytes_accessed=parts * depth * columns * 2 + parts * rows * columns * 4,
+            transcendentals=0,
+        ),
+        name="part_product",
+    )(*operands, *deps)
+
+
+def part_back(left, right, first=0, start=None, deps=()):
+    parts, rows, columns = left.shape
+    width = right.shape[1]
+    fold = parts // right.shape[0]
+    tile = tile_of(columns)
+    while first % tile:
+        tile = tile_of(columns, tile - 128)
+    begin = first // tile
+    count = columns // tile
+    in_specs = [
+        pl.BlockSpec((1, rows, tile), lambda m, n: (m, 0, n)),
+        pl.BlockSpec(
+            (1, width, tile), lambda m, n: (m // fold, 0, begin + (m % fold) * count + n)
+        ),
+    ]
+    operands = [left, right]
+    if start is not None:
+        in_specs.append(pl.BlockSpec((rows, width), lambda m, n: (0, 0)))
+        operands.append(start)
+    in_specs += [pl.BlockSpec(memory_space=pl.ANY)] * len(deps)
+
+    def body(left_ref, right_ref, *others):
+        out_ref = others[-1]
+        total = dot_nt(left_ref[0], right_ref[0])
+        opening = (pl.program_id(0) == 0) & (pl.program_id(1) == 0)
+
+        @pl.when(opening)
+        def _():
+            out_ref[...] = total if start is None else total + others[0][...]
+
+        @pl.when(jnp.logical_not(opening))
+        def _():
+            out_ref[...] += total
+
+    return pl.pallas_call(
+        body,
+        grid=(parts, count),
+        in_specs=in_specs,
+        out_specs=pl.BlockSpec((rows, width), lambda m, n: (0, 0)),
+        out_shape=jax.ShapeDtypeStruct((rows, width), jnp.float32),
+        compiler_params=pltpu.CompilerParams(vmem_limit_bytes=VMEM_LIMIT),
+        cost_estimate=pl.CostEstimate(
+            flops=2 * parts * rows * columns * width,
+            bytes_accessed=2 * parts * columns * (rows + width) + 4 * rows * width,
+            transcendentals=0,
+        ),
+        name="part_back",
+    )(*operands, *deps)
+
+
+def outer_kernel(left_ref, right_ref, out_ref):
+    total = dot_tn(left_ref[0], right_ref[...]).astype(jnp.bfloat16)
+    rows = out_ref.shape[1]
+    width = right_ref.shape[1]
+    wraps = total.shape[0] // rows
+    piece = 64
+    for i in range(rows // piece):
+        for w in range(wraps):
+            begin = (i * wraps + w) * piece
+            out_ref[0, pl.ds(i * piece, piece), pl.ds(w * width, width)] = total[
+                begin : begin + piece
+            ]
+
+
+def outer_into(left, right, wraps, place, room):
+    parts, length, columns = left.shape
+    width = right.shape[1]
+    tile = 256 * wraps
+    begin = place // (wraps * width)
+    return pl.pallas_call(
+        outer_kernel,
+        grid=(parts, columns // tile),
+        in_specs=[
+            pl.BlockSpec((1, length, tile), lambda m, n: (m, 0, n)),
+            pl.BlockSpec((length, width), lambda m, n: (0, 0)),
+        ],
+        out_specs=pl.BlockSpec((1, tile // wraps, wraps * width), lambda m, n: (m, n, begin)),
+        out_shape=jax.ShapeDtypeStruct((parts, columns // wraps, room), jnp.bfloat16),
+        compiler_params=pltpu.CompilerParams(vmem_limit_bytes=VMEM_LIMIT),
+        cost_estimate=pl.CostEstimate(
+            flops=2 * parts * length * columns * width,
+            bytes_accessed=2 * parts * columns * (length + width),
+            transcendentals=0,
+        ),
+        name="outer_into",
+    )(left, right)
+
+
+def unfold_kernel(in_ref, out_ref):
+    count = out_ref.shape[1]
+    width = out_ref.shape[2]
+    for j in range(count):
+        out_ref[:, j, :] = in_ref[:, j * width : (j + 1) * width].astype(jnp.float32)
+
+
+def unfold(value, count, width):
+    rows = value.shape[0]
+    step = 128
+    return pl.pallas_call(
+        unfold_kernel,
+        grid=(rows // step,),
+        in_specs=[pl.BlockSpec((step, count * width), lambda n: (n, 0))],
+        out_specs=pl.BlockSpec((step, count, width), lambda n: (n, 0, 0)),
+        out_shape=jax.ShapeDtypeStruct((rows, count, width), jnp.float32),
+        compiler_params=pltpu.CompilerParams(vmem_limit_bytes=VMEM_LIMIT),
+        cost_estimate=pl.CostEstimate(
+            flops=0, bytes_accessed=6 * rows * count * width, transcendentals=0
+        ),
+        name="unfold",
+    )(value)
+
+
+def ffn_in_kernel(left_ref, gate_w_ref, up_w_ref, gate_ref, up_ref, hidden_ref):
+    gate = dot_nn(left_ref[...], gate_w_ref[0])
+    upper = dot_nn(left_ref[...], up_w_ref[0])
+    gate_ref[0] = gate.astype(jnp.bfloat16)
+    up_ref[0] = upper.astype(jnp.bfloat16)
+    hidden_ref[0] = (gate * sigmoid(gate) * upper).astype(jnp.bfloat16)
+
+
+def ffn_forward(left, right, half):
+    parts, depth, _ = right.shape
+    rows = left.shape[0]
+    tile = tile_of(half)
+    count = half // tile
+    block = pl.BlockSpec((1, rows, tile), lambda m, n: (m, 0, n))
+    shape = jax.ShapeDtypeStruct((parts, rows, half), jnp.bfloat16)
+    return pl.pallas_call(
+        ffn_in_kernel,
+        grid=(parts, count),
+        in_specs=[
+            pl.BlockSpec((rows, depth), lambda m, n: (0, 0)),
+            pl.BlockSpec((1, depth, tile), lambda m, n: (m, 0, n)),
+            pl.BlockSpec((1, depth, tile), lambda m, n: (m, 0, count + n)),
+        ],
+        out_specs=[block, block, block],
+        out_shape=[shape, shape, shape],
+        compiler_params=pltpu.CompilerParams(vmem_limit_bytes=VMEM_LIMIT),
+        cost_estimate=pl.CostEstimate(
+            flops=4 * parts * rows * depth * half,
+            bytes_accessed=parts * half * (4 * depth + 6 * rows),
+            transcendentals=0,
+        ),
+        name="ffn_in",
+    )(left, right, right)
+
+
+def ffn_back_kernel(left_ref, right_ref, gate_ref, up_ref, out_ref):
+    grad = dot_nn(left_ref[...], right_ref[0])
+    gate = gate_ref[0].astype(jnp.float32)
+    sig = sigmoid(gate)
+    act = gate * sig
+    slope = sig + act * (1.0 - sig)
+    out_ref[0, 0] = (grad * up_ref[0].astype(jnp.float32) * slope).astype(jnp.bfloat16)
+    out_ref[0, 1] = (grad * act).astype(jnp.bfloat16)
+
+
+def ffn_backward(left, right, first, gate, upper):
+    parts, rows, half = gate.shape
+    depth = left.shape[1]
+    tile = tile_of(half)
+    begin = first // tile
+    block = pl.BlockSpec((1, rows, tile), lambda m, n: (m, 0, n))
+    return pl.pallas_call(
+        ffn_back_kernel,
+        grid=(parts, half // tile),
+        in_specs=[
+            pl.BlockSpec((rows, depth), lambda m, n: (0, 0)),
+            pl.BlockSpec((1, depth, tile), lambda m, n: (m, 0, begin + n)),
+            block,
+            block,
+        ],
+        out_specs=pl.BlockSpec((1, 2, rows, tile), lambda m, n: (m, 0, 0, n)),
+        out_shape=jax.ShapeDtypeStruct((parts, 2, rows, half), jnp.bfloat16),
+        compiler_params=pltpu.CompilerParams(vmem_limit_bytes=VMEM_LIMIT),
+        cost_estimate=pl.CostEstimate(
+            flops=2 * parts * rows * depth * half,
+            bytes_accessed=parts * half * (2 * depth + 8 * rows),
+            transcendentals=0,
+        ),
+        name="ffn_back",
+    )(left, right, gate, upper)
+
+
+def bit_of(index, bit):
+    return (index >> bit) & 1
+
+
+def swap(value, stage):
+    if stage is None:
+        return lax.ppermute(value, "mp", [(0, 1), (1, 0)])
+    count = lax.axis_size("dp")
+    return lax.ppermute(value, "dp", [(i, i ^ (1 << stage)) for i in range(count)])
+
+
+def my_bit(stage):
+    if stage is None:
+        return lax.axis_index("mp")
+    return bit_of(lax.axis_index("dp"), stage)
+
+
+def take_half(value, which):
+    half = value.shape[0] // 2
+    return lax.dynamic_slice_in_dim(value, which * half, half, 0)
+
+
+def join(own, other, bit):
+    first = jnp.where(bit == 0, own, other)
+    second = jnp.where(bit == 0, other, own)
+    return jnp.concatenate([first, second], axis=0)
+
+
+def add_low(left, right):
+    return (left.astype(jnp.float32) + right.astype(jnp.float32)).astype(jnp.bfloat16)
+
+
+def dp_bits():
+    return lax.axis_size("dp").bit_length() - 1
+
+
+def ring_order():
+    order = []
+    layers = lax.axis_size("dp") // 4
+    for side in range(2):
+        for spot in range(layers):
+            layer = spot if side == 0 else layers - 1 - spot
+            for core in range(2):
+                order.append(layer * 4 + side * 2 + core)
+    return order
+
+
+def block_of(device, bits):
+    value = 0
+    for bit in range(bits):
+        value = value * 2 + ((device >> bit) & 1)
+    return value
+
+
+def sum_stages(total, order):
+    for stage in order:
+        mine = my_bit(stage)
+        if stage is None:
+            received = swap(lax.dynamic_index_in_dim(total, 1 - mine, 0, keepdims=False), None)
+            kept = lax.dynamic_index_in_dim(total, mine, 0, keepdims=False)
+        else:
+            axis = total.ndim - 2
+            half = total.shape[axis] // 2
+            received = swap(
+                lax.dynamic_slice_in_dim(total, (1 - mine) * half, half, axis), stage
+            )
+            kept = lax.dynamic_slice_in_dim(total, mine * half, half, axis)
+        total = add_low(kept, received)
+    return total
+
+
+def x_first():
+    return [None] + list(range(1, dp_bits()))
+
+
+def y_first():
+    return [1, None] + list(range(2, dp_bits()))
+
+
+def gather_sum(piece, reversed_blocks=True):
+    bits = dp_bits()
+    order = ring_order()
+    ringed = lax.all_gather(piece, "dp", axis=0, axis_index_groups=[order])
+    blocks = [None] * len(order)
+    for place, device in enumerate(order):
+        blocks[block_of(device, bits) if reversed_blocks else device] = ringed[place]
+    return jnp.concatenate(blocks, axis=0)
+
+
+def around_order(part):
+    layers = lax.axis_size("dp") // 4
+    order = []
+    for turn in range(2):
+        side = turn if part == 0 else 1 - turn
+        for spot in range(layers):
+            layer = layers - 1 - spot if turn == 0 else spot
+            for core in range(2):
+                order.append((layer * 4 + side * 2 + core) * 2 + part)
+    return order
+
+
+def ring_scatter(value):
+    order = around_order(0) + around_order(1)
+    return lax.psum_scatter(
+        value,
+        ("dp", "mp"),
+        scatter_dimension=0,
+        tiled=True,
+        axis_index_groups=[order],
+    )
+
+
+def ring_gather(piece):
+    return lax.all_gather(
+        piece,
+        ("dp", "mp"),
+        axis=0,
+        tiled=True,
+        axis_index_groups=[around_order(0), around_order(1)],
+    )
+
+
+def gather_steps(shard, order):
+    bits = dp_bits()
+    value = shard.reshape((1,) * (bits + 1) + shard.shape)
+    for stage in order:
+        axis = 0 if stage is None else bits - stage
+        other = swap(value, stage)
+        bit = my_bit(stage)
+        value = jnp.concatenate(
+            [jnp.where(bit == 0, value, other), jnp.where(bit == 0, other, value)], axis=axis
+        )
+    return value.reshape(2, -1, shard.shape[1])
+
+
+def gather_y_last():
+    return list(range(dp_bits() - 1, 1, -1)) + [None, 1, 0]
+
+
+def gather_x_last():
+    return list(range(dp_bits() - 1, 1, -1)) + [1, None, 0]
+
+
+def spread_all(value):
+    for stage in [0, 1, None] + list(range(2, dp_bits())):
+        value = value + swap(value, stage)
+    return value
+
+
+def reduce_table(value):
+    stages = [0, None] + list(range(1, dp_bits()))
+    for stage in stages:
+        mine = my_bit(stage)
+        value = take_half(value, mine) + swap(take_half(value, 1 - mine), stage)
+    for stage in reversed(stages):
+        value = join(value, swap(value, stage), my_bit(stage))
+    return value
+
+
+def gather_small(shard):
+    bits = dp_bits()
+    value = shard[None]
+    for bit in range(bits):
+        value = join(value, swap(value, bit), my_bit(bit))
+    return value.reshape((-1,) + shard.shape[1:])
+
+
+def gather_weight(shard):
+    return lax.all_gather(shard, ("mp", "dp"), axis=0, tiled=True).reshape(
+        lax.axis_size("mp"), -1, shard.shape[1]
+    )
+
+
+def rms_back(hidden, gain, grad):
+    inv = lax.rsqrt(jnp.mean(hidden * hidden, axis=-1, keepdims=True) + 1e-05)
+    weighted = grad * gain
+    mean = jnp.mean(hidden * weighted, axis=-1, keepdims=True)
+    d_gain = jnp.sum(hidden * inv * grad, axis=0)
+    return inv * weighted - hidden * (inv * inv * inv * mean), d_gain
+
+
+def in_groups(per_head, groups):
+    length = per_head.shape[0]
+    return per_head.reshape(length, groups, -1).transpose(1, 0, 2)
+
+
+def wide128(column):
+    return jnp.broadcast_to(column, (column.shape[0], 128))
+
+
+def dot_parts(left, right):
+    return lax.dot_general(
+        left, right, (((1,), (1,)), ((), ())), preferred_element_type=jnp.float32
+    ).transpose(1, 0, 2)
+
+
+def dot_back(left, right):
+    total = dot_nt(left[0], right[0])
+    for part in range(1, left.shape[0]):
+        total = total + dot_nt(left[part], right[part])
+    return total
+
+
+def on_device_rows(
+    byte_ids,
+    segment_ids,
+    embed_table,
+    patch_weight,
+    norm1_gain,
+    mamba_in,
+    mamba_dt,
+    mamba_bc,
+    conv_x,
+    conv_bc,
+    dt_bias,
+    a_log,
+    d_skip,
+    gate_gain,
+    mamba_out,
+    norm2_gain,
+    attn_qkv,
+    attn_out,
+    norm3_gain,
+    ffn_in,
+    ffn_out,
+    d_out,
+):
+    low = jnp.bfloat16
+    parts = lax.axis_size("mp")
+    part = lax.axis_index("mp")
+    shard = mamba_in.shape[0]
+    per_pos = PATCH // parts
+    inner_width = mamba_in.shape[2]
+    heads_part = mamba_dt.shape[1]
+    state = mamba_bc.shape[1] // 2
+    lanes = 256
+    groups = parts * inner_width // lanes
+
+    def exchange(value):
+        own = lax.dynamic_index_in_dim(value, part, 0, keepdims=False)
+        other = swap(lax.dynamic_index_in_dim(value, 1 - part, 0, keepdims=False), None)
+        return join(own, other, part)
+
+    ids = exchange(byte_ids)
+    seg = exchange(segment_ids)
+    length = seg.shape[0]
+
+    def both_parts(value):
+        own = value
+        other = swap(value, None)
+        return join(own[None], other[None], part)
+
+    conv_full = jnp.concatenate(list(both_parts(conv_x)), axis=1)
+    vectors = both_parts(jnp.concatenate([dt_bias, a_log, d_skip, gate_gain]))
+    heads = parts * heads_part
+    bias_full, alog_full, skip_full = (
+        vectors[:, i * heads_part : (i + 1) * heads_part].reshape(heads) for i in range(3)
+    )
+    ggain_full = vectors[:, 3 * heads_part :].reshape(parts * inner_width)
+
+    bc_half = lax.dynamic_slice_in_dim(mamba_bc, part * state, state, 1)
+    pad = (-heads_part) % 128
+    shard_z = mamba_in[:, 0]
+    shard_x = jnp.concatenate(
+        [mamba_in[:, 1], bc_half, mamba_dt, jnp.zeros((shard, pad), low)], axis=1
+    )
+    shard_qkv = attn_qkv.reshape(shard, -1)
+    shard_mid = jnp.concatenate([shard_qkv, mamba_out.T, attn_out.T], axis=1)
+    shard_ffn = jnp.concatenate([ffn_in.reshape(shard, -1), ffn_out.T], axis=1)
+    width_in = ffn_in.shape[1] * ffn_in.shape[2]
+
+    table = gather_small(embed_table)
+    rows_by_pos = patch_weight.reshape(per_pos, -1, patch_weight.shape[1])
+    mapped = lax.dot_general(
+        rows_by_pos, table, (((1,), (1,)), ((), ())), preferred_element_type=jnp.float32
+    ).astype(low)
+    mapped = mapped.transpose(1, 0, 2).reshape(rows_by_pos.shape[2], -1)
+    mapped = gather_steps(mapped, gather_y_last())
+    w_z = gather_steps(shard_z, gather_x_last())
+    w_x = gather_steps(shard_x, gather_y_last())
+    mapped_ready = mapped[0, 0, 0] * 0
+    ready = (w_z[0, 0, 0] + w_x[0, 0, 0]) * 0 + mapped_ready
+    w_mid = gather_weight(shard_mid + ready)
+    w_ffn = gather_weight(shard_ffn + ready)
+    width_qkv = shard_qkv.shape[1]
+
+    onehot = (ids[:, :, None] == jnp.arange(VOCAB, dtype=jnp.int32)[None, None, :]).astype(low)
+    onehot = onehot.reshape(length, parts, per_pos * VOCAB).transpose(1, 0, 2)
+    resid0 = dot_back(onehot, mapped)
+
+    spots = jnp.arange(length, dtype=jnp.int32)
+    changed = jnp.concatenate([jnp.ones((1,), bool), seg[1:] != seg[:-1]])
+    same = seg[:, None] == seg[None, :]
+    pos = jnp.sum((same & (spots[None, :] < spots[:, None])).astype(jnp.int32), axis=1)
+    rem = jnp.sum((same & (spots[None, :] > spots[:, None])).astype(jnp.int32), axis=1)
+    posb = wide128(pos.astype(jnp.float32)[:, None])
+    remb = wide128(rem.astype(jnp.float32)[:, None])
+
+    u1 = rms_apply(resid0, norm1_gain).astype(low)
+    gate = part_product(u1, w_z, jnp.float32)
+    fed = part_product(u1, w_x, jnp.float32)
+    first_dt = inner_width + state
+    bc = jnp.concatenate([fed[p, :, inner_width:first_dt] for p in range(parts)], axis=1)
+    dtr = jnp.concatenate([fed[p, :, first_dt : first_dt + heads_part] for p in range(parts)], 1)
+    bc_act, pull_bc = jax.vjp(
+        lambda signal, taps: jax.nn.silu(conv_rows(signal, taps, seg)), bc, conv_bc
+    )
+    bcs = bc_act.astype(low)
+    bs = bcs[:, :state]
+    cs = bcs[:, state:]
+    steps = jax.nn.softplus(dtr + bias_full)
+    rate = -jnp.exp(alog_full)
+    lower = (spots[:, None] >= spots[None, :]).astype(jnp.float32)
+    cum = lax.dot_general(
+        lower, rate * steps, (((1,), (0,)), ((), ())), precision=lax.Precision.HIGHEST
+    )
+    chunk = spots // BLK
+    chunk_first = chunk * BLK
+    ends = cum.reshape(length // BLK, BLK, heads)[:, BLK - 1]
+    starts = jnp.concatenate([jnp.zeros((1, heads), jnp.float32), ends[:-1]], axis=0)
+    start_wide = jnp.repeat(starts, BLK, axis=0)
+    end_wide = jnp.repeat(ends, BLK, axis=0)
+    carried = (pos > spots - chunk_first) & (chunk > 0)
+    carry = jnp.where(carried[:, None], jnp.exp(cum - start_wide), 0.0)
+    lasting = spots + rem >= chunk_first + BLK - 1
+    last = jnp.where(lasting[:, None], jnp.exp(end_wide - cum), 0.0)
+    cum2 = cum * LOG2E
+    cols = jnp.concatenate([steps, cum2, carry, last], axis=1)
+    cumt = cum2.T.reshape(groups, -1, length)
+    skip_wide = jnp.repeat(skip_full, PM)[None]
+    ssm, states, squares = mix_forward(
+        gate, fed, cols, cumt, conv_full, skip_wide, posb, bs, cs, bs.T
+    )
+    factor = lax.rsqrt(jnp.sum(squares, axis=1, keepdims=True) / DIN + 1e-05)
+    gain_parts = ggain_full.reshape(parts, 1, inner_width)
+    gnormed = (ssm * gate * sigmoid(gate) * factor[None] * gain_parts).astype(low)
+    resid1 = part_back(gnormed, w_mid, first=width_qkv, start=resid0)
+
+    u2 = rms_apply(resid1, norm2_gain).astype(low)
+    qkv = part_product(u2, w_mid, low, columns=width_qkv)
+    attended, logs = attn_forward(qkv, posb)
+    resid2 = part_back(attended, w_mid, first=width_qkv + inner_width, start=resid1)
+
+    u3 = rms_apply(resid2, norm3_gain).astype(low)
+    half = width_in // 2
+    gate3, up3, hidden = ffn_forward(u3, w_ffn, half)
+    mixed_row = part_back(hidden, w_ffn, first=width_in, start=resid2)
+
+    piece = length // parts
+    mine = lax.dynamic_slice_in_dim(mixed_row, part * piece, piece, 0)
+    theirs = swap(lax.dynamic_slice_in_dim(mixed_row, (1 - part) * piece, piece, 0), None)
+    mixed = join(mine[None], theirs[None], part)
+
+    core = my_bit(0)
+
+    def half_rows(value, which):
+        count = value.shape[0] // 2
+        return lax.dynamic_slice_in_dim(value, which * count, count, 0)
+
+    def half_lanes(value, which):
+        count = value.shape[2] // 2
+        return lax.dynamic_slice_in_dim(value, which * count, count, 2)
+
+    def sum_cores(left_t, right):
+        received = swap(part_product(half_rows(left_t, 1 - core), right, low), 0)
+        return part_product(half_rows(left_t, core), right, low, extra=received)
+
+    def outer_parts(left, right):
+        return lax.dot_general(
+            left, right, (((1,), (0,)), ((), ())), preferred_element_type=jnp.float32
+        )
+
+    def sum_cores_back(left, right):
+        received = swap(outer_parts(half_lanes(left, 1 - core), right).astype(low), 0)
+        return add_low(outer_parts(half_lanes(left, core), right), received)
+
+    cot = exchange(d_out + ssm[0, 0, 0] * 0)
+    dm3 = cot.astype(low)
+    d_gate_up = ffn_backward(dm3, w_ffn, width_in, gate3, up3)
+    quarter = d_gate_up.reshape(2 * parts, length, half)
+    part_ffn = outer_into(hidden, dm3, 2, width_in, 3 * width_in // 2)
+    part_ffn = part_product(u3.T, quarter, low, fold=2, into=part_ffn)
+    sum_ffn = ring_scatter(part_ffn.reshape(-1, part_ffn.shape[2]))
+    back_u3 = part_back(quarter, w_ffn, deps=[part_ffn])
+    back, d_gain3 = rms_back(resid2, norm3_gain, back_u3)
+    cot = cot + back
+
+    dm2 = cot.astype(low)
+    d_att = part_product(dm2, w_mid, low, first=width_qkv + inner_width)
+    part_aout = sum_cores_back(attended, dm2)
+    log_rows = jnp.pad(logs[:, :, :4].transpose(0, 2, 1), ((0, 0), (0, 4), (0, 0)))
+    d_qkv = attn_backward(
+        qkv, attended, d_att, log_rows, remb, []
+    )
+    part_qkv = sum_cores(u2.T, d_qkv)
+    back, d_gain2 = rms_back(resid1, norm2_gain, part_back(d_qkv, w_mid, deps=[part_qkv]))
+    cot = cot + back
+
+    dm1 = cot.astype(low)
+    d_gn = part_product(dm1, w_mid, jnp.float32, first=width_qkv, columns=inner_width)
+    part_mout = sum_cores_back(gnormed, dm1)
+    gated = ssm * gate * sigmoid(gate)
+    cross = jnp.sum(jnp.sum(gated * gain_parts * d_gn, axis=2), axis=0)[:, None]
+    cross = factor * factor * factor * cross / DIN
+    d_z, d_fed, d_cols, sums, d_bs, d_cs = mix_backward(
+        gate,
+        fed,
+        ssm,
+        d_gn,
+        cols,
+        cumt,
+        conv_full,
+        skip_wide,
+        ggain_full[None],
+        posb,
+        remb,
+        wide128(factor),
+        wide128(cross),
+        bs,
+        cs,
+        cs.T,
+        states,
+        [part_qkv, part_mout, part_aout, sum_ffn],
+    )
+    order = x_first()
+    stage_qkv = sum_stages(part_qkv, order[:1])
+    last_qkv = sum_stages(stage_qkv, order[1:2])
+    piece_qkv = sum_stages(last_qkv, order[2:])
+    order = y_first()
+    stage_mout = sum_stages(part_mout, order[:1])
+    last_mout = sum_stages(stage_mout, order[1:2])
+    piece_mout = sum_stages(last_mout, order[2:])
+    stage_aout = sum_stages(part_aout, order[:1])
+    last_aout = sum_stages(stage_aout, order[1:2])
+    piece_aout = sum_stages(last_aout, order[2:])
+    rows_aout = jnp.concatenate(jnp.split(piece_aout, 2, axis=1), axis=0)
+    grad_mid = gather_sum(jnp.concatenate([piece_qkv, piece_mout, rows_aout], axis=1))
+    width_mout = piece_mout.shape[1]
+    grad_qkv = grad_mid[:, :width_qkv]
+    grad_mout = grad_mid[:, width_qkv : width_qkv + width_mout]
+    count = rows_aout.shape[0]
+    grad_aout = grad_mid[:, width_qkv + width_mout :].reshape(-1, 2, count // 2, width_mout // 2)
+    grad_aout = grad_aout.transpose(0, 2, 1, 3).reshape(-1, width_mout)
+    d_cum = d_cols[:, :heads]
+    d_step = d_cols[:, heads : 2 * heads]
+    d_decay = lax.dot_general(
+        lower, d_cum, (((0,), (0,)), ((), ())), precision=lax.Precision.HIGHEST
+    )
+    d_alog = jnp.sum(d_decay * rate * steps, axis=0)
+    d_dtr = (d_step + d_decay * rate) * sigmoid(dtr + bias_full)
+    d_bias = jnp.sum(d_dtr, axis=0)
+    d_bcs = jnp.concatenate([d_bs, d_cs], axis=1).astype(low).astype(jnp.float32)
+    d_bc, d_convbc = pull_bc(d_bcs)
+    d_rest = jnp.stack(
+        [
+            jnp.concatenate(
+                [
+                    d_bc[:, p * state : (p + 1) * state].astype(low),
+                    d_dtr[:, p * heads_part : (p + 1) * heads_part].astype(low),
+                    jnp.zeros((length, pad), low),
+                ],
+                axis=1,
+            )
+            for p in range(parts)
+        ]
+    )
+    d_fed = lax.dynamic_update_slice(d_fed, d_rest, (0, 0, inner_width))
+    u1_t = u1.T
+    width_fed = d_fed.shape[2]
+    part_mix = part_product(
+        u1_t, d_fed, low, place=inner_width, room=inner_width + width_fed
+    )
+    part_mix = part_product(u1_t, d_z, low, into=part_mix)
+    grad_mix = ring_gather(ring_scatter(part_mix.reshape(-1, inner_width + width_fed)))
+    first_dt = 2 * inner_width + state
+    grad_ffn = ring_gather(sum_ffn)
+    back_u1 = part_back(
+        d_z, w_z, deps=[part_mix, stage_qkv, stage_mout, stage_aout]
+    )
+    back_u1 = part_back(
+        d_fed, w_x, start=back_u1, deps=[last_qkv, last_mout, last_aout, grad_ffn]
+    )
+    back, d_gain1 = rms_back(resid0, norm1_gain, back_u1)
+    cot = cot + back
+
+    bits = dp_bits()
+    columns = cot.T.astype(low).reshape((2,) * bits + (shard, length))
+    columns = columns.transpose(tuple(range(bits - 1, -1, -1)) + (bits, bits + 1))
+    counted = sum_stages(sum_cores(columns.reshape(-1, length), onehot), y_first())
+    counted_all = gather_sum(counted, reversed_blocks=False)
+    grad_patch = jnp.einsum(
+        "vd,cpv->pdc",
+        table,
+        counted_all.reshape(-1, per_pos, VOCAB),
+        preferred_element_type=jnp.float32,
+    ).reshape(patch_weight.shape[0], -1)
+    grad_table = reduce_table(
+        jnp.einsum(
+            "cpv,pdc->vd",
+            counted.reshape(-1, per_pos, VOCAB),
+            rows_by_pos,
+            preferred_element_type=jnp.float32,
+        )
+    )
+
+    taps = conv_x.shape[0]
+    small = [
+        d_gain1,
+        d_gain2,
+        d_gain3,
+        d_convbc.reshape(-1),
+        d_bias,
+        d_alog,
+        sums[taps].reshape(heads, PM).sum(axis=1),
+        sums[taps + 1],
+        sums[:taps].reshape(-1),
+    ]
+    counts = [item.shape[0] for item in small]
+    packed = jnp.concatenate(small)
+    fill = (-packed.shape[0]) % 1024
+    packed = spread_all(jnp.pad(packed, (0, fill)).reshape(-1, 1024)).reshape(-1)
+    split = []
+    begin = 0
+    for count in counts:
+        split.append(packed[begin : begin + count])
+        begin += count
+    d_gain1, d_gain2, d_gain3, d_convbc, d_bias, d_alog, d_skipped, d_ggain, d_convx = split
+
+    def own_half(vector):
+        count = vector.shape[-1] // parts
+        return lax.dynamic_slice_in_dim(vector, part * count, count, vector.ndim - 1)
+
+    model_width = grad_mix.shape[0]
+    wide = jnp.float32
+    half_bc = grad_mix[:, 2 * inner_width : 2 * inner_width + state]
+    grad_bc = jnp.concatenate(list(both_parts(half_bc)), axis=1).astype(wide)
+    grad_out = grad_ffn[:, width_in:].reshape(lax.axis_size("dp"), shard, 2, model_width)
+    grad_out = grad_out.transpose(0, 2, 1, 3).reshape(-1, model_width)
+    return (
+        mixed,
+        grad_table,
+        grad_patch,
+        d_gain1,
+        unfold(grad_mix[:, : 2 * inner_width], 2, inner_width),
+        grad_mix[:, first_dt : first_dt + heads_part].astype(wide),
+        grad_bc,
+        own_half(d_convx.reshape(taps, -1)),
+        d_convbc.reshape(conv_bc.shape),
+        own_half(d_bias),
+        own_half(d_alog),
+        own_half(d_skipped),
+        own_half(d_ggain),
+        grad_mout.astype(wide),
+        d_gain2,
+        unfold(grad_qkv, attn_qkv.shape[1], attn_qkv.shape[2]),
+        grad_aout.astype(wide),
+        d_gain3,
+        unfold(grad_ffn[:, :width_in], ffn_in.shape[1], half),
+        grad_out.astype(wide),
+    )
 
 
 def product(left, right):
@@ -394,8 +1738,10 @@
 
 
 def solution(mesh):
+    sizes = dict(mesh.shape)
+    by_rows = sizes["mp"] == MB and sizes["dp"] == 16
     return jax.shard_map(
-        on_device,
+        on_device_rows if by_rows else on_device,
         mesh=mesh,
         in_specs=(
             P(None, ("dp", "mp"), None),

time: 3580 us -> 1280 us (0.36)
  waiting for transfers between devices: 1940 us -> 332 us
  matrix products: 824 us -> 35.6 us
  Pallas kernels: 0 us -> 484 us
  other arithmetic: 378 us -> 118 us
  blocking collectives: 198 us -> 0 us
  starting transfers between devices: 2.67 us -> 101 us
    psum x3 -> x0, waiting for transfers between devices: 1000 us -> none  [the longest x2 1000 us: on_device(): lax.psum((acc_patch, grad_mix, grad_dt, acc_mout, acc_convx, acc_bias, ac...]
    dot_general x72 -> x10, matrix products: 824 us -> 35.3 us  [the longest x4 16.4 us: outer_parts(): lax.dot_general(left, right, (((1,), (0,)), ((), ())), preferred_element_...]
    reduce_scatter x14 -> x2, waiting for transfers between devices: 506 us -> 0.02 us  [ring_scatter(): lax.psum_scatter(value, ('dp', 'mp'), scatter_dimension=0, tiled=True, ax...]
    pallas_call x0 -> x29, Pallas kernels: none -> 484 us  [the longest x12 124 us: part_product(): pl.pallas_call(body, grid=(parts, count), in_specs=in_specs, out_specs=pl...]
    all_gather x21 -> x6, waiting for transfers between devices: 430 us -> 8.68 us  [the longest x2 8.67 us: gather_weight(): lax.all_gather(shard, ('mp', 'dp'), axis=0, tiled=True)]
    ppermute x0 -> x61, waiting for transfers between devices: none -> 322 us  [the longest x17 163 us: swap(): return lax.ppermute(value, 'mp', [(0, 1), (1, 0)])]
    reduce_sum x15 -> x7, other arithmetic: 178 us -> 22.7 us  [the longest x3 11.5 us: rms_back(): d_gain = jnp.sum(hidden * inv * grad, axis=0)]
    psum x4 -> x0, blocking collectives: 111 us -> none  [the longest x1 62.4 us: on_device(): lax.psum((acc_patch, grad_mix, grad_dt, acc_mout, acc_convx, acc_bias, ac...]
  transfers between devices with their start and end apart: 38 -> 69, of which waited for: 27 -> 38; matrix products, arithmetic and copies ran while one was open for 26% -> 23% of each run, Pallas kernels for 0% -> 32%
where the time goes in v1:
time: 1280 us; the launch traced here: 1260 us
  Pallas kernels  484 us (38%)
  waiting for transfers between devices  332 us (26%)
  local copies, waits for them, and re-layouts  173 us (14%)
  other arithmetic  118 us (9%)
  starting transfers between devices  101 us (8%)
  matrix products  35.6 us (3%)
  between operations  19.8 us (2%)
    ppermute x17, waiting for transfers between devices, swap(): return lax.ppermute(value, 'mp', [(0, 1), (1, 0)])  163 us
    ppermute x44, waiting for transfers between devices, swap(): lax.ppermute(value, 'dp', [(i, i ^ 1 << stage) for i in range(count)])  159 us
    pallas_call x12, Pallas kernels, part_product(): pl.pallas_call(body, grid=(parts, count), in_specs=in_specs, out_specs=pl...  124 us
    pallas_call x7, Pallas kernels, part_back(): pl.pallas_call(body, grid=(parts, count), in_specs=in_specs, out_specs=pl...  111 us
    ppermute x44, starting transfers between devices, swap(): lax.ppermute(value, 'dp', [(i, i ^ 1 << stage) for i in range(count)])  81.6 us
    unnamed x289, local copies, waits for them, and re-layouts  62.2 us
    pallas_call x1, Pallas kernels, mix_backward(): pl.pallas_call(mix_bwd_kernel, grid=(groups,), in_specs=[pl.BlockSpec(blo...  60.2 us
    pallas_call x1, Pallas kernels, attn_backward(): pl.pallas_call(attn_bwd_kernel, grid=(groups,), in_specs=[pl.BlockSpec(bl...  38.6 us
  transfers between devices with their start and end apart: 69, of which 38 were waited for; matrix products, arithmetic and copies ran while one was open for 23% of the time, Pallas kernels for 32%

profile of v1, /device:TPU:0, one launch (start us, length us, event | category | flops | bytes accessed | tf_op | source)
XLA Modules:
  0.0 1263.1 jit_solution(5355089235862907129)
XLA Ops:
  83.5 22.1 %collective-permute-done.8 = bf16[2,2,2,1,1,64,1024]{6,5,4,3,2,1,0:T(8,128)(2,1)S(1)} collective-permute-done((bf16[2,2,2,1,1,64,1024]{6,5,4,3,2,1,0:T(8,128)(2,1)S(1)}, bf16[2,2,2,1,1,64,1024]{6,5,4,3,2,1,0:T(8,128)(2,1)S(1)}, u32[]{:S(2)}, u32[]{:S(2)}) %collective-permute-start.8) | collective-permute-done | bytes 1048608 | tf_op jit(solution)/shard_map/ppermute | solution.py:803
  107.0 23.0 %collective-permute-done.18 = bf16[2,2,2,1,1,64,1280]{6,5,4,3,2,1,0:T(8,128)(2,1)S(1)} collective-permute-done((bf16[2,2,2,1,1,64,1280]{6,5,4,3,2,1,0:T(8,128)(2,1)S(1)}, bf16[2,2,2,1,1,64,1280]{6,5,4,3,2,1,0:T(8,128)(2,1)S(1)}, u32[]{:S(2)}, u32[]{:S(2)}) %collective-permute-start.18) | collective-permute-done | bytes 1310752 | tf_op jit(solution)/shard_map/ppermute | solution.py:803
  190.2 13.1 %part_product.13.x_ref = f32[2,1024,1280]{2,1,0:T(8,128)} custom-call(bf16[1024,1024]{1,0:T(8,128)(2,1)} %multiply_convert_fusion.3.left_ref, bf16[2,1024,1280]{2,1,0:T(8,128)(2,1)} %bitcast.280), custom_call_target="tpu_custom_call" | custom-call | flops 5368709120 | bytes 15728640 | tf_op jit(solution)/shard_map/part_product/pallas_call | solution.py:592
  218.0 37.5 %mix_fwd.1 = (f32[2,1024,1024]{2,1,0:T(8,128)}, bf16[4,128,2048]{2,1,0:T(8,128)(2,1)}, f32[1024,128]{1,0:T(8,128)}) custom-call(f32[2,1024,1024]{2,1,0:T(8,128)} %part_product.12.z_ref, f32[2,1024,1280]{2,1,0:T(8,128)} %part_product.13.x_ref, f32[1024,128]{1,0:T(8,128)} %pad_maximum_fusion.17.cols_ref, f32[8,4,1024]{2,1,0:T(4,128)} %reshape.399.cumt_ref, ...), custom_call_target="tpu_custom_call" | custom-call | flops 20000000000 | bytes 30000000 | tf_op jit(solution)/shard_map/mix_fwd/pallas_call | solution.py:322
  272.0 57.8 %collective-permute-done.24 = f32[512,1024]{1,0:T(8,128)S(1)} collective-permute-done((f32[512,1024]{1,0:T(8,128)}, f32[512,1024]{1,0:T(8,128)S(1)}, u32[]{:S(2)}, u32[]{:S(2)}) %collective-permute-start.24) | collective-permute-done | bytes 2097184 | tf_op jit(solution)/shard_map/ppermute | solution.py:801
  333.9 12.1 part_back.7.others_0_
  351.3 11.3 part_product.14.q_ref.k_ref.v_ref
  362.6 25.3 %attn_fwd.1 = (bf16[2,1024,512]{2,1,0:T(8,128)(2,1)}, f32[4,1024,128]{2,1,0:T(8,128)}) custom-call(bf16[2,1024,1536]{2,1,0:T(8,128)(2,1)} %part_product.14.q_ref.k_ref.v_ref, bf16[2,1024,1536]{2,1,0:T(8,128)(2,1)} %part_product.14.q_ref.k_ref.v_ref, bf16[2,1024,1536]{2,1,0:T(8,128)(2,1)} %part_product.14.q_ref.k_ref.v_ref, f32[1024,128]{1,0:T(8,128)} %broadcast_in_dim.37.pos_ref), custom_call_target="tpu_custom_call" | custom-call | flops 30000001024 | bytes 10000000 | tf_op jit(solution)/shard_map/attn_fwd/pallas_call | solution.py:100
  416.1 23.2 %ffn_in.1 = (bf16[2,1024,2048]{2,1,0:T(8,128)(2,1)}, bf16[2,1024,2048]{2,1,0:T(8,128)(2,1)}, bf16[2,1024,2048]{2,1,0:T(8,128)(2,1)}) custom-call(bf16[1024,1024]{1,0:T(8,128)(2,1)} %multiply_convert_fusion.1.left_ref, bf16[2,1024,6144]{2,1,0:T(8,128)(2,1)} %bitcast.269, bf16[2,1024,6144]{2,1,0:T(8,128)(2,1)} %bitcast.270), custom_call_target="tpu_custom_call" | custom-call | flops 17179869184 | bytes 41943040 | tf_op jit(solution)/shard_map/ffn_in/pallas_call | solution.py:738
  439.3 14.4 %outer_into.1.others_0_ = bf16[2,1024,6144]{2,1,0:T(8,128)(2,1)} custom-call(bf16[2,1024,2048]{2,1,0:T(8,128)(2,1)} %get-tuple-element.37.left_ref, bf16[1024,1024]{1,0:T(8,128)(2,1)} %fusion.4.left_ref.right_ref), custom_call_target="tpu_custom_call" | custom-call | flops 8589934592 | bytes 16777216 | tf_op jit(solution)/shard_map/outer_into/pallas_call | solution.py:680
  453.7 22.5 %ffn_back.1 = bf16[2,2,1024,2048]{3,2,1,0:T(8,128)(2,1)} custom-call(bf16[1024,1024]{1,0:T(8,128)(2,1)} %fusion.4.left_ref.right_ref, bf16[2,1024,6144]{2,1,0:T(8,128)(2,1)} %bitcast.271, bf16[2,1024,2048]{2,1,0:T(8,128)(2,1)} %get-tuple-element.38.gate_ref, bf16[2,1024,2048]{2,1,0:T(8,128)(2,1)} %get-tuple-element.39.up_ref), custom_call_target="tpu_custom_call" | custom-call | flops 8589934592 | bytes 41943040 | tf_op jit(solution)/shard_map/ffn_back/pallas_call | solution.py:774
  476.2 25.9 %part_product.15.others_0_ = bf16[2,1024,6144]{2,1,0:T(8,128)(2,1)} custom-call(bf16[1024,1024]{1,0:T(8,128)(2,1)} %copy.221.left_ref, bf16[4,1024,2048]{2,1,0:T(8,128)(2,1)} %bitcast.274, bf16[2,1024,6144]{2,1,0:T(8,128)(2,1)} %outer_into.1.others_0_), custom_call_target="tpu_custom_call", output_to_operand_aliasing={{}: (2, {})} | custom-call | flops 17179869184 | bytes 50331648 | tf_op jit(solution)/shard_map/part_product/pallas_call | solution.py:592
  510.9 31.0 %part_back.10 = f32[1024,1024]{1,0:T(8,128)} custom-call(bf16[4,1024,2048]{2,1,0:T(8,128)(2,1)} %bitcast.275, bf16[2,1024,6144]{2,1,0:T(8,128)(2,1)} %bitcast.272, bf16[2,1024,6144]{2,1,0:T(8,128)(2,1)} %part_product.15.others_0_), custom_call_target="tpu_custom_call" | custom-call | flops 17179869184 | bytes 37748736 | tf_op jit(solution)/shard_map/part_back/pallas_call | solution.py:645
  556.9 38.6 %attn_bwd.1.right_ref.left_ref = bf16[2,1024,1536]{2,1,0:T(8,128)(2,1)} custom-call(bf16[2,1024,1536]{2,1,0:T(8,128)(2,1)} %part_product.14.q_ref.k_ref.v_ref, bf16[2,1024,1536]{2,1,0:T(8,128)(2,1)} %part_product.14.q_ref.k_ref.v_ref, bf16[2,1024,1536]{2,1,0:T(8,128)(2,1)} %part_product.14.q_ref.k_ref.v_ref, ...), custom_call_target="tpu_custom_call" | custom-call | flops 70000001024 | bytes 20000000 | tf_op jit(solution)/shard_map/attn_bwd/pallas_call | solution.py:196
  624.8 13.9 %part_back.11 = f32[1024,1024]{1,0:T(8,128)} custom-call(bf16[2,1024,1536]{2,1,0:T(8,128)(2,1)} %attn_bwd.1.right_ref.left_ref, bf16[2,1024,3072]{2,1,0:T(8,128)(2,1)} %bitcast.267, bf16[2,512,1536]{2,1,0:T(8,128)(2,1)} %part_product.18.others_0_), custom_call_target="tpu_custom_call" | custom-call | flops 6442450944 | bytes 16777216 | tf_op jit(solution)/shard_map/part_back/pallas_call | solution.py:645
  653.7 13.0 %collective-permute-done.30 = bf16[2,128,1024]{2,1,0:T(8,128)(2,1)} collective-permute-done((bf16[2,128,1024]{2,1,0:T(8,128)(2,1)}, bf16[2,128,1024]{2,1,0:T(8,128)(2,1)}, u32[]{:S(2)}, u32[]{:S(2)}) %collective-permute-start.30) | collective-permute-done | bytes 524320 | tf_op jit(solution)/shard_map/ppermute | solution.py:803
  694.3 16.0 %collective-permute-done.28 = bf16[512,1536]{1,0:T(8,128)(2,1)} collective-permute-done((bf16[512,1536]{1,0:T(8,128)(2,1)}, bf16[512,1536]{1,0:T(8,128)(2,1)}, u32[]{:S(2)}, u32[]{:S(2)}) %collective-permute-start.28) | collective-permute-done | bytes 1572896 | tf_op jit(solution)/shard_map/ppermute | solution.py:801
  735.4 11.2 collective-permute-done.55
  768.0 9.1 part_product.19.dgn_ref
  777.1 10.0 multiply_reduce_fusion
  789.2 60.2 %mix_bwd.1 = (bf16[2,1024,1024]{2,1,0:T(8,128)(2,1)}, bf16[2,1024,1280]{2,1,0:T(8,128)(2,1)}, f32[1024,128]{1,0:T(8,128)}, f32[8,2048]{1,0:T(8,128)}, f32[1024,128]{1,0:T(8,128)}, /*index=5*/f32[1024,128]{1,0:T(8,128)}) custom-call(f32[2,1024,1024]{2,1,0:T(8,128)} %part_product.12.z_ref, f32[2,1024,1280]{2,1,0:T(8,128)} %part_product.13.x_ref, ...), custom_call_target="tpu_custom_call" | custom-call | flops 49999998976 | bytes 50000000 | tf_op jit(solution)/shard_map/mix_bwd/pallas_call | solution.py:495
  859.9 12.1 part_product.20.others_0_
  880.5 18.6 %part_back.9 = f32[1024,1024]{1,0:T(8,128)} custom-call(bf16[2,1024,2048]{2,1,0:T(8,128)(2,1)} %get-tuple-element.37.left_ref, bf16[2,1024,6144]{2,1,0:T(8,128)(2,1)} %bitcast.273, f32[1024,1024]{1,0:T(8,128)} %part_back.8.others_0_), custom_call_target="tpu_custom_call" | custom-call | flops 8589934592 | bytes 20971520 | tf_op jit(solution)/shard_map/part_back/pallas_call | solution.py:645
  903.7 43.6 %collective-permute-done.23 = f32[512,1024]{1,0:T(8,128)S(1)} collective-permute-done((f32[512,1024]{1,0:T(8,128)}, f32[512,1024]{1,0:T(8,128)S(1)}, u32[]{:S(2)}, u32[]{:S(2)}) %collective-permute-start.23) | collective-permute-done | bytes 2097184 | tf_op jit(solution)/shard_map/ppermute | solution.py:801
  959.0 10.1 part_back.12.others_0_
  969.1 16.6 %part_back.13 = f32[1024,1024]{1,0:T(8,128)} custom-call(bf16[2,1024,1280]{2,1,0:T(8,128)(2,1)} %maximum_dynamic-update-slice_fusion.right_ref.left_ref, bf16[2,1024,1280]{2,1,0:T(8,128)(2,1)} %bitcast.281, f32[1024,1024]{1,0:T(8,128)} %part_back.12.others_0_, bf16[256,1536]{1,0:T(8,128)(2,1)} %copy-done.41, bf16[256,1024]{1,0:T(8,128)(2,1)} %copy-done.42, ...), custom_call_target="tpu_custom_call" | custom-call | flops 5368709120 | bytes 14680064 | tf_op jit(solution)/shard_map/part_back/pallas_call | solution.py:645
  1024.8 20.4 %collective-permute-done.35 = bf16[2,256,1024]{2,1,0:T(8,128)(2,1)} collective-permute-done((bf16[2,256,1024]{2,1,0:T(8,128)(2,1)S(1)}, bf16[2,256,1024]{2,1,0:T(8,128)(2,1)}, u32[]{:S(2)}, u32[]{:S(2)}) %collective-permute-start.35) | collective-permute-done | bytes 1048608 | tf_op jit(solution)/shard_map/ppermute | solution.py:803
  1050.3 10.2 collective-permute-done.36
  1071.2 31.3 %collective-permute-start.38 = (bf16[64,1024]{1,0:T(8,128)(2,1)S(1)}, bf16[64,1024]{1,0:T(8,128)(2,1)S(1)}, u32[]{:S(2)}, u32[]{:S(2)}) collective-permute-start(bf16[64,1024]{1,0:T(8,128)(2,1)S(1)} %constant_dynamic-slice_fusion.12), channel_id=1, source_target_pairs={{0,16},{2,18},{4,20},{6,22},{8,24},{10,26},{12,28},{14,30},{16,0},... | collective-permute-start | bytes 393224 | tf_op jit(solution)/shard_map/ppermute | solution.py:803
  1178.8 11.4 unfold.5
  1190.2 11.7 reshape.430
  1201.9 9.4 copy.255
  (703 shorter events, 556.4 us)
Async XLA Ops:
  7.2 326.7 %all-gather.9.cloned.1.call-start = ((), (), s32[]{:S(2)}) async-start(), calls=%async_computation.2 | async-start | bytes 12976128 | tf_op jit(solution)/shard_map/all_gather | solution.py:963
  20.7 34.1 %collective-permute-start.11 = (bf16[1,2,1,1,1,64,1024]{6,5,4,3,2,1,0:T(8,128)(2,1)S(1)}, bf16[1,2,1,1,1,64,1024]{6,5,4,3,2,1,0:T(8,128)(2,1)S(1)}, u32[]{:S(2)}, u32[]{:S(2)}) collective-permute-start(bf16[1,2,1,1,1,64,1024]{6,5,4,3,2,1,0:T(8,128)(2,1)S(1)} %pad_maximum_fusion.22), channel_id=1, source_target_pairs={{0,8},{2,10},{4,12},{6,14},{8,0},{10,2},{12,4},{14,6},{16,24},{18,... | collective-permute-start | bytes 786440 | tf_op jit(solution)/shard_map/ppermute | solution.py:803
  24.6 17.5 %collective-permute-start.4 = (bf16[8,16,1024]{2,1,0:T(8,128)(2,1)S(1)}, bf16[8,16,1024]{2,1,0:T(8,128)(2,1)S(1)}, u32[]{:S(2)}, u32[]{:S(2)}) collective-permute-start(bf16[8,16,1024]{2,1,0:T(8,128)(2,1)S(1)} %pad_maximum_fusion.20), channel_id=1, source_target_pairs={{0,16},{2,18},{4,20},{6,22},{8,24},{10,26},{12,28},{14,30},{16,0},... | collective-permute-start | bytes 786440 | tf_op jit(solution)/shard_map/ppermute | solution.py:803
  53.2 17.7 %collective-permute-start.17 = (bf16[1,2,2,1,1,64,1280]{6,5,4,3,2,1,0:T(8,128)(2,1)S(1)}, bf16[1,2,2,1,1,64,1280]{6,5,4,3,2,1,0:T(8,128)(2,1)S(1)}, u32[]{:S(2)}, u32[]{:S(2)}) collective-permute-start(bf16[1,2,2,1,1,64,1280]{6,5,4,3,2,1,0:T(8,128)(2,1)S(1)} %pad_maximum_fusion.13), channel_id=1, source_target_pairs={{0,1},{1,0},{2,3},{3,2},{4,5},{5,4},{6,7},{7,6},{8,9},{9,8},{10,11... | collective-permute-start | bytes 1966088 | tf_op jit(solution)/shard_map/ppermute | solution.py:801
  59.8 19.5 %collective-permute-start.7 = (bf16[1,2,2,1,1,64,1024]{6,5,4,3,2,1,0:T(8,128)(2,1)S(1)}, bf16[1,2,2,1,1,64,1024]{6,5,4,3,2,1,0:T(8,128)(2,1)S(1)}, u32[]{:S(2)}, u32[]{:S(2)}) collective-permute-start(bf16[1,2,2,1,1,64,1024]{6,5,4,3,2,1,0:T(8,128)(2,1)S(1)} %pad_maximum_fusion.15), channel_id=1, source_target_pairs={{0,1},{1,0},{2,3},{3,2},{4,5},{5,4},{6,7},{7,6},{8,9},{9,8},{10,11... | collective-permute-start | bytes 1572872 | tf_op jit(solution)/shard_map/ppermute | solution.py:801
  61.5 18.1 %collective-permute-start.12 = (bf16[1,2,2,1,1,64,1024]{6,5,4,3,2,1,0:T(8,128)(2,1)S(1)}, bf16[1,2,2,1,1,64,1024]{6,5,4,3,2,1,0:T(8,128)(2,1)S(1)}, u32[]{:S(2)}, u32[]{:S(2)}) collective-permute-start(bf16[1,2,2,1,1,64,1024]{6,5,4,3,2,1,0:T(8,128)(2,1)S(1)} %pad_maximum_fusion.16), channel_id=1, source_target_pairs={{0,4},{2,6},{4,0},{6,2},{8,12},{10,14},{12,8},{14,10},{16,20},{18,... | collective-permute-start | bytes 1572872 | tf_op jit(solution)/shard_map/ppermute | solution.py:803
  79.5 26.2 %collective-permute-start.8 = (bf16[2,2,2,1,1,64,1024]{6,5,4,3,2,1,0:T(8,128)(2,1)S(1)}, bf16[2,2,2,1,1,64,1024]{6,5,4,3,2,1,0:T(8,128)(2,1)S(1)}, u32[]{:S(2)}, u32[]{:S(2)}) collective-permute-start(bf16[2,2,2,1,1,64,1024]{6,5,4,3,2,1,0:T(8,128)(2,1)S(1)} %pad_maximum_fusion.10), channel_id=1, source_target_pairs={{0,4},{2,6},{4,0},{6,2},{8,12},{10,14},{12,8},{14,10},{16,20},{18,... | collective-permute-start | bytes 3145736 | tf_op jit(solution)/shard_map/ppermute | solution.py:803
  79.8 26.3 %collective-permute-start.13 = (bf16[1,2,2,2,1,64,1024]{6,5,4,3,2,1,0:T(8,128)(2,1)S(1)}, bf16[1,2,2,2,1,64,1024]{6,5,4,3,2,1,0:T(8,128)(2,1)S(1)}, u32[]{:S(2)}, u32[]{:S(2)}) collective-permute-start(bf16[1,2,2,2,1,64,1024]{6,5,4,3,2,1,0:T(8,128)(2,1)S(1)} %pad_maximum_fusion.11), channel_id=1, source_target_pairs={{0,1},{1,0},{2,3},{3,2},{4,5},{5,4},{6,7},{7,6},{8,9},{9,8},{10,11... | collective-permute-start | bytes 3145736 | tf_op jit(solution)/shard_map/ppermute | solution.py:801
  81.5 48.5 %collective-permute-start.18 = (bf16[2,2,2,1,1,64,1280]{6,5,4,3,2,1,0:T(8,128)(2,1)S(1)}, bf16[2,2,2,1,1,64,1280]{6,5,4,3,2,1,0:T(8,128)(2,1)S(1)}, u32[]{:S(2)}, u32[]{:S(2)}) collective-permute-start(bf16[2,2,2,1,1,64,1280]{6,5,4,3,2,1,0:T(8,128)(2,1)S(1)} %pad_maximum_fusion.9), channel_id=1, source_target_pairs={{0,4},{2,6},{4,0},{6,2},{8,12},{10,14},{12,8},{14,10},{16,20},{18,... | collective-permute-start | bytes 3932168 | tf_op jit(solution)/shard_map/ppermute | solution.py:803
  106.0 27.2 %collective-permute-start.9 = (bf16[2,2,2,2,1,64,1024]{6,5,4,3,2,1,0:T(8,128)(2,1)S(1)}, bf16[2,2,2,2,1,64,1024]{6,5,4,3,2,1,0:T(8,128)(2,1)S(1)}, u32[]{:S(2)}, u32[]{:S(2)}) collective-permute-start(bf16[2,2,2,2,1,64,1024]{6,5,4,3,2,1,0:T(8,128)(2,1)S(1)} %pad_maximum_fusion.6), channel_id=1, source_target_pairs={{0,2},{2,0},{4,6},{6,4},{8,10},{10,8},{12,14},{14,12},{16,18},{18,... | collective-permute-start | bytes 6291464 | tf_op jit(solution)/shard_map/ppermute | solution.py:803
  106.5 24.1 %collective-permute-start.14 = (bf16[2,2,2,2,1,64,1024]{6,5,4,3,2,1,0:T(8,128)(2,1)S(1)}, bf16[2,2,2,2,1,64,1024]{6,5,4,3,2,1,0:T(8,128)(2,1)S(1)}, u32[]{:S(2)}, u32[]{:S(2)}) collective-permute-start(bf16[2,2,2,2,1,64,1024]{6,5,4,3,2,1,0:T(8,128)(2,1)S(1)} %pad_maximum_fusion.7), channel_id=1, source_target_pairs={{0,2},{2,0},{4,6},{6,4},{8,10},{10,8},{12,14},{14,12},{16,18},{18,... | collective-permute-start | bytes 6291464 | tf_op jit(solution)/shard_map/ppermute | solution.py:803
  141.9 274.1 %all-gather.11.cloned.1.call-start = ((), (), s32[]{:S(2)}) async-start(), calls=%async_computation.3 | async-start | bytes 25952256 | tf_op jit(solution)/shard_map/all_gather | solution.py:963
  143.2 616.9 %reduce-scatter.3.cloned.1.call-start = ((), (), s32[]{:S(2)}) async-start(), calls=%async_computation.4 | async-start | bytes 25952256 | tf_op jit(solution)/shard_map/reduce_scatter | solution.py:898
  147.0 18.4 %collective-permute-start.22 = (f32[4,1024]{1,0:T(4,128)S(1)}, f32[4,1024]{1,0:T(4,128)S(1)}, u32[]{:S(2)}, u32[]{:S(2)}) collective-permute-start(f32[4,1024]{1,0:T(4,128)S(1)} %copy-done.103), channel_id=1, source_target_pairs={{0,1},{1,0},{2,3},{3,2},{4,5},{5,4},{6,7},{7,6},{8,9},{9,8},{10,11... | collective-permute-start | bytes 49160 | tf_op jit(solution)/shard_map/ppermute | solution.py:801
  261.3 68.5 %collective-permute-start.24 = (f32[512,1024]{1,0:T(8,128)}, f32[512,1024]{1,0:T(8,128)S(1)}, u32[]{:S(2)}, u32[]{:S(2)}) collective-permute-start(f32[512,1024]{1,0:T(8,128)} %dynamic-slice_bitcast_fusion), channel_id=1, source_target_pairs={{0,1},{1,0},{2,3},{3,2},{4,5},{5,4},{6,7},{7,6},{8,9},{9,8},{10,11... | collective-permute-start | bytes 6291464 | tf_op jit(solution)/shard_map/ppermute | solution.py:801
  502.2 449.8 %all-gather.19.cloned.1.call-start = ((), (), s32[]{:S(2)}) async-start(), calls=%async_computation.9 | async-start | bytes 6684672 | tf_op jit(solution)/shard_map/all_gather | solution.py:877
  651.2 35.2 %collective-permute-start.26 = (bf16[2,512,1024]{2,1,0:T(8,128)(2,1)}, bf16[2,512,1024]{2,1,0:T(8,128)(2,1)}, u32[]{:S(2)}, u32[]{:S(2)}) collective-permute-start(bf16[2,512,1024]{2,1,0:T(8,128)(2,1)} %fusion.20), channel_id=1, source_target_pairs={{0,2},{2,0},{4,6},{6,4},{8,10},{10,8},{12,14},{14,12},{16,18},{18,... | collective-permute-start | bytes 6291464 | tf_op jit(solution)/shard_map/ppermute | solution.py:803
  671.6 38.7 %collective-permute-start.28 = (bf16[512,1536]{1,0:T(8,128)(2,1)}, bf16[512,1536]{1,0:T(8,128)(2,1)}, u32[]{:S(2)}, u32[]{:S(2)}) collective-permute-start(bf16[512,1536]{1,0:T(8,128)(2,1)} %dynamic-slice_bitcast_fusion.1), channel_id=1, source_target_pairs={{0,1},{1,0},{2,3},{3,2},{4,5},{5,4},{6,7},{7,6},{8,9},{9,8},{10,11... | collective-permute-start | bytes 4718600 | tf_op jit(solution)/shard_map/ppermute | solution.py:801
  692.8 28.4 %collective-permute-start.29 = (bf16[2,256,1024]{2,1,0:T(8,128)(2,1)}, bf16[2,256,1024]{2,1,0:T(8,128)(2,1)}, u32[]{:S(2)}, u32[]{:S(2)}) collective-permute-start(bf16[2,256,1024]{2,1,0:T(8,128)(2,1)} %constant_dynamic-slice_fusion.19), channel_id=1, source_target_pairs={{0,4},{2,6},{4,0},{6,2},{8,12},{10,14},{12,8},{14,10},{16,20},{18,... | collective-permute-start | bytes 3145736 | tf_op jit(solution)/shard_map/ppermute | solution.py:803
  713.3 18.2 %collective-permute-start.31 = (bf16[256,1536]{1,0:T(8,128)(2,1)S(1)}, bf16[256,1536]{1,0:T(8,128)(2,1)}, u32[]{:S(2)}, u32[]{:S(2)}) collective-permute-start(bf16[256,1536]{1,0:T(8,128)(2,1)S(1)} %constant_dynamic-slice_fusion.17), channel_id=1, source_target_pairs={{0,4},{2,6},{4,0},{6,2},{8,12},{10,14},{12,8},{14,10},{16,20},{18,... | collective-permute-start | bytes 2359304 | tf_op jit(solution)/shard_map/ppermute | solution.py:803
  760.1 209.1 %all-gather.13.cloned.1.call-start = ((), (), s32[]{:S(2)}) async-start(), calls=%async_computation.5 | async-start | bytes 13369344 | tf_op jit(solution)/shard_map/all_gather | solution.py:908
  760.7 262.2 %reduce-scatter.5.cloned.1.call-start = ((), (), s32[]{:S(2)}) async-start(), calls=%async_computation.6 | async-start | bytes 9732096 | tf_op jit(solution)/shard_map/reduce_scatter | solution.py:898
  880.4 341.1 %all-gather.15.cloned.1.call-start = ((), (), s32[]{:S(2)}) async-start(), calls=%async_computation.7 | async-start | bytes 5013504 | tf_op jit(solution)/shard_map/all_gather | solution.py:908
  902.3 45.1 %collective-permute-start.23 = (f32[512,1024]{1,0:T(8,128)}, f32[512,1024]{1,0:T(8,128)S(1)}, u32[]{:S(2)}, u32[]{:S(2)}) collective-permute-start(f32[512,1024]{1,0:T(8,128)} %constant_dynamic-slice_fusion.20), channel_id=1, source_target_pairs={{0,1},{1,0},{2,3},{3,2},{4,5},{5,4},{6,7},{7,6},{8,9},{9,8},{10,11... | collective-permute-start | bytes 6291464 | tf_op jit(solution)/shard_map/ppermute | solution.py:801
  1019.4 25.7 %collective-permute-start.35 = (bf16[2,256,1024]{2,1,0:T(8,128)(2,1)S(1)}, bf16[2,256,1024]{2,1,0:T(8,128)(2,1)}, u32[]{:S(2)}, u32[]{:S(2)}) collective-permute-start(bf16[2,256,1024]{2,1,0:T(8,128)(2,1)S(1)} %constant_dynamic-slice_fusion.14), channel_id=1, source_target_pairs={{0,4},{2,6},{4,0},{6,2},{8,12},{10,14},{12,8},{14,10},{16,20},{18,... | collective-permute-start | bytes 3145736 | tf_op jit(solution)/shard_map/ppermute | solution.py:803
  1023.0 222.0 %all-gather.17.cloned.1.call-start = ((), (), s32[]{:S(2)}) async-start(), calls=%async_computation.8 | async-start | bytes 2228224 | tf_op jit(solution)/shard_map/all_gather | solution.py:877
  1071.2 36.8 %collective-permute-start.38 = (bf16[64,1024]{1,0:T(8,128)(2,1)S(1)}, bf16[64,1024]{1,0:T(8,128)(2,1)S(1)}, u32[]{:S(2)}, u32[]{:S(2)}) collective-permute-start(bf16[64,1024]{1,0:T(8,128)(2,1)S(1)} %constant_dynamic-slice_fusion.12), channel_id=1, source_target_pairs={{0,16},{2,18},{4,20},{6,22},{8,24},{10,26},{12,28},{14,30},{16,0},... | collective-permute-start | bytes 393224 | tf_op jit(solution)/shard_map/ppermute | solution.py:803
  1135.7 25.6 %collective-permute-start.52 = (f32[15,1024]{1,0:T(8,128)S(1)}, f32[15,1024]{1,0:T(8,128)S(1)}, u32[]{:S(2)}, u32[]{:S(2)}) collective-permute-start(f32[15,1024]{1,0:T(8,128)S(1)} %add.482), channel_id=1, source_target_pairs={{0,8},{2,10},{4,12},{6,14},{8,0},{10,2},{12,4},{14,6},{16,24},{18,... | collective-permute-start | bytes 184328 | tf_op jit(solution)/shard_map/ppermute | solution.py:803
  1137.7 26.4 %collective-permute-start.44 = (f32[8,1024]{1,0:T(8,128)S(1)}, f32[8,1024]{1,0:T(8,128)S(1)}, u32[]{:S(2)}, u32[]{:S(2)}) collective-permute-start(f32[8,1024]{1,0:T(8,128)S(1)} %dynamic-slice_add_fusion.4), channel_id=1, source_target_pairs={{0,16},{2,18},{4,20},{6,22},{8,24},{10,26},{12,28},{14,30},{16,0},... | collective-permute-start | bytes 98312 | tf_op jit(solution)/shard_map/ppermute | solution.py:803
  1161.3 50.0 %collective-permute-start.53 = (f32[15,1024]{1,0:T(8,128)S(1)}, f32[15,1024]{1,0:T(8,128)S(1)}, u32[]{:S(2)}, u32[]{:S(2)}) collective-permute-start(f32[15,1024]{1,0:T(8,128)S(1)} %add.483), channel_id=1, source_target_pairs={{0,16},{2,18},{4,20},{6,22},{8,24},{10,26},{12,28},{14,30},{16,0},... | collective-permute-start | bytes 184328 | tf_op jit(solution)/shard_map/ppermute | solution.py:803
  1164.1 47.4 %collective-permute-start.45 = (f32[16,1024]{1,0:T(8,128)S(1)}, f32[16,1024]{1,0:T(8,128)S(1)}, u32[]{:S(2)}, u32[]{:S(2)}) collective-permute-start(f32[16,1024]{1,0:T(8,128)S(1)} %pad_maximum_fusion.27), channel_id=1, source_target_pairs={{0,8},{2,10},{4,12},{6,14},{8,0},{10,2},{12,4},{14,6},{16,24},{18,... | collective-permute-start | bytes 196616 | tf_op jit(solution)/shard_map/ppermute | solution.py:803
  1217.1 19.0 %collective-permute-start.47 = (f32[64,1024]{1,0:T(8,128)S(1)}, f32[64,1024]{1,0:T(8,128)S(1)}, u32[]{:S(2)}, u32[]{:S(2)}) collective-permute-start(f32[64,1024]{1,0:T(8,128)S(1)} %pad_maximum_fusion.23), channel_id=1, source_target_pairs={{0,1},{1,0},{2,3},{3,2},{4,5},{5,4},{6,7},{7,6},{8,9},{9,8},{10,11... | collective-permute-start | bytes 786440 | tf_op jit(solution)/shard_map/ppermute | solution.py:801
  (159 other events, 2561.1 us)
Sparse Core Ops, SparseCore 0:
  142.1 94.6 all-gather.8
  240.2 175.7 all-gather.10
  502.3 138.7 reduce-scatter.2
  760.2 38.7 all-gather.18
  800.4 71.7 all-gather.12
  880.5 116.2 reduce-scatter.4
  1023.1 76.7 all-gather.14
  1137.8 30.7 all-gather.16

commit v2 on v1

--- a/solution.py
+++ b/solution.py
@@ -241,8 +241,8 @@
 
 
 def mix_fwd_kernel(
-    z_ref, x_ref, cols_ref, cumt_ref, conv_ref, skip_ref, pos_ref, bs_ref, cs_ref, bst_ref,
-    ssm_ref, state_ref, ssq_ref, inner_ref,
+    z_ref, x_ref, cols_ref, cumt_ref, conv_ref, skip_ref, gain_ref, pos_ref, bs_ref, cs_ref,
+    bst_ref, ssm_ref, scaled_ref, state_ref, ssq_ref, inner_ref,
 ):
     length = pos_ref.shape[0]
     width = x_ref.shape[2]
@@ -297,6 +297,7 @@
         ssm_ref[0, rows, :] = out
         gate = z_ref[0, rows, :]
         gated = out * gate * sigmoid(gate)
+        scaled_ref[0, rows, :] = (gated * gain_ref[...]).astype(jnp.bfloat16)
         square = gated * gated
         total = square[:, 0:128]
         for lane in range(128, width, 128):
@@ -311,7 +312,7 @@
             ssq_ref[rows, :] += total
 
 
-def mix_forward(z, x, cols, cumt, conv, skip, posb, bs, cs, bst):
+def mix_forward(z, x, cols, cumt, conv, skip, gain, posb, bs, cs, bst):
     parts, length, inner_width = z.shape
     state = bs.shape[1]
     lanes = 256
@@ -329,6 +330,7 @@
             pl.BlockSpec((1,) + cumt.shape[1:], lambda g: (g, 0, 0)),
             pl.BlockSpec((TAPS, lanes), lambda g: (0, g)),
             pl.BlockSpec((1, lanes), lambda g: (0, g)),
+            pl.BlockSpec((1, lanes), lambda g: (0, g)),
             pl.BlockSpec((length, 128), whole),
             pl.BlockSpec((length, state), whole),
             pl.BlockSpec((length, state), whole),
@@ -336,11 +338,13 @@
         ],
         out_specs=[
             pl.BlockSpec(block, lambda g: (g // per, 0, g % per)),
+            pl.BlockSpec(block, lambda g: (g // per, 0, g % per)),
             pl.BlockSpec((length // BLK, state, lanes), lambda g: (0, 0, g)),
             pl.BlockSpec((length, 128), whole),
         ],
         out_shape=[
             jax.ShapeDtypeStruct((parts, length, inner_width), jnp.float32),
+            jax.ShapeDtypeStruct((parts, length, inner_width), jnp.bfloat16),
             jax.ShapeDtypeStruct((length // BLK, state, parts * inner_width), jnp.bfloat16),
             jax.ShapeDtypeStruct((length, 128), jnp.float32),
         ],
@@ -350,7 +354,7 @@
             flops=20_000_000_000, bytes_accessed=30_000_000, transcendentals=0
         ),
         name="mix_fwd",
-    )(z, x, cols, cumt, conv, skip, posb, bs, cs, bst)
+    )(z, x, cols, cumt, conv, skip, gain, posb, bs, cs, bst)
 
 
 def mix_bwd_kernel(
@@ -608,7 +612,7 @@
     )(*operands, *deps)
 
 
-def part_back(left, right, first=0, start=None, deps=()):
+def part_back(left, right, first=0, start=None, scale=None, deps=()):
     parts, rows, columns = left.shape
     width = right.shape[1]
     fold = parts // right.shape[0]
@@ -627,12 +631,18 @@
     if start is not None:
         in_specs.append(pl.BlockSpec((rows, width), lambda m, n: (0, 0)))
         operands.append(start)
+    if scale is not None:
+        in_specs.append(pl.BlockSpec(scale.shape, lambda m, n: (0, 0)))
+        operands.append(scale)
     in_specs += [pl.BlockSpec(memory_space=pl.ANY)] * len(deps)
 
     def body(left_ref, right_ref, *others):
         out_ref = others[-1]
         total = dot_nt(left_ref[0], right_ref[0])
         opening = (pl.program_id(0) == 0) & (pl.program_id(1) == 0)
+
+        if scale is not None:
+            total = total * others[1][:, 0:1]
 
         @pl.when(opening)
         def _():
@@ -658,7 +668,8 @@
     )(*operands, *deps)
 
 
-def outer_kernel(left_ref, right_ref, out_ref):
+def outer_kernel(left_ref, right_ref, *others):
+    out_ref = others[-1]
     total = dot_tn(left_ref[0], right_ref[...]).astype(jnp.bfloat16)
     rows = out_ref.shape[1]
     width = right_ref.shape[1]
@@ -672,18 +683,21 @@
             ]
 
 
-def outer_into(left, right, wraps, place, room):
+def outer_into(left, right, wraps, place, room, into=None):
     parts, length, columns = left.shape
     width = right.shape[1]
     tile = 256 * wraps
     begin = place // (wraps * width)
+    before = [] if into is None else [into]
     return pl.pallas_call(
         outer_kernel,
         grid=(parts, columns // tile),
         in_specs=[
             pl.BlockSpec((1, length, tile), lambda m, n: (m, 0, n)),
             pl.BlockSpec((length, width), lambda m, n: (0, 0)),
-        ],
+        ]
+        + [pl.BlockSpec(memory_space=pl.ANY)] * len(before),
+        input_output_aliases={2: 0} if before else {},
         out_specs=pl.BlockSpec((1, tile // wraps, wraps * width), lambda m, n: (m, n, begin)),
         out_shape=jax.ShapeDtypeStruct((parts, columns // wraps, room), jnp.bfloat16),
         compiler_params=pltpu.CompilerParams(vmem_limit_bytes=VMEM_LIMIT),
@@ -693,7 +707,7 @@
             transcendentals=0,
         ),
         name="outer_into",
-    )(left, right)
+    )(left, right, *before)
 
 
 def unfold_kernel(in_ref, out_ref):
@@ -792,6 +806,110 @@
     )(left, right, gate, upper)
 
 
+def span_kernel(col_ref, row_ref, pos_ref, rem_ref):
+    length = col_ref.shape[0]
+    row = row_ref[...]
+    other = lax.broadcasted_iota(jnp.int32, (BLK, length), 1)
+    for i in range(length // BLK):
+        rows = pl.ds(i * BLK, BLK)
+        spot = i * BLK + lax.broadcasted_iota(jnp.int32, (BLK, length), 0)
+        same = col_ref[rows, 0:1] == row
+        before = jnp.where(same & (other < spot), 1.0, 0.0)
+        after = jnp.where(same & (other > spot), 1.0, 0.0)
+        before = jnp.sum(before, axis=1, keepdims=True)
+        after = jnp.sum(after, axis=1, keepdims=True)
+        pos_ref[rows, :] = jnp.broadcast_to(before, (BLK, 128))
+        rem_ref[rows, :] = jnp.broadcast_to(after, (BLK, 128))
+
+
+def spans(seg):
+    length = seg.shape[0]
+    shape = jax.ShapeDtypeStruct((length, 128), jnp.float32)
+    return pl.pallas_call(
+        span_kernel,
+        out_shape=[shape, shape],
+        compiler_params=pltpu.CompilerParams(vmem_limit_bytes=VMEM_LIMIT),
+        name="spans",
+    )(seg[:, None], seg[None, :])
+
+
+def refold_kernel(in_ref, out_ref):
+    rows, width = in_ref.shape
+    count = out_ref.shape[0] // rows
+    width = width // count
+    piece = 64
+    for i in range(rows // piece):
+        for j in range(count):
+            out_ref[pl.ds((i * count + j) * piece, piece), :] = in_ref[
+                i * piece : (i + 1) * piece, j * width : (j + 1) * width
+            ].astype(jnp.float32)
+
+
+def refold(value, first, count, width, step):
+    rows = value.shape[0]
+    begin = first // (count * width)
+    return pl.pallas_call(
+        refold_kernel,
+        grid=(rows // step,),
+        in_specs=[pl.BlockSpec((step, count * width), lambda n: (n, begin))],
+        out_specs=pl.BlockSpec((step * count, width), lambda n: (n, 0)),
+        out_shape=jax.ShapeDtypeStruct((rows * count, width), jnp.float32),
+        compiler_params=pltpu.CompilerParams(vmem_limit_bytes=VMEM_LIMIT),
+        cost_estimate=pl.CostEstimate(
+            flops=0, bytes_accessed=6 * rows * count * width, transcendentals=0
+        ),
+        name="refold",
+    )(value)
+
+
+def embed_kernel(ids_ref, mapped_ref, onehot_ref, out_ref):
+    length = ids_ref.shape[1]
+    value = lax.broadcasted_iota(jnp.int32, (length, VOCAB), 1)
+    total = None
+    for p in range(ids_ref.shape[2]):
+        span = pl.ds(p * VOCAB, VOCAB)
+        hit = jnp.where(ids_ref[0, :, p : p + 1] == value, 1.0, 0.0).astype(jnp.bfloat16)
+        onehot_ref[0, :, span] = hit
+        part = dot_nt(hit, mapped_ref[0, :, span])
+        total = part if total is None else total + part
+
+    @pl.when(pl.program_id(0) == 0)
+    def _():
+        out_ref[...] = total
+
+    @pl.when(pl.program_id(0) > 0)
+    def _():
+        out_ref[...] += total
+
+
+def embed_rows(ids, mapped):
+    parts, length, count = ids.shape
+    width = mapped.shape[1]
+    return pl.pallas_call(
+        embed_kernel,
+        grid=(parts,),
+        in_specs=[
+            pl.BlockSpec((1, length, count), lambda m: (m, 0, 0)),
+            pl.BlockSpec((1, width, count * VOCAB), lambda m: (m, 0, 0)),
+        ],
+        out_specs=[
+            pl.BlockSpec((1, length, count * VOCAB), lambda m: (m, 0, 0)),
+            pl.BlockSpec((length, width), lambda m: (0, 0)),
+        ],
+        out_shape=[
+            jax.ShapeDtypeStruct((parts, length, count * VOCAB), jnp.bfloat16),
+            jax.ShapeDtypeStruct((length, width), jnp.float32),
+        ],
+        compiler_params=pltpu.CompilerParams(vmem_limit_bytes=VMEM_LIMIT),
+        cost_estimate=pl.CostEstimate(
+            flops=2 * parts * length * width * count * VOCAB,
+            bytes_accessed=12 * length * width,
+            transcendentals=0,
+        ),
+        name="embed_rows",
+    )(ids, mapped)
+
+
 def bit_of(index, bit):
     return (index >> bit) & 1
 
@@ -846,8 +964,8 @@
     return value
 
 
-def sum_stages(total, order):
-    for stage in order:
+def sum_stages(total, order, after=()):
+    for turn, stage in enumerate(order):
         mine = my_bit(stage)
         if stage is None:
             received = swap(lax.dynamic_index_in_dim(total, 1 - mine, 0, keepdims=False), None)
@@ -859,6 +977,8 @@
                 lax.dynamic_slice_in_dim(total, (1 - mine) * half, half, axis), stage
             )
             kept = lax.dynamic_slice_in_dim(total, mine * half, half, axis)
+        if turn < len(after):
+            kept = kept.astype(jnp.float32) + after[turn]
         total = add_low(kept, received)
     return total
 
@@ -914,17 +1034,23 @@
     )
 
 
-def gather_steps(shard, order):
+def gather_steps(shard, order, peek=None, after=None):
     bits = dp_bits()
     value = shard.reshape((1,) * (bits + 1) + shard.shape)
-    for stage in order:
+    seen = None
+    for turn, stage in enumerate(order):
         axis = 0 if stage is None else bits - stage
         other = swap(value, stage)
         bit = my_bit(stage)
+        if turn == peek:
+            seen = value
+        if turn == 3 and after is not None:
+            value = value + after
         value = jnp.concatenate(
             [jnp.where(bit == 0, value, other), jnp.where(bit == 0, other, value)], axis=axis
         )
-    return value.reshape(2, -1, shard.shape[1])
+    value = value.reshape(2, -1, shard.shape[1])
+    return value if peek is None else (value, seen)
 
 
 def gather_y_last():
@@ -1059,7 +1185,7 @@
         [mamba_in[:, 1], bc_half, mamba_dt, jnp.zeros((shard, pad), low)], axis=1
     )
     shard_qkv = attn_qkv.reshape(shard, -1)
-    shard_mid = jnp.concatenate([shard_qkv, mamba_out.T, attn_out.T], axis=1)
+    shard_mid = jnp.concatenate([mamba_out.T, shard_qkv, attn_out.T], axis=1)
     shard_ffn = jnp.concatenate([ffn_in.reshape(shard, -1), ffn_out.T], axis=1)
     width_in = ffn_in.shape[1] * ffn_in.shape[2]
 
@@ -1069,26 +1195,26 @@
         rows_by_pos, table, (((1,), (1,)), ((), ())), preferred_element_type=jnp.float32
     ).astype(low)
     mapped = mapped.transpose(1, 0, 2).reshape(rows_by_pos.shape[2], -1)
-    mapped = gather_steps(mapped, gather_y_last())
-    w_z = gather_steps(shard_z, gather_x_last())
-    w_x = gather_steps(shard_x, gather_y_last())
+    table_ready = table[0, 0] * 0
+    posb, remb = spans(seg)
+    ids_parts = ids.reshape(length, parts, per_pos).transpose(1, 0, 2)
+    prepared = posb[0, 0] + ids_parts[0, 0, 0].astype(jnp.float32)
+    prepared = ((prepared + conv_full[0, 0] + ggain_full[0]) * 0).astype(low)
+    mapped, early = gather_steps(mapped, gather_y_last(), peek=3, after=prepared)
+    early = early.reshape(-1)[0] * 0
+    w_z = gather_steps(shard_z + table_ready, gather_x_last())
+    w_x = gather_steps(shard_x + table_ready, gather_y_last())
     mapped_ready = mapped[0, 0, 0] * 0
     ready = (w_z[0, 0, 0] + w_x[0, 0, 0]) * 0 + mapped_ready
-    w_mid = gather_weight(shard_mid + ready)
+    w_mid = gather_weight(shard_mid + early)
     w_ffn = gather_weight(shard_ffn + ready)
     width_qkv = shard_qkv.shape[1]
 
-    onehot = (ids[:, :, None] == jnp.arange(VOCAB, dtype=jnp.int32)[None, None, :]).astype(low)
-    onehot = onehot.reshape(length, parts, per_pos * VOCAB).transpose(1, 0, 2)
-    resid0 = dot_back(onehot, mapped)
+    onehot, resid0 = embed_rows(ids_parts, mapped)
 
     spots = jnp.arange(length, dtype=jnp.int32)
-    changed = jnp.concatenate([jnp.ones((1,), bool), seg[1:] != seg[:-1]])
-    same = seg[:, None] == seg[None, :]
-    pos = jnp.sum((same & (spots[None, :] < spots[:, None])).astype(jnp.int32), axis=1)
-    rem = jnp.sum((same & (spots[None, :] > spots[:, None])).astype(jnp.int32), axis=1)
-    posb = wide128(pos.astype(jnp.float32)[:, None])
-    remb = wide128(rem.astype(jnp.float32)[:, None])
+    pos = posb[:, 0]
+    rem = remb[:, 0]
 
     u1 = rms_apply(resid0, norm1_gain).astype(low)
     gate = part_product(u1, w_z, jnp.float32)
@@ -1114,24 +1240,23 @@
     starts = jnp.concatenate([jnp.zeros((1, heads), jnp.float32), ends[:-1]], axis=0)
     start_wide = jnp.repeat(starts, BLK, axis=0)
     end_wide = jnp.repeat(ends, BLK, axis=0)
-    carried = (pos > spots - chunk_first) & (chunk > 0)
+    carried = (pos > (spots - chunk_first).astype(jnp.float32)) & (chunk > 0)
     carry = jnp.where(carried[:, None], jnp.exp(cum - start_wide), 0.0)
-    lasting = spots + rem >= chunk_first + BLK - 1
+    lasting = rem >= (chunk_first + BLK - 1 - spots).astype(jnp.float32)
     last = jnp.where(lasting[:, None], jnp.exp(end_wide - cum), 0.0)
     cum2 = cum * LOG2E
     cols = jnp.concatenate([steps, cum2, carry, last], axis=1)
     cumt = cum2.T.reshape(groups, -1, length)
     skip_wide = jnp.repeat(skip_full, PM)[None]
-    ssm, states, squares = mix_forward(
-        gate, fed, cols, cumt, conv_full, skip_wide, posb, bs, cs, bs.T
+    ssm, scaled, states, squares = mix_forward(
+        gate, fed, cols, cumt, conv_full, skip_wide, ggain_full[None], posb, bs, cs, bs.T
     )
     factor = lax.rsqrt(jnp.sum(squares, axis=1, keepdims=True) / DIN + 1e-05)
     gain_parts = ggain_full.reshape(parts, 1, inner_width)
-    gnormed = (ssm * gate * sigmoid(gate) * factor[None] * gain_parts).astype(low)
-    resid1 = part_back(gnormed, w_mid, first=width_qkv, start=resid0)
+    resid1 = part_back(scaled, w_mid, start=resid0, scale=wide128(factor))
 
     u2 = rms_apply(resid1, norm2_gain).astype(low)
-    qkv = part_product(u2, w_mid, low, columns=width_qkv)
+    qkv = part_product(u2, w_mid, low, first=inner_width, columns=width_qkv)
     attended, logs = attn_forward(qkv, posb)
     resid2 = part_back(attended, w_mid, first=width_qkv + inner_width, start=resid1)
 
@@ -1151,24 +1276,15 @@
         count = value.shape[0] // 2
         return lax.dynamic_slice_in_dim(value, which * count, count, 0)
 
-    def half_lanes(value, which):
-        count = value.shape[2] // 2
-        return lax.dynamic_slice_in_dim(value, which * count, count, 2)
-
-    def sum_cores(left_t, right):
+    def sum_cores(left_t, right, deps=()):
         received = swap(part_product(half_rows(left_t, 1 - core), right, low), 0)
-        return part_product(half_rows(left_t, core), right, low, extra=received)
-
-    def outer_parts(left, right):
-        return lax.dot_general(
-            left, right, (((1,), (0,)), ((), ())), preferred_element_type=jnp.float32
-        )
-
-    def sum_cores_back(left, right):
-        received = swap(outer_parts(half_lanes(left, 1 - core), right).astype(low), 0)
-        return add_low(outer_parts(half_lanes(left, core), right), received)
-
-    cot = exchange(d_out + ssm[0, 0, 0] * 0)
+        return part_product(half_rows(left_t, core), right, low, extra=received, deps=deps)
+
+    started = ssm[0, 0, 0] * 0
+    ended = hidden[0, 0, 0].astype(jnp.float32) * 0
+    cot_own = lax.dynamic_index_in_dim(d_out, part, 0, keepdims=False) + ended
+    cot_other = lax.dynamic_index_in_dim(d_out, 1 - part, 0, keepdims=False) + started
+    cot = join(cot_own, swap(cot_other, None), part)
     dm3 = cot.astype(low)
     d_gate_up = ffn_backward(dm3, w_ffn, width_in, gate3, up3)
     quarter = d_gate_up.reshape(2 * parts, length, half)
@@ -1181,18 +1297,21 @@
 
     dm2 = cot.astype(low)
     d_att = part_product(dm2, w_mid, low, first=width_qkv + inner_width)
-    part_aout = sum_cores_back(attended, dm2)
+    part_mid = part_product(
+        dm2.T, attended, low, place=inner_width + width_qkv, room=inner_width + width_qkv + width_qkv // 3
+    )
     log_rows = jnp.pad(logs[:, :, :4].transpose(0, 2, 1), ((0, 0), (0, 4), (0, 0)))
     d_qkv = attn_backward(
         qkv, attended, d_att, log_rows, remb, []
     )
-    part_qkv = sum_cores(u2.T, d_qkv)
-    back, d_gain2 = rms_back(resid1, norm2_gain, part_back(d_qkv, w_mid, deps=[part_qkv]))
+    part_mid = part_product(u2.T, d_qkv, low, into=part_mid, place=inner_width)
+    back, d_gain2 = rms_back(resid1, norm2_gain, part_back(d_qkv, w_mid, first=inner_width, deps=[part_mid]))
     cot = cot + back
 
     dm1 = cot.astype(low)
-    d_gn = part_product(dm1, w_mid, jnp.float32, first=width_qkv, columns=inner_width)
-    part_mout = sum_cores_back(gnormed, dm1)
+    d_gn = part_product(dm1, w_mid, jnp.float32, columns=inner_width)
+    part_mid = outer_into(scaled, (cot * factor).astype(low), 1, 0, part_mid.shape[2], into=part_mid)
+    sum_mid = ring_scatter(part_mid.reshape(-1, part_mid.shape[2]))
     gated = ssm * gate * sigmoid(gate)
     cross = jnp.sum(jnp.sum(gated * gain_parts * d_gn, axis=2), axis=0)[:, None]
     cross = factor * factor * factor * cross / DIN
@@ -1214,27 +1333,8 @@
         cs,
         cs.T,
         states,
-        [part_qkv, part_mout, part_aout, sum_ffn],
-    )
-    order = x_first()
-    stage_qkv = sum_stages(part_qkv, order[:1])
-    last_qkv = sum_stages(stage_qkv, order[1:2])
-    piece_qkv = sum_stages(last_qkv, order[2:])
-    order = y_first()
-    stage_mout = sum_stages(part_mout, order[:1])
-    last_mout = sum_stages(stage_mout, order[1:2])
-    piece_mout = sum_stages(last_mout, order[2:])
-    stage_aout = sum_stages(part_aout, order[:1])
-    last_aout = sum_stages(stage_aout, order[1:2])
-    piece_aout = sum_stages(last_aout, order[2:])
-    rows_aout = jnp.concatenate(jnp.split(piece_aout, 2, axis=1), axis=0)
-    grad_mid = gather_sum(jnp.concatenate([piece_qkv, piece_mout, rows_aout], axis=1))
-    width_mout = piece_mout.shape[1]
-    grad_qkv = grad_mid[:, :width_qkv]
-    grad_mout = grad_mid[:, width_qkv : width_qkv + width_mout]
-    count = rows_aout.shape[0]
-    grad_aout = grad_mid[:, width_qkv + width_mout :].reshape(-1, 2, count // 2, width_mout // 2)
-    grad_aout = grad_aout.transpose(0, 2, 1, 3).reshape(-1, width_mout)
+        [part_mid, sum_ffn],
+    )
     d_cum = d_cols[:, :heads]
     d_step = d_cols[:, heads : 2 * heads]
     d_decay = lax.dot_general(
@@ -1259,28 +1359,39 @@
         ]
     )
     d_fed = lax.dynamic_update_slice(d_fed, d_rest, (0, 0, inner_width))
+    bits = dp_bits()
+    devices = lax.axis_size("dp")
     u1_t = u1.T
-    width_fed = d_fed.shape[2]
-    part_mix = part_product(
-        u1_t, d_fed, low, place=inner_width, room=inner_width + width_fed
-    )
-    part_mix = part_product(u1_t, d_z, low, into=part_mix)
-    grad_mix = ring_gather(ring_scatter(part_mix.reshape(-1, inner_width + width_fed)))
-    first_dt = 2 * inner_width + state
-    grad_ffn = ring_gather(sum_ffn)
-    back_u1 = part_back(
-        d_z, w_z, deps=[part_mix, stage_qkv, stage_mout, stage_aout]
-    )
-    back_u1 = part_back(
-        d_fed, w_x, start=back_u1, deps=[last_qkv, last_mout, last_aout, grad_ffn]
-    )
+    rank = {device: place for place, device in enumerate(ring_order())}
+    source = {block_of(device, bits): rank[device] for device in range(devices)}
+    u1_t = jnp.concatenate(
+        [u1_t[source[b] * shard : (source[b] + 1) * shard] for b in range(devices)], axis=0
+    )
+    part_z = sum_cores(u1_t, d_z)
+    part_x = sum_cores(u1_t, d_fed)
+    back_u1 = part_back(d_z, w_z, deps=[part_z, part_x, sum_mid])
+    back_u1 = part_back(d_fed, w_x, start=back_u1)
     back, d_gain1 = rms_back(resid0, norm1_gain, back_u1)
     cot = cot + back
 
-    bits = dp_bits()
     columns = cot.T.astype(low).reshape((2,) * bits + (shard, length))
     columns = columns.transpose(tuple(range(bits - 1, -1, -1)) + (bits, bits + 1))
-    counted = sum_stages(sum_cores(columns.reshape(-1, length), onehot), y_first())
+    grad_ffn = ring_gather(sum_ffn)
+    grad_mid = ring_gather(sum_mid)
+    counted = sum_cores(columns.reshape(-1, length), onehot, deps=[grad_ffn])
+    later = (counted[0, 0, 0].astype(jnp.float32) + mixed_row[0, 0]) * 0
+    after_theirs = theirs[0, 0] * 0
+    piece_z = sum_stages(part_z, x_first(), [later])
+    piece_x = sum_stages(part_x, y_first(), [later, 0.0, 0.0, after_theirs])
+    counted = sum_stages(counted, y_first())
+    grad_mix = lax.all_gather(
+        jnp.concatenate([piece_z, piece_x], axis=1),
+        "dp",
+        axis=0,
+        tiled=True,
+        axis_index_groups=[ring_order()],
+    )
+    first_dt = 2 * inner_width + state
     counted_all = gather_sum(counted, reversed_blocks=False)
     grad_patch = jnp.einsum(
         "vd,cpv->pdc",
@@ -1328,14 +1439,12 @@
     wide = jnp.float32
     half_bc = grad_mix[:, 2 * inner_width : 2 * inner_width + state]
     grad_bc = jnp.concatenate(list(both_parts(half_bc)), axis=1).astype(wide)
-    grad_out = grad_ffn[:, width_in:].reshape(lax.axis_size("dp"), shard, 2, model_width)
-    grad_out = grad_out.transpose(0, 2, 1, 3).reshape(-1, model_width)
     return (
         mixed,
         grad_table,
         grad_patch,
         d_gain1,
-        unfold(grad_mix[:, : 2 * inner_width], 2, inner_width),
+        unfold(grad_mix, 2, inner_width),
         grad_mix[:, first_dt : first_dt + heads_part].astype(wide),
         grad_bc,
         own_half(d_convx.reshape(taps, -1)),
@@ -1344,13 +1453,15 @@
         own_half(d_alog),
         own_half(d_skipped),
         own_half(d_ggain),
-        grad_mout.astype(wide),
+        refold(grad_mid, 0, 1, inner_width, 256),
         d_gain2,
-        unfold(grad_qkv, attn_qkv.shape[1], attn_qkv.shape[2]),
-        grad_aout.astype(wide),
+        grad_mid[:, inner_width : inner_width + width_qkv]
+        .astype(wide)
+        .reshape(model_width, attn_qkv.shape[1], -1),
+        grad_mid[:, inner_width + width_qkv :].T.astype(wide),
         d_gain3,
-        unfold(grad_ffn[:, :width_in], ffn_in.shape[1], half),
-        grad_out.astype(wide),
+        unfold(grad_ffn, ffn_in.shape[1], half),
+        refold(grad_ffn, width_in, 2, model_width, 256),
     )
 
 

time: 1280 us -> 1110 us (0.87)
  waiting for transfers between devices: 332 us -> 252 us
  local copies, waits for them, and re-layouts: 173 us -> 116 us
  starting transfers between devices: 101 us -> 53.3 us
  Pallas kernels: 484 us -> 521 us
  matrix products: 35.6 us -> 14.2 us
    ppermute x17 -> x16, waiting for transfers between devices: 163 us -> 115 us  [swap(): return lax.ppermute(value, 'mp', [(0, 1), (1, 0)])]
    ppermute x44 -> x40, starting transfers between devices: 81.6 us -> 36.2 us  [swap(): lax.ppermute(value, 'dp', [(i, i ^ 1 << stage) for i in range(count)])]
    ppermute x44 -> x40, waiting for transfers between devices: 159 us -> 115 us  [swap(): lax.ppermute(value, 'dp', [(i, i ^ 1 << stage) for i in range(count)])]
    unnamed x289 -> x241, local copies, waits for them, and re-layouts: 62.2 us -> 32.5 us
    convert_element_type x4 -> x0, local copies, waits for them, and re-layouts: 25.7 us -> none  [the longest x2 21.1 us: on_device_rows(): grad_out.astype(wide)]
    pallas_call x0 -> x4, Pallas kernels: none -> 23 us  [the longest x2 10.1 us: refold(): pl.pallas_call(refold_kernel, grid=(rows // step,), in_specs=[pl.BlockSpe...]
    dot_general x6 -> x0, matrix products: 21.3 us -> none  [the longest x4 16.4 us: outer_parts(): lax.dot_general(left, right, (((1,), (0,)), ((), ())), preferred_element_...]
    convert_element_type x6 -> x2, other arithmetic: 19.9 us -> 5.05 us  [the longest x1 3.53 us: on_device_rows(): (cot * factor).astype(low)]
  transfers between devices with their start and end apart: 69 -> 64, of which waited for: 38 -> 32; matrix products, arithmetic and copies ran while one was open for 23% -> 19% of each run, Pallas kernels for 32% -> 42%
where the time goes in v2:
time: 1110 us; the launch traced here: 1100 us
  Pallas kernels  521 us (47%)
  waiting for transfers between devices  252 us (23%)
  local copies, waits for them, and re-layouts  116 us (10%)
  other arithmetic  116 us (10%)
  starting transfers between devices  53.3 us (5%)
  between operations  25.9 us (2%)
  matrix products  14.2 us (1%)
    pallas_call x14, Pallas kernels, part_product(): pl.pallas_call(body, grid=(parts, count), in_specs=in_specs, out_specs=pl...  136 us
    ppermute x16, waiting for transfers between devices, swap(): return lax.ppermute(value, 'mp', [(0, 1), (1, 0)])  115 us
    ppermute x40, waiting for transfers between devices, swap(): lax.ppermute(value, 'dp', [(i, i ^ 1 << stage) for i in range(count)])  115 us
    pallas_call x7, Pallas kernels, part_back(): pl.pallas_call(body, grid=(parts, count), in_specs=in_specs, out_specs=pl...  110 us
    pallas_call x1, Pallas kernels, mix_backward(): pl.pallas_call(mix_bwd_kernel, grid=(groups,), in_specs=[pl.BlockSpec(blo...  60.4 us
    pallas_call x1, Pallas kernels, attn_backward(): pl.pallas_call(attn_bwd_kernel, grid=(groups,), in_specs=[pl.BlockSpec(bl...  38.8 us
    pallas_call x1, Pallas kernels, mix_forward(): pl.pallas_call(mix_fwd_kernel, grid=(groups,), in_specs=[pl.BlockSpec(blo...  38.2 us
    ppermute x40, starting transfers between devices, swap(): lax.ppermute(value, 'dp', [(i, i ^ 1 << stage) for i in range(count)])  36.2 us
  transfers between devices with their start and end apart: 64, of which 32 were waited for; matrix products, arithmetic and copies ran while one was open for 19% of the time, Pallas kernels for 42%

profile of v2, /device:TPU:0, one launch (start us, length us, event | category | flops | bytes accessed | tf_op | source)
XLA Modules:
  0.0 1097.5 jit_solution(17263027434622106363)
XLA Ops:
  24.6 9.2 collective-permute-done.4
  61.2 12.2 %collective-permute-done.7 = bf16[1,2,2,1,1,64,1024]{6,5,4,3,2,1,0:T(8,128)(2,1)S(1)} collective-permute-done((bf16[1,2,2,1,1,64,1024]{6,5,4,3,2,1,0:T(8,128)(2,1)S(1)}, bf16[1,2,2,1,1,64,1024]{6,5,4,3,2,1,0:T(8,128)(2,1)S(1)}, u32[]{:S(2)}, u32[]{:S(2)}) %collective-permute-start.7) | collective-permute-done | bytes 524320 | tf_op jit(solution)/shard_map/ppermute | solution.py:919
  91.5 11.5 %collective-permute-done.19 = bf16[1,2,1,1,1,64,1280]{6,5,4,3,2,1,0:T(8,128)(2,1)S(1)} collective-permute-done((bf16[1,2,1,1,1,64,1280]{6,5,4,3,2,1,0:T(8,128)(2,1)S(1)}, bf16[1,2,1,1,1,64,1280]{6,5,4,3,2,1,0:T(8,128)(2,1)S(1)}, u32[]{:S(2)}, u32[]{:S(2)}) %collective-permute-start.19) | collective-permute-done | bytes 327712 | tf_op jit(solution)/shard_map/ppermute | solution.py:921
  107.0 25.1 %collective-permute-done.20 = bf16[1,2,2,1,1,64,1280]{6,5,4,3,2,1,0:T(8,128)(2,1)S(1)} collective-permute-done((bf16[1,2,2,1,1,64,1280]{6,5,4,3,2,1,0:T(8,128)(2,1)S(1)}, bf16[1,2,2,1,1,64,1280]{6,5,4,3,2,1,0:T(8,128)(2,1)S(1)}, u32[]{:S(2)}, u32[]{:S(2)}) %collective-permute-start.20) | collective-permute-done | bytes 655392 | tf_op jit(solution)/shard_map/ppermute | solution.py:919
  139.1 20.9 %collective-permute-done.16 = bf16[1,2,2,2,1,64,1024]{6,5,4,3,2,1,0:T(8,128)(2,1)} collective-permute-done((bf16[1,2,2,2,1,64,1024]{6,5,4,3,2,1,0:T(8,128)(2,1)}, bf16[1,2,2,2,1,64,1024]{6,5,4,3,2,1,0:T(8,128)(2,1)}, u32[]{:S(2)}, u32[]{:S(2)}) %collective-permute-start.16) | collective-permute-done | bytes 1048608 | tf_op jit(solution)/shard_map/ppermute | solution.py:919
  163.8 17.3 %collective-permute-done.21 = bf16[2,2,2,1,1,64,1280]{6,5,4,3,2,1,0:T(8,128)(2,1)} collective-permute-done((bf16[2,2,2,1,1,64,1280]{6,5,4,3,2,1,0:T(8,128)(2,1)}, bf16[2,2,2,1,1,64,1280]{6,5,4,3,2,1,0:T(8,128)(2,1)}, u32[]{:S(2)}, u32[]{:S(2)}) %collective-permute-start.21) | collective-permute-done | bytes 1310752 | tf_op jit(solution)/shard_map/ppermute | solution.py:921
  199.2 10.0 embed_rows.1
  224.0 12.9 %part_product.15.x_ref = f32[2,1024,1280]{2,1,0:T(8,128)} custom-call(bf16[1024,1024]{1,0:T(8,128)(2,1)} %multiply_convert_fusion.3.left_ref, bf16[2,1024,1280]{2,1,0:T(8,128)(2,1)} %bitcast.258), custom_call_target="tpu_custom_call" | custom-call | flops 5368709120 | bytes 15728640 | tf_op jit(solution)/shard_map/part_product/pallas_call | solution.py:596
  250.6 38.2 %mix_fwd.1 = (f32[2,1024,1024]{2,1,0:T(8,128)}, bf16[2,1024,1024]{2,1,0:T(8,128)(2,1)}, bf16[4,128,2048]{2,1,0:T(8,128)(2,1)}, f32[1024,128]{1,0:T(8,128)}) custom-call(f32[2,1024,1024]{2,1,0:T(8,128)} %part_product.14.z_ref, f32[2,1024,1280]{2,1,0:T(8,128)} %part_product.15.x_ref, f32[1024,128]{1,0:T(8,128)} %pad_maximum_fusion.17.cols_ref, ...), custom_call_target="tpu_custom_call" | custom-call | flops 20000000000 | bytes 30000000 | tf_op jit(solution)/shard_map/mix_fwd/pallas_call | solution.py:323
  297.0 11.7 %part_back.7.others_0_ = f32[1024,1024]{1,0:T(8,128)} custom-call(bf16[2,1024,1024]{2,1,0:T(8,128)(2,1)} %get-tuple-element.42.left_ref, bf16[2,1024,3072]{2,1,0:T(8,128)(2,1)} %bitcast.235, f32[1024,1024]{1,0:T(8,128)} %get-tuple-element.40.others_0_, f32[1024,128]{1,0:T(8,128)} %broadcast_in_dim.49.others_1_.rg_ref), custom_call_target="tpu_custom_call" | custom-call | flops 4294967296 | bytes 12582912 | tf_op jit(solution)/shard_map/part_back/pallas_call | solution.py:655
  314.0 11.3 %part_product.16.q_ref.k_ref.v_ref = bf16[2,1024,1536]{2,1,0:T(8,128)(2,1)} custom-call(bf16[1024,1024]{1,0:T(8,128)(2,1)} %multiply_convert_fusion.2.left_ref, bf16[2,1024,3072]{2,1,0:T(8,128)(2,1)} %bitcast.236), custom_call_target="tpu_custom_call" | custom-call | flops 6442450944 | bytes 18874368 | tf_op jit(solution)/shard_map/part_product/pallas_call | solution.py:596
  325.3 25.3 %attn_fwd.1 = (bf16[2,1024,512]{2,1,0:T(8,128)(2,1)}, f32[4,1024,128]{2,1,0:T(8,128)}) custom-call(bf16[2,1024,1536]{2,1,0:T(8,128)(2,1)} %part_product.16.q_ref.k_ref.v_ref, bf16[2,1024,1536]{2,1,0:T(8,128)(2,1)} %part_product.16.q_ref.k_ref.v_ref, bf16[2,1024,1536]{2,1,0:T(8,128)(2,1)} %part_product.16.q_ref.k_ref.v_ref, f32[1024,128]{1,0:T(8,128)} %get-tuple-element.39.pos_ref), custom_call_target="tpu_custom_call" | custom-call | flops 30000001024 | bytes 10000000 | tf_op jit(solution)/shard_map/attn_fwd/pallas_call | solution.py:100
  369.3 20.3 %all-gather.10.cloned.1.call-done = bf16[2048,6144]{1,0:T(8,128)(2,1)} async-done(((bf16[64,6144]{1,0:T(8,128)(2,1)}), bf16[2048,6144]{1,0:T(8,128)(2,1)}) %all-gather.10.cloned.1.call-update) | async-done | bytes 25165840 | tf_op jit(solution)/shard_map/all_gather | solution.py:1089
  389.6 23.3 %ffn_in.1 = (bf16[2,1024,2048]{2,1,0:T(8,128)(2,1)}, bf16[2,1024,2048]{2,1,0:T(8,128)(2,1)}, bf16[2,1024,2048]{2,1,0:T(8,128)(2,1)}) custom-call(bf16[1024,1024]{1,0:T(8,128)(2,1)} %multiply_convert_fusion.1.left_ref, bf16[2,1024,6144]{2,1,0:T(8,128)(2,1)} %bitcast.242, bf16[2,1024,6144]{2,1,0:T(8,128)(2,1)} %bitcast.243), custom_call_target="tpu_custom_call" | custom-call | flops 17179869184 | bytes 41943040 | tf_op jit(solution)/shard_map/ffn_in/pallas_call | solution.py:752
  419.8 14.6 %outer_into.2.others_0_ = bf16[2,1024,6144]{2,1,0:T(8,128)(2,1)} custom-call(bf16[2,1024,2048]{2,1,0:T(8,128)(2,1)} %get-tuple-element.45.left_ref, bf16[1024,1024]{1,0:T(8,128)(2,1)} %fusion.2.left_ref.right_ref), custom_call_target="tpu_custom_call" | custom-call | flops 8589934592 | bytes 16777216 | tf_op jit(solution)/shard_map/outer_into/pallas_call | solution.py:692
  434.4 22.3 %ffn_back.1 = bf16[2,2,1024,2048]{3,2,1,0:T(8,128)(2,1)} custom-call(bf16[1024,1024]{1,0:T(8,128)(2,1)} %fusion.2.left_ref.right_ref, bf16[2,1024,6144]{2,1,0:T(8,128)(2,1)} %bitcast.244, bf16[2,1024,2048]{2,1,0:T(8,128)(2,1)} %get-tuple-element.47.gate_ref, bf16[2,1024,2048]{2,1,0:T(8,128)(2,1)} %get-tuple-element.48.up_ref), custom_call_target="tpu_custom_call" | custom-call | flops 8589934592 | bytes 41943040 | tf_op jit(solution)/shard_map/ffn_back/pallas_call | solution.py:788
  456.7 25.9 %part_product.17.others_0_ = bf16[2,1024,6144]{2,1,0:T(8,128)(2,1)} custom-call(bf16[1024,1024]{1,0:T(8,128)(2,1)} %copy.206.left_ref, bf16[4,1024,2048]{2,1,0:T(8,128)(2,1)} %bitcast.247, bf16[2,1024,6144]{2,1,0:T(8,128)(2,1)} %outer_into.2.others_0_), custom_call_target="tpu_custom_call", output_to_operand_aliasing={{}: (2, {})} | custom-call | flops 17179869184 | bytes 50331648 | tf_op jit(solution)/shard_map/part_product/pallas_call | solution.py:596
  495.2 31.1 %part_back.10 = f32[1024,1024]{1,0:T(8,128)} custom-call(bf16[4,1024,2048]{2,1,0:T(8,128)(2,1)} %bitcast.248, bf16[2,1024,6144]{2,1,0:T(8,128)(2,1)} %bitcast.245, bf16[2,1024,6144]{2,1,0:T(8,128)(2,1)} %part_product.17.others_0_), custom_call_target="tpu_custom_call" | custom-call | flops 17179869184 | bytes 37748736 | tf_op jit(solution)/shard_map/part_back/pallas_call | solution.py:655
  549.3 38.8 %attn_bwd.1.right_ref.left_ref = bf16[2,1024,1536]{2,1,0:T(8,128)(2,1)} custom-call(bf16[2,1024,1536]{2,1,0:T(8,128)(2,1)} %part_product.16.q_ref.k_ref.v_ref, bf16[2,1024,1536]{2,1,0:T(8,128)(2,1)} %part_product.16.q_ref.k_ref.v_ref, bf16[2,1024,1536]{2,1,0:T(8,128)(2,1)} %part_product.16.q_ref.k_ref.v_ref, ...), custom_call_target="tpu_custom_call" | custom-call | flops 70000001024 | bytes 20000000 | tf_op jit(solution)/shard_map/attn_bwd/pallas_call | solution.py:196
  588.0 11.4 %part_product.20.others_0_ = bf16[2,1024,3072]{2,1,0:T(8,128)(2,1)} custom-call(bf16[1024,1024]{1,0:T(8,128)(2,1)} %copy.209.left_ref, bf16[2,1024,1536]{2,1,0:T(8,128)(2,1)} %attn_bwd.1.right_ref.left_ref, bf16[2,1024,3072]{2,1,0:T(8,128)(2,1)} %part_product.19.others_0_), custom_call_target="tpu_custom_call", output_to_operand_aliasing={{}: (2, {})} | custom-call | flops 6442450944 | bytes 18874368 | tf_op jit(solution)/shard_map/part_product/pallas_call | solution.py:596
  599.5 13.7 %part_back.11 = f32[1024,1024]{1,0:T(8,128)} custom-call(bf16[2,1024,1536]{2,1,0:T(8,128)(2,1)} %attn_bwd.1.right_ref.left_ref, bf16[2,1024,3072]{2,1,0:T(8,128)(2,1)} %bitcast.239, bf16[2,1024,3072]{2,1,0:T(8,128)(2,1)} %part_product.20.others_0_), custom_call_target="tpu_custom_call" | custom-call | flops 6442450944 | bytes 16777216 | tf_op jit(solution)/shard_map/part_back/pallas_call | solution.py:655
  621.7 10.2 outer_into.3.others_0_
  660.1 9.9 multiply_reduce_fusion
  671.1 60.4 %mix_bwd.1 = (bf16[2,1024,1024]{2,1,0:T(8,128)(2,1)}, bf16[2,1024,1280]{2,1,0:T(8,128)(2,1)}, f32[1024,128]{1,0:T(8,128)}, f32[8,2048]{1,0:T(8,128)}, f32[1024,128]{1,0:T(8,128)}, /*index=5*/f32[1024,128]{1,0:T(8,128)}) custom-call(f32[2,1024,1024]{2,1,0:T(8,128)} %part_product.14.z_ref, f32[2,1024,1280]{2,1,0:T(8,128)} %part_product.15.x_ref, ...), custom_call_target="tpu_custom_call" | custom-call | flops 49999998976 | bytes 50000000 | tf_op jit(solution)/shard_map/mix_bwd/pallas_call | solution.py:499
  742.8 9.7 part_product.24
  771.1 10.2 part_product.25.others_1_
  781.4 10.1 part_back.12.others_0_
  791.5 16.7 %part_back.13 = f32[1024,1024]{1,0:T(8,128)} custom-call(bf16[2,1024,1280]{2,1,0:T(8,128)(2,1)} %maximum_dynamic-update-slice_fusion.right_ref.left_ref, bf16[2,1024,1280]{2,1,0:T(8,128)(2,1)} %bitcast.259, f32[1024,1024]{1,0:T(8,128)} %part_back.12.others_0_), custom_call_target="tpu_custom_call" | custom-call | flops 5368709120 | bytes 14680064 | tf_op jit(solution)/shard_map/part_back/pallas_call | solution.py:655
  825.7 18.7 %part_back.9 = f32[1024,1024]{1,0:T(8,128)} custom-call(bf16[2,1024,2048]{2,1,0:T(8,128)(2,1)} %get-tuple-element.45.left_ref, bf16[2,1024,6144]{2,1,0:T(8,128)(2,1)} %bitcast.246, f32[1024,1024]{1,0:T(8,128)} %part_back.8.others_0_), custom_call_target="tpu_custom_call" | custom-call | flops 8589934592 | bytes 20971520 | tf_op jit(solution)/shard_map/part_back/pallas_call | solution.py:655
  862.2 33.6 %collective-permute-done.23 = f32[512,1024]{1,0:T(8,128)} collective-permute-done((f32[512,1024]{1,0:T(8,128)}, f32[512,1024]{1,0:T(8,128)}, u32[]{:S(2)}, u32[]{:S(2)}) %collective-permute-start.23) | collective-permute-done | bytes 2097184 | tf_op jit(solution)/shard_map/ppermute | solution.py:919
  912.1 14.3 %collective-permute-done.47 = bf16[512,1024]{1,0:T(8,128)(2,1)} collective-permute-done((bf16[512,1024]{1,0:T(8,128)(2,1)}, bf16[512,1024]{1,0:T(8,128)(2,1)}, u32[]{:S(2)}, u32[]{:S(2)}) %collective-permute-start.47) | collective-permute-done | bytes 1048608 | tf_op jit(solution)/shard_map/ppermute | solution.py:919
  1053.6 11.4 %unfold.3 = f32[1024,2,2048]{2,1,0:T(2,128)} custom-call(bf16[1024,6144]{1,0:T(8,128)(2,1)} %all-gather.12.cloned.1.call-done.others_1_.in_ref), custom_call_target="tpu_custom_call" | custom-call | bytes 25165824 | tf_op jit(solution)/shard_map/unfold/pallas_call | solution.py:723
  (639 shorter events, 459.3 us)
Async XLA Ops:
  7.2 288.8 %all-gather.8.cloned.1.call-start = ((), (), s32[]{:S(2)}) async-start(), calls=%async_computation.2 | async-start | bytes 12976128 | tf_op jit(solution)/shard_map/all_gather | solution.py:1089
  78.2 311.4 %all-gather.10.cloned.1.call-start = ((), (), s32[]{:S(2)}) async-start(), calls=%async_computation.3 | async-start | bytes 25952256 | tf_op jit(solution)/shard_map/all_gather | solution.py:1089
  79.2 25.4 %collective-permute-start.10 = (f32[1072]{0:T(1024)S(1)}, f32[1072]{0:T(1024)S(1)}, u32[]{:S(2)}, u32[]{:S(2)}) collective-permute-start(f32[1072]{0:T(1024)S(1)} %concatenate.224), channel_id=1, source_target_pairs={{0,1},{1,0},{2,3},{3,2},{4,5},{5,4},{6,7},{7,6},{8,9},{9,8},{10,11... | collective-permute-start | bytes 12872 | tf_op jit(solution)/shard_map/ppermute | solution.py:919
  81.0 52.4 %collective-permute-start = (s32[512,8]{0,1:T(8,128)S(1)}, s32[512,8]{0,1:T(8,128)S(1)}, u32[]{:S(2)}, u32[]{:S(2)}) collective-permute-start(s32[512,8]{0,1:T(8,128)S(1)} %dynamic-slice_bitcast_fusion.4), channel_id=1, source_target_pairs={{0,1},{1,0},{2,3},{3,2},{4,5},{5,4},{6,7},{7,6},{8,9},{9,8},{10,11... | collective-permute-start | bytes 49160 | tf_op jit(solution)/shard_map/ppermute | solution.py:919
  81.3 52.1 %collective-permute-start.9 = (f32[4,1024]{1,0:T(4,128)S(1)}, f32[4,1024]{1,0:T(4,128)S(1)}, u32[]{:S(2)}, u32[]{:S(2)}) collective-permute-start(f32[4,1024]{1,0:T(4,128)S(1)} %copy-done.86), channel_id=1, source_target_pairs={{0,1},{1,0},{2,3},{3,2},{4,5},{5,4},{6,7},{7,6},{8,9},{9,8},{10,11... | collective-permute-start | bytes 49160 | tf_op jit(solution)/shard_map/ppermute | solution.py:919
  86.2 16.8 %collective-permute-start.19 = (bf16[1,2,1,1,1,64,1280]{6,5,4,3,2,1,0:T(8,128)(2,1)S(1)}, bf16[1,2,1,1,1,64,1280]{6,5,4,3,2,1,0:T(8,128)(2,1)S(1)}, u32[]{:S(2)}, u32[]{:S(2)}) collective-permute-start(bf16[1,2,1,1,1,64,1280]{6,5,4,3,2,1,0:T(8,128)(2,1)S(1)} %pad_maximum_fusion.19), channel_id=1, source_target_pairs={{0,8},{2,10},{4,12},{6,14},{8,0},{10,2},{12,4},{14,6},{16,24},{18,... | collective-permute-start | bytes 983048 | tf_op jit(solution)/shard_map/ppermute | solution.py:921
  103.1 29.0 %collective-permute-start.20 = (bf16[1,2,2,1,1,64,1280]{6,5,4,3,2,1,0:T(8,128)(2,1)S(1)}, bf16[1,2,2,1,1,64,1280]{6,5,4,3,2,1,0:T(8,128)(2,1)S(1)}, u32[]{:S(2)}, u32[]{:S(2)}) collective-permute-start(bf16[1,2,2,1,1,64,1280]{6,5,4,3,2,1,0:T(8,128)(2,1)S(1)} %pad_maximum_fusion.13), channel_id=1, source_target_pairs={{0,1},{1,0},{2,3},{3,2},{4,5},{5,4},{6,7},{7,6},{8,9},{9,8},{10,11... | collective-permute-start | bytes 1966088 | tf_op jit(solution)/shard_map/ppermute | solution.py:919
  105.3 56.4 %collective-permute-start.11 = (bf16[2,2,2,1,1,64,1024]{6,5,4,3,2,1,0:T(8,128)(2,1)}, bf16[2,2,2,1,1,64,1024]{6,5,4,3,2,1,0:T(8,128)(2,1)}, u32[]{:S(2)}, u32[]{:S(2)}) collective-permute-start(bf16[2,2,2,1,1,64,1024]{6,5,4,3,2,1,0:T(8,128)(2,1)} %pad_maximum_fusion.10), channel_id=1, source_target_pairs={{0,4},{2,6},{4,0},{6,2},{8,12},{10,14},{12,8},{14,10},{16,20},{18,... | collective-permute-start | bytes 3145736 | tf_op jit(solution)/shard_map/ppermute | solution.py:921
  106.5 53.6 %collective-permute-start.16 = (bf16[1,2,2,2,1,64,1024]{6,5,4,3,2,1,0:T(8,128)(2,1)}, bf16[1,2,2,2,1,64,1024]{6,5,4,3,2,1,0:T(8,128)(2,1)}, u32[]{:S(2)}, u32[]{:S(2)}) collective-permute-start(bf16[1,2,2,2,1,64,1024]{6,5,4,3,2,1,0:T(8,128)(2,1)} %pad_maximum_fusion.11), channel_id=1, source_target_pairs={{0,1},{1,0},{2,3},{3,2},{4,5},{5,4},{6,7},{7,6},{8,9},{9,8},{10,11... | collective-permute-start | bytes 3145736 | tf_op jit(solution)/shard_map/ppermute | solution.py:919
  133.4 47.8 %collective-permute-start.21 = (bf16[2,2,2,1,1,64,1280]{6,5,4,3,2,1,0:T(8,128)(2,1)}, bf16[2,2,2,1,1,64,1280]{6,5,4,3,2,1,0:T(8,128)(2,1)}, u32[]{:S(2)}, u32[]{:S(2)}) collective-permute-start(bf16[2,2,2,1,1,64,1280]{6,5,4,3,2,1,0:T(8,128)(2,1)} %pad_maximum_fusion.9), channel_id=1, source_target_pairs={{0,4},{2,6},{4,0},{6,2},{8,12},{10,14},{12,8},{14,10},{16,20},{18,... | collective-permute-start | bytes 3932168 | tf_op jit(solution)/shard_map/ppermute | solution.py:921
  161.6 22.2 %collective-permute-start.17 = (bf16[2,2,2,2,1,64,1024]{6,5,4,3,2,1,0:T(8,128)(2,1)S(1)}, bf16[2,2,2,2,1,64,1024]{6,5,4,3,2,1,0:T(8,128)(2,1)S(1)}, u32[]{:S(2)}, u32[]{:S(2)}) collective-permute-start(bf16[2,2,2,2,1,64,1024]{6,5,4,3,2,1,0:T(8,128)(2,1)S(1)} %pad_maximum_fusion.7), channel_id=1, source_target_pairs={{0,2},{2,0},{4,6},{6,4},{8,10},{10,8},{12,14},{14,12},{16,18},{18,... | collective-permute-start | bytes 6291464 | tf_op jit(solution)/shard_map/ppermute | solution.py:921
  163.3 21.8 %collective-permute-start.12 = (bf16[2,2,2,2,1,64,1024]{6,5,4,3,2,1,0:T(8,128)(2,1)S(1)}, bf16[2,2,2,2,1,64,1024]{6,5,4,3,2,1,0:T(8,128)(2,1)S(1)}, u32[]{:S(2)}, u32[]{:S(2)}) collective-permute-start(bf16[2,2,2,2,1,64,1024]{6,5,4,3,2,1,0:T(8,128)(2,1)S(1)} %pad_maximum_fusion.6), channel_id=1, source_target_pairs={{0,2},{2,0},{4,6},{6,4},{8,10},{10,8},{12,14},{14,12},{16,18},{18,... | collective-permute-start | bytes 6291464 | tf_op jit(solution)/shard_map/ppermute | solution.py:921
  195.6 436.4 %reduce-scatter.3.cloned.1.call-start = ((), (), s32[]{:S(2)}) async-start(), calls=%async_computation.4 | async-start | bytes 25952256 | tf_op jit(solution)/shard_map/reduce_scatter | solution.py:1018
  295.1 119.7 %collective-permute-start.24 = (f32[512,1024]{1,0:T(8,128)}, f32[512,1024]{1,0:T(8,128)}, u32[]{:S(2)}, u32[]{:S(2)}) collective-permute-start(f32[512,1024]{1,0:T(8,128)} %add_bitcast_fusion), channel_id=1, source_target_pairs={{0,1},{1,0},{2,3},{3,2},{4,5},{5,4},{6,7},{7,6},{8,9},{9,8},{10,11... | collective-permute-start | bytes 6291464 | tf_op jit(solution)/shard_map/ppermute | solution.py:919
  482.7 276.4 %reduce-scatter.5.cloned.1.call-start = ((), (), s32[]{:S(2)}) async-start(), calls=%async_computation.5 | async-start | bytes 12976128 | tf_op jit(solution)/shard_map/reduce_scatter | solution.py:1018
  632.0 215.7 %all-gather.12.cloned.1.call-start = ((), (), s32[]{:S(2)}) async-start(), calls=%async_computation.6 | async-start | bytes 13369344 | tf_op jit(solution)/shard_map/all_gather | solution.py:1028
  632.5 381.6 %all-gather.16.cloned.1.call-start = ((), (), s32[]{:S(2)}) async-start(), calls=%async_computation.8 | async-start | bytes 6684672 | tf_op jit(solution)/shard_map/all_gather | solution.py:1028
  752.5 18.7 %collective-permute-start.26 = (bf16[2,512,1280]{2,1,0:T(8,128)(2,1)}, bf16[2,512,1280]{2,1,0:T(8,128)(2,1)}, u32[]{:S(2)}, u32[]{:S(2)}) collective-permute-start(bf16[2,512,1280]{2,1,0:T(8,128)(2,1)} %part_product.24), channel_id=1, source_target_pairs={{0,2},{2,0},{4,6},{6,4},{8,10},{10,8},{12,14},{14,12},{16,18},{18,... | collective-permute-start | bytes 7864328 | tf_op jit(solution)/shard_map/ppermute | solution.py:921
  759.1 307.1 %all-gather.18.cloned.1.call-start = ((), (), s32[]{:S(2)}) async-start(), calls=%async_computation.9 | async-start | bytes 2228224 | tf_op jit(solution)/shard_map/all_gather | solution.py:997
  825.6 22.0 %collective-permute-start.27 = (bf16[2,512,1024]{2,1,0:T(8,128)(2,1)}, bf16[2,512,1024]{2,1,0:T(8,128)(2,1)S(1)}, u32[]{:S(2)}, u32[]{:S(2)}) collective-permute-start(bf16[2,512,1024]{2,1,0:T(8,128)(2,1)} %part_product.26), channel_id=1, source_target_pairs={{0,2},{2,0},{4,6},{6,4},{8,10},{10,8},{12,14},{14,12},{16,18},{18,... | collective-permute-start | bytes 6291464 | tf_op jit(solution)/shard_map/ppermute | solution.py:921
  847.6 48.2 %collective-permute-start.23 = (f32[512,1024]{1,0:T(8,128)}, f32[512,1024]{1,0:T(8,128)}, u32[]{:S(2)}, u32[]{:S(2)}) collective-permute-start(f32[512,1024]{1,0:T(8,128)} %constant_dynamic-slice_fusion.19), channel_id=1, source_target_pairs={{0,1},{1,0},{2,3},{3,2},{4,5},{5,4},{6,7},{7,6},{8,9},{9,8},{10,11... | collective-permute-start | bytes 6291464 | tf_op jit(solution)/shard_map/ppermute | solution.py:919
  858.0 46.2 %collective-permute-start.28 = (bf16[2,256,1024]{2,1,0:T(8,128)(2,1)}, bf16[2,256,1024]{2,1,0:T(8,128)(2,1)}, u32[]{:S(2)}, u32[]{:S(2)}) collective-permute-start(bf16[2,256,1024]{2,1,0:T(8,128)(2,1)} %constant_dynamic-slice_fusion.14), channel_id=1, source_target_pairs={{0,4},{2,6},{4,0},{6,2},{8,12},{10,14},{12,8},{14,10},{16,20},{18,... | collective-permute-start | bytes 3145736 | tf_op jit(solution)/shard_map/ppermute | solution.py:921
  900.0 26.4 %collective-permute-start.47 = (bf16[512,1024]{1,0:T(8,128)(2,1)}, bf16[512,1024]{1,0:T(8,128)(2,1)}, u32[]{:S(2)}, u32[]{:S(2)}) collective-permute-start(bf16[512,1024]{1,0:T(8,128)(2,1)} %dynamic-slice_bitcast_fusion), channel_id=1, source_target_pairs={{0,1},{1,0},{2,3},{3,2},{4,5},{5,4},{6,7},{7,6},{8,9},{9,8},{10,11... | collective-permute-start | bytes 3145736 | tf_op jit(solution)/shard_map/ppermute | solution.py:919
  901.4 34.9 %collective-permute-start.51 = (bf16[2,256,1280]{2,1,0:T(8,128)(2,1)}, bf16[2,256,1280]{2,1,0:T(8,128)(2,1)}, u32[]{:S(2)}, u32[]{:S(2)}) collective-permute-start(bf16[2,256,1280]{2,1,0:T(8,128)(2,1)} %constant_dynamic-slice_fusion.3), channel_id=1, source_target_pairs={{0,4},{2,6},{4,0},{6,2},{8,12},{10,14},{12,8},{14,10},{16,20},{18,... | collective-permute-start | bytes 3932168 | tf_op jit(solution)/shard_map/ppermute | solution.py:921
  907.6 28.4 %collective-permute-start.29 = (bf16[256,1024]{1,0:T(8,128)(2,1)}, bf16[256,1024]{1,0:T(8,128)(2,1)S(1)}, u32[]{:S(2)}, u32[]{:S(2)}) collective-permute-start(bf16[256,1024]{1,0:T(8,128)(2,1)} %dynamic-slice_bitcast_fusion.2), channel_id=1, source_target_pairs={{0,1},{1,0},{2,3},{3,2},{4,5},{5,4},{6,7},{7,6},{8,9},{9,8},{10,11... | collective-permute-start | bytes 1572872 | tf_op jit(solution)/shard_map/ppermute | solution.py:919
  928.4 15.6 %collective-permute-start.48 = (bf16[256,1024]{1,0:T(8,128)(2,1)S(1)}, bf16[256,1024]{1,0:T(8,128)(2,1)S(1)}, u32[]{:S(2)}, u32[]{:S(2)}) collective-permute-start(bf16[256,1024]{1,0:T(8,128)(2,1)S(1)} %constant_dynamic-slice_fusion.6), channel_id=1, source_target_pairs={{0,4},{2,6},{4,0},{6,2},{8,12},{10,14},{12,8},{14,10},{16,20},{18,... | collective-permute-start | bytes 1572872 | tf_op jit(solution)/shard_map/ppermute | solution.py:921
  940.0 15.5 %collective-permute-start.52 = (bf16[256,1280]{1,0:T(8,128)(2,1)}, bf16[256,1280]{1,0:T(8,128)(2,1)S(1)}, u32[]{:S(2)}, u32[]{:S(2)}) collective-permute-start(bf16[256,1280]{1,0:T(8,128)(2,1)} %dynamic-slice_bitcast_fusion.1), channel_id=1, source_target_pairs={{0,1},{1,0},{2,3},{3,2},{4,5},{5,4},{6,7},{7,6},{8,9},{9,8},{10,11... | collective-permute-start | bytes 1966088 | tf_op jit(solution)/shard_map/ppermute | solution.py:919
  951.1 117.2 %all-gather.14.cloned.1.call-start = ((), (), s32[]{:S(2)}) async-start(), calls=%async_computation.7 | async-start | bytes 5013504 | tf_op jit(solution)/shard_map/all_gather | solution.py:1387
  1019.7 23.3 %collective-permute-start.46 = (f32[15,1024]{1,0:T(8,128)S(1)}, f32[15,1024]{1,0:T(8,128)S(1)}, u32[]{:S(2)}, u32[]{:S(2)}) collective-permute-start(f32[15,1024]{1,0:T(8,128)S(1)} %add.522), channel_id=1, source_target_pairs={{0,16},{2,18},{4,20},{6,22},{8,24},{10,26},{12,28},{14,30},{16,0},... | collective-permute-start | bytes 184328 | tf_op jit(solution)/shard_map/ppermute | solution.py:921
  1020.9 22.3 %collective-permute-start.40 = (f32[64,1024]{1,0:T(8,128)S(1)}, f32[64,1024]{1,0:T(8,128)S(1)}, u32[]{:S(2)}, u32[]{:S(2)}) collective-permute-start(f32[64,1024]{1,0:T(8,128)S(1)} %pad_maximum_fusion.24), channel_id=1, source_target_pairs={{0,1},{1,0},{2,3},{3,2},{4,5},{5,4},{6,7},{7,6},{8,9},{9,8},{10,11... | collective-permute-start | bytes 786440 | tf_op jit(solution)/shard_map/ppermute | solution.py:919
  1043.3 21.7 %collective-permute-start.41 = (f32[128,1024]{1,0:T(8,128)S(1)}, f32[128,1024]{1,0:T(8,128)S(1)}, u32[]{:S(2)}, u32[]{:S(2)}) collective-permute-start(f32[128,1024]{1,0:T(8,128)S(1)} %pad_maximum_fusion.18), channel_id=1, source_target_pairs={{0,2},{2,0},{4,6},{6,4},{8,10},{10,8},{12,14},{14,12},{16,18},{18,... | collective-permute-start | bytes 1572872 | tf_op jit(solution)/shard_map/ppermute | solution.py:921
  1069.3 19.1 %collective-permute-start.55 = (bf16[1024,128]{1,0:T(8,128)(2,1)S(1)}, bf16[1024,128]{1,0:T(8,128)(2,1)S(1)}, u32[]{:S(2)}, u32[]{:S(2)}) collective-permute-start(bf16[1024,128]{1,0:T(8,128)(2,1)S(1)} %slice.500), channel_id=1, source_target_pairs={{0,1},{1,0},{2,3},{3,2},{4,5},{5,4},{6,7},{7,6},{8,9},{9,8},{10,11... | collective-permute-start | bytes 786440 | tf_op jit(solution)/shard_map/ppermute | solution.py:919
  (138 other events, 1889.6 us)
Sparse Core Ops, SparseCore 0:
  78.4 121.5 all-gather.7
  202.8 186.7 all-gather.9
  482.8 139.1 reduce-scatter.2
  632.1 100.9 reduce-scatter.4
  734.4 72.3 all-gather.11
  808.2 50.6 all-gather.15
  951.2 34.8 all-gather.17
  988.3 40.0 all-gather.13

commit v3 on v2

--- a/solution.py
+++ b/solution.py
@@ -683,12 +683,12 @@
             ]
 
 
-def outer_into(left, right, wraps, place, room, into=None):
+def outer_into(left, right, wraps, place, room, into=None, deps=()):
     parts, length, columns = left.shape
     width = right.shape[1]
     tile = 256 * wraps
     begin = place // (wraps * width)
-    before = [] if into is None else [into]
+    before = ([] if into is None else [into]) + list(deps)
     return pl.pallas_call(
         outer_kernel,
         grid=(parts, columns // tile),
@@ -697,7 +697,7 @@
             pl.BlockSpec((length, width), lambda m, n: (0, 0)),
         ]
         + [pl.BlockSpec(memory_space=pl.ANY)] * len(before),
-        input_output_aliases={2: 0} if before else {},
+        input_output_aliases={} if into is None else {2: 0},
         out_specs=pl.BlockSpec((1, tile // wraps, wraps * width), lambda m, n: (m, n, begin)),
         out_shape=jax.ShapeDtypeStruct((parts, columns // wraps, room), jnp.bfloat16),
         compiler_params=pltpu.CompilerParams(vmem_limit_bytes=VMEM_LIMIT),
@@ -862,7 +862,7 @@
     )(value)
 
 
-def embed_kernel(ids_ref, mapped_ref, onehot_ref, out_ref):
+def embed_kernel(ids_ref, first_ref, second_ref, onehot_ref, out_ref):
     length = ids_ref.shape[1]
     value = lax.broadcasted_iota(jnp.int32, (length, VOCAB), 1)
     total = None
@@ -870,7 +870,9 @@
         span = pl.ds(p * VOCAB, VOCAB)
         hit = jnp.where(ids_ref[0, :, p : p + 1] == value, 1.0, 0.0).astype(jnp.bfloat16)
         onehot_ref[0, :, span] = hit
-        part = dot_nt(hit, mapped_ref[0, :, span])
+        half = ids_ref.shape[2] // 2
+        source = first_ref if p < half else second_ref
+        part = dot_nt(hit, source[0, :, pl.ds((p % half) * VOCAB, VOCAB)])
         total = part if total is None else total + part
 
     @pl.when(pl.program_id(0) == 0)
@@ -882,15 +884,16 @@
         out_ref[...] += total
 
 
-def embed_rows(ids, mapped):
+def embed_rows(ids, first, second):
     parts, length, count = ids.shape
-    width = mapped.shape[1]
+    width = first.shape[1]
     return pl.pallas_call(
         embed_kernel,
         grid=(parts,),
         in_specs=[
             pl.BlockSpec((1, length, count), lambda m: (m, 0, 0)),
-            pl.BlockSpec((1, width, count * VOCAB), lambda m: (m, 0, 0)),
+            pl.BlockSpec((1,) + first.shape[1:], lambda m: (m, 0, 0)),
+            pl.BlockSpec((1,) + second.shape[1:], lambda m: (m, 0, 0)),
         ],
         out_specs=[
             pl.BlockSpec((1, length, count * VOCAB), lambda m: (m, 0, 0)),
@@ -907,7 +910,7 @@
             transcendentals=0,
         ),
         name="embed_rows",
-    )(ids, mapped)
+    )(ids, first, second)
 
 
 def bit_of(index, bit):
@@ -1044,8 +1047,8 @@
         bit = my_bit(stage)
         if turn == peek:
             seen = value
-        if turn == 3 and after is not None:
-            value = value + after
+        if after is not None and turn in after:
+            value = value + after[turn].astype(value.dtype)
         value = jnp.concatenate(
             [jnp.where(bit == 0, value, other), jnp.where(bit == 0, other, value)], axis=axis
         )
@@ -1185,7 +1188,8 @@
         [mamba_in[:, 1], bc_half, mamba_dt, jnp.zeros((shard, pad), low)], axis=1
     )
     shard_qkv = attn_qkv.reshape(shard, -1)
-    shard_mid = jnp.concatenate([mamba_out.T, shard_qkv, attn_out.T], axis=1)
+    shard_back = jnp.concatenate([mamba_out.T, attn_out.T], axis=1)
+    width_qkv = shard_qkv.shape[1]
     shard_ffn = jnp.concatenate([ffn_in.reshape(shard, -1), ffn_out.T], axis=1)
     width_in = ffn_in.shape[1] * ffn_in.shape[2]
 
@@ -1195,30 +1199,29 @@
         rows_by_pos, table, (((1,), (1,)), ((), ())), preferred_element_type=jnp.float32
     ).astype(low)
     mapped = mapped.transpose(1, 0, 2).reshape(rows_by_pos.shape[2], -1)
-    table_ready = table[0, 0] * 0
     posb, remb = spans(seg)
     ids_parts = ids.reshape(length, parts, per_pos).transpose(1, 0, 2)
     prepared = posb[0, 0] + ids_parts[0, 0, 0].astype(jnp.float32)
-    prepared = ((prepared + conv_full[0, 0] + ggain_full[0]) * 0).astype(low)
-    mapped, early = gather_steps(mapped, gather_y_last(), peek=3, after=prepared)
+    prepared = (prepared + conv_full[0, 0] + ggain_full[0]) * 0
+    half_map = mapped.shape[1] // 2
+    mapped_a, early = gather_steps(
+        mapped[:, :half_map], gather_y_last(), peek=3, after={3: prepared}
+    )
+    mapped_b = gather_steps(mapped[:, half_map:], gather_x_last())
     early = early.reshape(-1)[0] * 0
-    w_z = gather_steps(shard_z + table_ready, gather_x_last())
-    w_x = gather_steps(shard_x + table_ready, gather_y_last())
-    mapped_ready = mapped[0, 0, 0] * 0
-    ready = (w_z[0, 0, 0] + w_x[0, 0, 0]) * 0 + mapped_ready
-    w_mid = gather_weight(shard_mid + early)
-    w_ffn = gather_weight(shard_ffn + ready)
-    width_qkv = shard_qkv.shape[1]
-
-    onehot, resid0 = embed_rows(ids_parts, mapped)
+    w_zx = gather_weight(jnp.concatenate([shard_z, shard_qkv, shard_x], axis=1) + early)
+    w_ffn = gather_weight(shard_ffn + early)
+    mapped_ready = (mapped_a[0, 0, 0] + mapped_b[0, 0, 0]) * 0
+
+    onehot, resid0 = embed_rows(ids_parts, mapped_a, mapped_b)
 
     spots = jnp.arange(length, dtype=jnp.int32)
     pos = posb[:, 0]
     rem = remb[:, 0]
 
     u1 = rms_apply(resid0, norm1_gain).astype(low)
-    gate = part_product(u1, w_z, jnp.float32)
-    fed = part_product(u1, w_x, jnp.float32)
+    gate = part_product(u1, w_zx, jnp.float32, columns=inner_width)
+    fed = part_product(u1, w_zx, jnp.float32, first=inner_width + width_qkv)
     first_dt = inner_width + state
     bc = jnp.concatenate([fed[p, :, inner_width:first_dt] for p in range(parts)], axis=1)
     dtr = jnp.concatenate([fed[p, :, first_dt : first_dt + heads_part] for p in range(parts)], 1)
@@ -1251,40 +1254,42 @@
     ssm, scaled, states, squares = mix_forward(
         gate, fed, cols, cumt, conv_full, skip_wide, ggain_full[None], posb, bs, cs, bs.T
     )
+    after_u1 = u1[0, 0] * 0
+    after_fed = fed[0, 0, 0] * 0
+    after_mix = ssm[0, 0, 0] * 0
+    w_back = gather_steps(
+        shard_back + mapped_ready, gather_y_last(), after={2: after_u1, 3: after_fed, 4: after_mix}
+    )
     factor = lax.rsqrt(jnp.sum(squares, axis=1, keepdims=True) / DIN + 1e-05)
     gain_parts = ggain_full.reshape(parts, 1, inner_width)
-    resid1 = part_back(scaled, w_mid, start=resid0, scale=wide128(factor))
+    resid1 = part_back(scaled, w_back, start=resid0, scale=wide128(factor))
 
     u2 = rms_apply(resid1, norm2_gain).astype(low)
-    qkv = part_product(u2, w_mid, low, first=inner_width, columns=width_qkv)
+    qkv = part_product(u2, w_zx, low, first=inner_width, columns=width_qkv)
     attended, logs = attn_forward(qkv, posb)
-    resid2 = part_back(attended, w_mid, first=width_qkv + inner_width, start=resid1)
+    resid2 = part_back(attended, w_back, first=inner_width, start=resid1)
 
     u3 = rms_apply(resid2, norm3_gain).astype(low)
     half = width_in // 2
     gate3, up3, hidden = ffn_forward(u3, w_ffn, half)
     mixed_row = part_back(hidden, w_ffn, first=width_in, start=resid2)
 
-    piece = length // parts
-    mine = lax.dynamic_slice_in_dim(mixed_row, part * piece, piece, 0)
-    theirs = swap(lax.dynamic_slice_in_dim(mixed_row, (1 - part) * piece, piece, 0), None)
-    mixed = join(mine[None], theirs[None], part)
-
     core = my_bit(0)
 
     def half_rows(value, which):
         count = value.shape[0] // 2
         return lax.dynamic_slice_in_dim(value, which * count, count, 0)
 
-    def sum_cores(left_t, right, deps=()):
-        received = swap(part_product(half_rows(left_t, 1 - core), right, low), 0)
+    def sum_cores(left_t, right, before=(), deps=()):
+        sent = part_product(half_rows(left_t, 1 - core), right, low, deps=before)
+        received = swap(sent, 0)
         return part_product(half_rows(left_t, core), right, low, extra=received, deps=deps)
 
     started = ssm[0, 0, 0] * 0
     ended = hidden[0, 0, 0].astype(jnp.float32) * 0
     cot_own = lax.dynamic_index_in_dim(d_out, part, 0, keepdims=False) + ended
     cot_other = lax.dynamic_index_in_dim(d_out, 1 - part, 0, keepdims=False) + started
-    cot = join(cot_own, swap(cot_other, None), part)
+    cot = join(cot_own, swap(cot_other.astype(low), None).astype(jnp.float32), part)
     dm3 = cot.astype(low)
     d_gate_up = ffn_backward(dm3, w_ffn, width_in, gate3, up3)
     quarter = d_gate_up.reshape(2 * parts, length, half)
@@ -1296,7 +1301,7 @@
     cot = cot + back
 
     dm2 = cot.astype(low)
-    d_att = part_product(dm2, w_mid, low, first=width_qkv + inner_width)
+    d_att = part_product(dm2, w_back, low, first=inner_width)
     part_mid = part_product(
         dm2.T, attended, low, place=inner_width + width_qkv, room=inner_width + width_qkv + width_qkv // 3
     )
@@ -1305,12 +1310,12 @@
         qkv, attended, d_att, log_rows, remb, []
     )
     part_mid = part_product(u2.T, d_qkv, low, into=part_mid, place=inner_width)
-    back, d_gain2 = rms_back(resid1, norm2_gain, part_back(d_qkv, w_mid, first=inner_width, deps=[part_mid]))
+    back, d_gain2 = rms_back(resid1, norm2_gain, part_back(d_qkv, w_zx, first=inner_width, deps=[part_mid]))
     cot = cot + back
 
     dm1 = cot.astype(low)
-    d_gn = part_product(dm1, w_mid, jnp.float32, columns=inner_width)
-    part_mid = outer_into(scaled, (cot * factor).astype(low), 1, 0, part_mid.shape[2], into=part_mid)
+    d_gn = part_product(dm1, w_back, jnp.float32, columns=inner_width)
+    part_mid = outer_into(scaled, (cot * factor).astype(low), 1, 0, part_mid.shape[2], into=part_mid, deps=[sum_ffn, d_gn])
     sum_mid = ring_scatter(part_mid.reshape(-1, part_mid.shape[2]))
     gated = ssm * gate * sigmoid(gate)
     cross = jnp.sum(jnp.sum(gated * gain_parts * d_gn, axis=2), axis=0)[:, None]
@@ -1369,8 +1374,8 @@
     )
     part_z = sum_cores(u1_t, d_z)
     part_x = sum_cores(u1_t, d_fed)
-    back_u1 = part_back(d_z, w_z, deps=[part_z, part_x, sum_mid])
-    back_u1 = part_back(d_fed, w_x, start=back_u1)
+    back_u1 = part_back(d_z, w_zx, deps=[part_z, part_x, sum_mid])
+    back_u1 = part_back(d_fed, w_zx, first=inner_width + width_qkv, start=back_u1)
     back, d_gain1 = rms_back(resid0, norm1_gain, back_u1)
     cot = cot + back
 
@@ -1378,12 +1383,41 @@
     columns = columns.transpose(tuple(range(bits - 1, -1, -1)) + (bits, bits + 1))
     grad_ffn = ring_gather(sum_ffn)
     grad_mid = ring_gather(sum_mid)
-    counted = sum_cores(columns.reshape(-1, length), onehot, deps=[grad_ffn])
-    later = (counted[0, 0, 0].astype(jnp.float32) + mixed_row[0, 0]) * 0
+    after_u1 = back_u1[0, 0] * 0
+    piece_z = sum_stages(part_z, x_first()[:1], [after_u1])
+    piece_x = sum_stages(part_x, y_first()[:1], [after_u1])
+    counted = sum_cores(
+        columns.reshape(-1, length), onehot, before=[piece_z, piece_x], deps=[grad_ffn]
+    )
+    width_in_mid = inner_width + width_qkv
+    out_ffn_in = unfold(grad_ffn, ffn_in.shape[1], half)
+    out_ffn_out = refold(grad_ffn, width_in, 2, mixed_row.shape[1], 256)
+    out_mout = refold(grad_mid, 0, 1, inner_width, 256)
+    out_qkv = grad_mid[:, inner_width:width_in_mid].astype(jnp.float32)
+    out_qkv = out_qkv.reshape(out_qkv.shape[0], attn_qkv.shape[1], -1)
+    out_aout = grad_mid[:, width_in_mid:].T.astype(jnp.float32)
+    after_in = out_ffn_in[0, 0, 0] * 0
+    after_ffn = out_ffn_out[0, 0] * 0
+    piece = length // parts
+    mine = lax.dynamic_slice_in_dim(mixed_row, part * piece, piece, 0)
+    theirs = lax.dynamic_slice_in_dim(mixed_row, (1 - part) * piece, piece, 0)
+    theirs = swap(theirs.astype(low), None).astype(jnp.float32)
+    mixed = join(mine[None], theirs[None], part)
     after_theirs = theirs[0, 0] * 0
-    piece_z = sum_stages(part_z, x_first(), [later])
-    piece_x = sum_stages(part_x, y_first(), [later, 0.0, 0.0, after_theirs])
-    counted = sum_stages(counted, y_first())
+    after_mout = out_mout[0, 0] * 0
+
+    def nothing(value):
+        return value[(0,) * value.ndim].astype(jnp.float32) * 0
+
+    extra = [after_in, after_ffn + after_mout, after_theirs]
+    waited = nothing(mixed_row)
+    for turn in range(bits):
+        counted = sum_stages(counted, y_first()[turn : turn + 1], [waited])
+        if turn + 1 < bits:
+            held = extra[turn] + nothing(counted)
+            piece_z = sum_stages(piece_z, x_first()[turn + 1 : turn + 2], [held])
+            piece_x = sum_stages(piece_x, y_first()[turn + 1 : turn + 2], [held])
+            waited = nothing(piece_z) + nothing(piece_x)
     grad_mix = lax.all_gather(
         jnp.concatenate([piece_z, piece_x], axis=1),
         "dp",
@@ -1453,15 +1487,13 @@
         own_half(d_alog),
         own_half(d_skipped),
         own_half(d_ggain),
-        refold(grad_mid, 0, 1, inner_width, 256),
+        out_mout,
         d_gain2,
-        grad_mid[:, inner_width : inner_width + width_qkv]
-        .astype(wide)
-        .reshape(model_width, attn_qkv.shape[1], -1),
-        grad_mid[:, inner_width + width_qkv :].T.astype(wide),
+        out_qkv,
+        out_aout,
         d_gain3,
-        unfold(grad_ffn, ffn_in.shape[1], half),
-        refold(grad_ffn, width_in, 2, model_width, 256),
+        out_ffn_in,
+        out_ffn_out,
     )
 
 

time: 1110 us -> 1070 us (0.964)
  waiting for transfers between devices: 252 us -> 205 us
    ppermute x16, waiting for transfers between devices: 115 us -> 56.8 us  [swap(): return lax.ppermute(value, 'mp', [(0, 1), (1, 0)])]
    ppermute x40, waiting for transfers between devices: 115 us -> 134 us  [swap(): lax.ppermute(value, 'dp', [(i, i ^ 1 << stage) for i in range(count)])]
    unnamed x241 -> x250, local copies, waits for them, and re-layouts: 32.5 us -> 25.9 us
  transfers between devices with their start and end apart: 64 -> 64, of which waited for: 32 -> 36; matrix products, arithmetic and copies ran while one was open for 19% -> 21% of each run, Pallas kernels for 42% -> 42%
where the time goes in v3:
time: 1070 us; the launch traced here: 1060 us
  Pallas kernels  522 us (49%)
  waiting for transfers between devices  205 us (19%)
  other arithmetic  119 us (11%)
  local copies, waits for them, and re-layouts  116 us (11%)
  starting transfers between devices  49.2 us (5%)
  between operations  33.9 us (3%)
  matrix products  15 us (1%)
    pallas_call x14, Pallas kernels, part_product(): pl.pallas_call(body, grid=(parts, count), in_specs=in_specs, out_specs=pl...  136 us
    ppermute x40, waiting for transfers between devices, swap(): lax.ppermute(value, 'dp', [(i, i ^ 1 << stage) for i in range(count)])  134 us
    pallas_call x7, Pallas kernels, part_back(): pl.pallas_call(body, grid=(parts, count), in_specs=in_specs, out_specs=pl...  110 us
    pallas_call x1, Pallas kernels, mix_backward(): pl.pallas_call(mix_bwd_kernel, grid=(groups,), in_specs=[pl.BlockSpec(blo...  60.2 us
    ppermute x16, waiting for transfers between devices, swap(): return lax.ppermute(value, 'mp', [(0, 1), (1, 0)])  56.8 us
    pallas_call x1, Pallas kernels, attn_backward(): pl.pallas_call(attn_bwd_kernel, grid=(groups,), in_specs=[pl.BlockSpec(bl...  38.4 us
    pallas_call x1, Pallas kernels, mix_forward(): pl.pallas_call(mix_fwd_kernel, grid=(groups,), in_specs=[pl.BlockSpec(blo...  38 us
    ppermute x40, starting transfers between devices, swap(): lax.ppermute(value, 'dp', [(i, i ^ 1 << stage) for i in range(count)])  37.9 us
  transfers between devices with their start and end apart: 64, of which 36 were waited for; matrix products, arithmetic and copies ran while one was open for 21% of the time, Pallas kernels for 42%

profile of v3, /device:TPU:0, one launch (start us, length us, event | category | flops | bytes accessed | tf_op | source)
XLA Modules:
  0.0 1059.6 jit_solution(17651184317153952167)
XLA Ops:
  24.2 9.5 collective-permute-done.4
  100.6 20.6 %collective-permute-done.18 = bf16[1,1,1,1,1,64,1536]{6,5,4,3,2,1,0:T(8,128)(2,1)S(1)} collective-permute-done((bf16[1,1,1,1,1,64,1536]{6,5,4,3,2,1,0:T(8,128)(2,1)S(1)}, bf16[1,1,1,1,1,64,1536]{6,5,4,3,2,1,0:T(8,128)(2,1)S(1)}, u32[]{:S(2)}, u32[]{:S(2)}) %collective-permute-start.18) | collective-permute-done | bytes 196640 | tf_op jit(solution)/shard_map/ppermute | solution.py:924
  121.3 10.2 embed_rows.1
  131.5 14.9 %collective-permute-done.19 = bf16[1,2,1,1,1,64,1536]{6,5,4,3,2,1,0:T(8,128)(2,1)S(1)} collective-permute-done((bf16[1,2,1,1,1,64,1536]{6,5,4,3,2,1,0:T(8,128)(2,1)S(1)}, bf16[1,2,1,1,1,64,1536]{6,5,4,3,2,1,0:T(8,128)(2,1)S(1)}, u32[]{:S(2)}, u32[]{:S(2)}) %collective-permute-start.19) | collective-permute-done | bytes 393248 | tf_op jit(solution)/shard_map/ppermute | solution.py:924
  151.8 21.5 %collective-permute-done.20 = bf16[1,2,2,1,1,64,1536]{6,5,4,3,2,1,0:T(8,128)(2,1)S(1)} collective-permute-done((bf16[1,2,2,1,1,64,1536]{6,5,4,3,2,1,0:T(8,128)(2,1)S(1)}, bf16[1,2,2,1,1,64,1536]{6,5,4,3,2,1,0:T(8,128)(2,1)S(1)}, u32[]{:S(2)}, u32[]{:S(2)}) %collective-permute-start.20) | collective-permute-done | bytes 786464 | tf_op jit(solution)/shard_map/ppermute | solution.py:922
  179.3 12.9 %all-gather.8.cloned.1.call-done = bf16[2048,3840]{1,0:T(8,128)(2,1)} async-done(((bf16[64,3840]{1,0:T(8,128)(2,1)}), bf16[2048,3840]{1,0:T(8,128)(2,1)}) %all-gather.8.cloned.1.call-update) | async-done | bytes 15728656 | tf_op jit(solution)/shard_map/all_gather | solution.py:1092
  192.2 13.1 %part_product.15.x_ref = f32[2,1024,1280]{2,1,0:T(8,128)} custom-call(bf16[1024,1024]{1,0:T(8,128)(2,1)} %copy-done.14, bf16[2,1024,3840]{2,1,0:T(8,128)(2,1)} %bitcast.253), custom_call_target="tpu_custom_call" | custom-call | flops 5368709120 | bytes 15728640 | tf_op jit(solution)/shard_map/part_product/pallas_call | solution.py:596
  249.6 38.0 %mix_fwd.1 = (f32[2,1024,1024]{2,1,0:T(8,128)}, bf16[2,1024,1024]{2,1,0:T(8,128)(2,1)}, bf16[4,128,2048]{2,1,0:T(8,128)(2,1)}, f32[1024,128]{1,0:T(8,128)}) custom-call(f32[2,1024,1024]{2,1,0:T(8,128)} %part_product.14.z_ref, f32[2,1024,1280]{2,1,0:T(8,128)} %part_product.15.x_ref, f32[1024,128]{1,0:T(8,128)} %pad_maximum_fusion.15.cols_ref, ...), custom_call_target="tpu_custom_call" | custom-call | flops 20000000000 | bytes 30000000 | tf_op jit(solution)/shard_map/mix_fwd/pallas_call | solution.py:323
  300.7 11.7 %part_back.7.others_0_ = f32[1024,1024]{1,0:T(8,128)} custom-call(bf16[2,1024,1024]{2,1,0:T(8,128)(2,1)} %get-tuple-element.42.left_ref, bf16[2,1024,1536]{2,1,0:T(8,128)(2,1)} %bitcast.266, f32[1024,1024]{1,0:T(8,128)} %get-tuple-element.40.others_0_, f32[1024,128]{1,0:T(8,128)} %broadcast_in_dim.49.others_1_.rg_ref), custom_call_target="tpu_custom_call" | custom-call | flops 4294967296 | bytes 12582912 | tf_op jit(solution)/shard_map/part_back/pallas_call | solution.py:655
  317.5 11.3 %part_product.16.q_ref.k_ref.v_ref = bf16[2,1024,1536]{2,1,0:T(8,128)(2,1)} custom-call(bf16[1024,1024]{1,0:T(8,128)(2,1)} %multiply_convert_fusion.2.left_ref, bf16[2,1024,3840]{2,1,0:T(8,128)(2,1)} %bitcast.255), custom_call_target="tpu_custom_call" | custom-call | flops 6442450944 | bytes 18874368 | tf_op jit(solution)/shard_map/part_product/pallas_call | solution.py:596
  328.9 25.5 %attn_fwd.1 = (bf16[2,1024,512]{2,1,0:T(8,128)(2,1)}, f32[4,1024,128]{2,1,0:T(8,128)}) custom-call(bf16[2,1024,1536]{2,1,0:T(8,128)(2,1)} %part_product.16.q_ref.k_ref.v_ref, bf16[2,1024,1536]{2,1,0:T(8,128)(2,1)} %part_product.16.q_ref.k_ref.v_ref, bf16[2,1024,1536]{2,1,0:T(8,128)(2,1)} %part_product.16.q_ref.k_ref.v_ref, f32[1024,128]{1,0:T(8,128)} %get-tuple-element.39.pos_ref), custom_call_target="tpu_custom_call" | custom-call | flops 30000001024 | bytes 10000000 | tf_op jit(solution)/shard_map/attn_fwd/pallas_call | solution.py:100
  373.5 23.4 %ffn_in.1 = (bf16[2,1024,2048]{2,1,0:T(8,128)(2,1)}, bf16[2,1024,2048]{2,1,0:T(8,128)(2,1)}, bf16[2,1024,2048]{2,1,0:T(8,128)(2,1)}) custom-call(bf16[1024,1024]{1,0:T(8,128)(2,1)} %multiply_convert_fusion.1.left_ref, bf16[2,1024,6144]{2,1,0:T(8,128)(2,1)} %bitcast.261, bf16[2,1024,6144]{2,1,0:T(8,128)(2,1)} %bitcast.262), custom_call_target="tpu_custom_call" | custom-call | flops 17179869184 | bytes 41943040 | tf_op jit(solution)/shard_map/ffn_in/pallas_call | solution.py:752
  404.2 14.6 %outer_into.2.others_0_ = bf16[2,1024,6144]{2,1,0:T(8,128)(2,1)} custom-call(bf16[2,1024,2048]{2,1,0:T(8,128)(2,1)} %get-tuple-element.46.left_ref, bf16[1024,1024]{1,0:T(8,128)(2,1)} %fusion.2.left_ref.right_ref), custom_call_target="tpu_custom_call" | custom-call | flops 8589934592 | bytes 16777216 | tf_op jit(solution)/shard_map/outer_into/pallas_call | solution.py:692
  418.8 22.3 %ffn_back.1 = bf16[2,2,1024,2048]{3,2,1,0:T(8,128)(2,1)} custom-call(bf16[1024,1024]{1,0:T(8,128)(2,1)} %fusion.2.left_ref.right_ref, bf16[2,1024,6144]{2,1,0:T(8,128)(2,1)} %bitcast.263, bf16[2,1024,2048]{2,1,0:T(8,128)(2,1)} %get-tuple-element.47.gate_ref, bf16[2,1024,2048]{2,1,0:T(8,128)(2,1)} %get-tuple-element.48.up_ref), custom_call_target="tpu_custom_call" | custom-call | flops 8589934592 | bytes 41943040 | tf_op jit(solution)/shard_map/ffn_back/pallas_call | solution.py:788
  441.1 25.9 %part_product.17.others_0_ = bf16[2,1024,6144]{2,1,0:T(8,128)(2,1)} custom-call(bf16[1024,1024]{1,0:T(8,128)(2,1)} %copy.206.left_ref, bf16[4,1024,2048]{2,1,0:T(8,128)(2,1)} %bitcast.270, bf16[2,1024,6144]{2,1,0:T(8,128)(2,1)} %outer_into.2.others_0_), custom_call_target="tpu_custom_call", output_to_operand_aliasing={{}: (2, {})} | custom-call | flops 17179869184 | bytes 50331648 | tf_op jit(solution)/shard_map/part_product/pallas_call | solution.py:596
  474.9 31.2 %part_back.10 = f32[1024,1024]{1,0:T(8,128)} custom-call(bf16[4,1024,2048]{2,1,0:T(8,128)(2,1)} %bitcast.271, bf16[2,1024,6144]{2,1,0:T(8,128)(2,1)} %bitcast.264, bf16[2,1024,6144]{2,1,0:T(8,128)(2,1)} %part_product.17.others_0_), custom_call_target="tpu_custom_call" | custom-call | flops 17179869184 | bytes 37748736 | tf_op jit(solution)/shard_map/part_back/pallas_call | solution.py:655
  529.0 38.4 %attn_bwd.1.right_ref.left_ref = bf16[2,1024,1536]{2,1,0:T(8,128)(2,1)} custom-call(bf16[2,1024,1536]{2,1,0:T(8,128)(2,1)} %part_product.16.q_ref.k_ref.v_ref, bf16[2,1024,1536]{2,1,0:T(8,128)(2,1)} %part_product.16.q_ref.k_ref.v_ref, bf16[2,1024,1536]{2,1,0:T(8,128)(2,1)} %part_product.16.q_ref.k_ref.v_ref, ...), custom_call_target="tpu_custom_call" | custom-call | flops 70000001024 | bytes 20000000 | tf_op jit(solution)/shard_map/attn_bwd/pallas_call | solution.py:196
  567.4 11.4 %part_product.20.others_0_ = bf16[2,1024,3072]{2,1,0:T(8,128)(2,1)} custom-call(bf16[1024,1024]{1,0:T(8,128)(2,1)} %copy.209.left_ref, bf16[2,1024,1536]{2,1,0:T(8,128)(2,1)} %attn_bwd.1.right_ref.left_ref, bf16[2,1024,3072]{2,1,0:T(8,128)(2,1)} %part_product.19.others_0_), custom_call_target="tpu_custom_call", output_to_operand_aliasing={{}: (2, {})} | custom-call | flops 6442450944 | bytes 18874368 | tf_op jit(solution)/shard_map/part_product/pallas_call | solution.py:596
  578.8 13.7 %part_back.11 = f32[1024,1024]{1,0:T(8,128)} custom-call(bf16[2,1024,1536]{2,1,0:T(8,128)(2,1)} %attn_bwd.1.right_ref.left_ref, bf16[2,1024,3840]{2,1,0:T(8,128)(2,1)} %bitcast.256, bf16[2,1024,3072]{2,1,0:T(8,128)(2,1)} %part_product.20.others_0_), custom_call_target="tpu_custom_call" | custom-call | flops 6442450944 | bytes 16777216 | tf_op jit(solution)/shard_map/part_back/pallas_call | solution.py:655
  604.1 9.2 part_product.21.others_2_.dgn_ref
  613.3 10.2 outer_into.3.others_0_
  638.5 10.0 multiply_reduce_fusion
  649.5 60.2 %mix_bwd.1 = (bf16[2,1024,1024]{2,1,0:T(8,128)(2,1)}, bf16[2,1024,1280]{2,1,0:T(8,128)(2,1)}, f32[1024,128]{1,0:T(8,128)}, f32[8,2048]{1,0:T(8,128)}, f32[1024,128]{1,0:T(8,128)}, /*index=5*/f32[1024,128]{1,0:T(8,128)}) custom-call(f32[2,1024,1024]{2,1,0:T(8,128)} %part_product.14.z_ref, f32[2,1024,1280]{2,1,0:T(8,128)} %part_product.15.x_ref, ...), custom_call_target="tpu_custom_call" | custom-call | flops 49999998976 | bytes 50000000 | tf_op jit(solution)/shard_map/mix_bwd/pallas_call | solution.py:499
  720.9 9.7 part_product.24
  752.9 10.2 part_product.25.others_1_
  767.7 10.2 part_back.12.others_0_
  777.8 16.5 %part_back.13 = f32[1024,1024]{1,0:T(8,128)} custom-call(bf16[2,1024,1280]{2,1,0:T(8,128)(2,1)} %maximum_dynamic-update-slice_fusion.right_ref.left_ref, bf16[2,1024,3840]{2,1,0:T(8,128)(2,1)} %bitcast.258, f32[1024,1024]{1,0:T(8,128)} %part_back.12.others_0_), custom_call_target="tpu_custom_call" | custom-call | flops 5368709120 | bytes 14680064 | tf_op jit(solution)/shard_map/part_back/pallas_call | solution.py:655
  818.6 18.6 %part_back.9 = f32[1024,1024]{1,0:T(8,128)} custom-call(bf16[2,1024,2048]{2,1,0:T(8,128)(2,1)} %get-tuple-element.46.left_ref, bf16[2,1024,6144]{2,1,0:T(8,128)(2,1)} %bitcast.265, f32[1024,1024]{1,0:T(8,128)} %part_back.8.others_0_), custom_call_target="tpu_custom_call" | custom-call | flops 8589934592 | bytes 20971520 | tf_op jit(solution)/shard_map/part_back/pallas_call | solution.py:655
  856.0 10.3 collective-permute-done.23
  874.6 11.8 %unfold.2 = f32[1024,2,2048]{2,1,0:T(2,128)} custom-call(bf16[1024,6144]{1,0:T(8,128)(2,1)} %all-gather.12.cloned.1.call-done.others_1_.in_ref), custom_call_target="tpu_custom_call" | custom-call | bytes 25165824 | tf_op jit(solution)/shard_map/unfold/pallas_call | solution.py:723
  894.2 11.1 %collective-permute-done.31 = bf16[256,1024]{1,0:T(8,128)(2,1)S(1)} collective-permute-done((bf16[256,1024]{1,0:T(8,128)(2,1)S(1)}, bf16[256,1024]{1,0:T(8,128)(2,1)S(1)}, u32[]{:S(2)}, u32[]{:S(2)}) %collective-permute-start.31) | collective-permute-done | bytes 524320 | tf_op jit(solution)/shard_map/ppermute | solution.py:924
  934.6 10.1 collective-permute-done.37
  (659 shorter events, 457.4 us)
Async XLA Ops:
  7.2 185.0 %all-gather.8.cloned.1.call-start = ((), (), s32[]{:S(2)}) async-start(), calls=%async_computation.2 | async-start | bytes 16220160 | tf_op jit(solution)/shard_map/all_gather | solution.py:1092
  59.8 313.7 %all-gather.10.cloned.1.call-start = ((), (), s32[]{:S(2)}) async-start(), calls=%async_computation.3 | async-start | bytes 25952256 | tf_op jit(solution)/shard_map/all_gather | solution.py:1092
  61.1 552.2 %reduce-scatter.3.cloned.1.call-start = ((), (), s32[]{:S(2)}) async-start(), calls=%async_computation.4 | async-start | bytes 25952256 | tf_op jit(solution)/shard_map/reduce_scatter | solution.py:1021
  63.4 15.0 %collective-permute-start = (s32[512,8]{0,1:T(8,128)S(1)}, s32[512,8]{0,1:T(8,128)S(1)}, u32[]{:S(2)}, u32[]{:S(2)}) collective-permute-start(s32[512,8]{0,1:T(8,128)S(1)} %dynamic-slice_bitcast_fusion.3), channel_id=1, source_target_pairs={{0,1},{1,0},{2,3},{3,2},{4,5},{5,4},{6,7},{7,6},{8,9},{9,8},{10,11... | collective-permute-start | bytes 49160 | tf_op jit(solution)/shard_map/ppermute | solution.py:922
  78.3 15.4 %collective-permute-start.11 = (bf16[2,2,2,1,1,64,512]{6,5,4,3,2,1,0:T(8,128)(2,1)S(1)}, bf16[2,2,2,1,1,64,512]{6,5,4,3,2,1,0:T(8,128)(2,1)}, u32[]{:S(2)}, u32[]{:S(2)}) collective-permute-start(bf16[2,2,2,1,1,64,512]{6,5,4,3,2,1,0:T(8,128)(2,1)S(1)} %pad_maximum_fusion.13), channel_id=1, source_target_pairs={{0,4},{2,6},{4,0},{6,2},{8,12},{10,14},{12,8},{14,10},{16,20},{18,... | collective-permute-start | bytes 1572872 | tf_op jit(solution)/shard_map/ppermute | solution.py:924
  100.1 21.1 %collective-permute-start.18 = (bf16[1,1,1,1,1,64,1536]{6,5,4,3,2,1,0:T(8,128)(2,1)S(1)}, bf16[1,1,1,1,1,64,1536]{6,5,4,3,2,1,0:T(8,128)(2,1)S(1)}, u32[]{:S(2)}, u32[]{:S(2)}) collective-permute-start(bf16[1,1,1,1,1,64,1536]{6,5,4,3,2,1,0:T(8,128)(2,1)S(1)} %maximum_add_fusion.2), channel_id=1, source_target_pairs={{0,16},{2,18},{4,20},{6,22},{8,24},{10,26},{12,28},{14,30},{16,0},... | collective-permute-start | bytes 589832 | tf_op jit(solution)/shard_map/ppermute | solution.py:924
  121.2 25.2 %collective-permute-start.19 = (bf16[1,2,1,1,1,64,1536]{6,5,4,3,2,1,0:T(8,128)(2,1)S(1)}, bf16[1,2,1,1,1,64,1536]{6,5,4,3,2,1,0:T(8,128)(2,1)S(1)}, u32[]{:S(2)}, u32[]{:S(2)}) collective-permute-start(bf16[1,2,1,1,1,64,1536]{6,5,4,3,2,1,0:T(8,128)(2,1)S(1)} %pad_maximum_fusion.17), channel_id=1, source_target_pairs={{0,8},{2,10},{4,12},{6,14},{8,0},{10,2},{12,4},{14,6},{16,24},{18,... | collective-permute-start | bytes 1179656 | tf_op jit(solution)/shard_map/ppermute | solution.py:924
  146.6 26.7 %collective-permute-start.20 = (bf16[1,2,2,1,1,64,1536]{6,5,4,3,2,1,0:T(8,128)(2,1)S(1)}, bf16[1,2,2,1,1,64,1536]{6,5,4,3,2,1,0:T(8,128)(2,1)S(1)}, u32[]{:S(2)}, u32[]{:S(2)}) collective-permute-start(bf16[1,2,2,1,1,64,1536]{6,5,4,3,2,1,0:T(8,128)(2,1)S(1)} %pad_maximum_fusion.11), channel_id=1, source_target_pairs={{0,1},{1,0},{2,3},{3,2},{4,5},{5,4},{6,7},{7,6},{8,9},{9,8},{10,11... | collective-permute-start | bytes 2359304 | tf_op jit(solution)/shard_map/ppermute | solution.py:922
  174.7 40.5 %collective-permute-start.21 = (bf16[2,2,2,1,1,64,1536]{6,5,4,3,2,1,0:T(8,128)(2,1)}, bf16[2,2,2,1,1,64,1536]{6,5,4,3,2,1,0:T(8,128)(2,1)}, u32[]{:S(2)}, u32[]{:S(2)}) collective-permute-start(bf16[2,2,2,1,1,64,1536]{6,5,4,3,2,1,0:T(8,128)(2,1)} %pad_maximum_fusion.7), channel_id=1, source_target_pairs={{0,4},{2,6},{4,0},{6,2},{8,12},{10,14},{12,8},{14,10},{16,20},{18,... | collective-permute-start | bytes 4718600 | tf_op jit(solution)/shard_map/ppermute | solution.py:924
  218.9 75.4 %collective-permute-start.22 = (bf16[2,2,2,2,1,64,1536]{6,5,4,3,2,1,0:T(8,128)(2,1)}, bf16[2,2,2,2,1,64,1536]{6,5,4,3,2,1,0:T(8,128)(2,1)}, u32[]{:S(2)}, u32[]{:S(2)}) collective-permute-start(bf16[2,2,2,2,1,64,1536]{6,5,4,3,2,1,0:T(8,128)(2,1)} %pad_maximum_fusion.3), channel_id=1, source_target_pairs={{0,2},{2,0},{4,6},{6,4},{8,10},{10,8},{12,14},{14,12},{16,18},{18,... | collective-permute-start | bytes 9437192 | tf_op jit(solution)/shard_map/ppermute | solution.py:924
  293.5 105.2 %collective-permute-start.24 = (bf16[512,1024]{1,0:T(8,128)(2,1)}, bf16[512,1024]{1,0:T(8,128)(2,1)}, u32[]{:S(2)}, u32[]{:S(2)}) collective-permute-start(bf16[512,1024]{1,0:T(8,128)(2,1)} %fusion.12), channel_id=1, source_target_pairs={{0,1},{1,0},{2,3},{3,2},{4,5},{5,4},{6,7},{7,6},{8,9},{9,8},{10,11... | collective-permute-start | bytes 3145736 | tf_op jit(solution)/shard_map/ppermute | solution.py:922
  467.0 263.5 %reduce-scatter.5.cloned.1.call-start = ((), (), s32[]{:S(2)}) async-start(), calls=%async_computation.5 | async-start | bytes 12976128 | tf_op jit(solution)/shard_map/reduce_scatter | solution.py:1021
  623.5 217.1 %all-gather.12.cloned.1.call-start = ((), (), s32[]{:S(2)}) async-start(), calls=%async_computation.6 | async-start | bytes 13369344 | tf_op jit(solution)/shard_map/all_gather | solution.py:1031
  624.1 286.3 %all-gather.14.cloned.1.call-start = ((), (), s32[]{:S(2)}) async-start(), calls=%async_computation.7 | async-start | bytes 6684672 | tf_op jit(solution)/shard_map/all_gather | solution.py:1031
  730.6 22.4 %collective-permute-start.26 = (bf16[2,512,1280]{2,1,0:T(8,128)(2,1)}, bf16[2,512,1280]{2,1,0:T(8,128)(2,1)}, u32[]{:S(2)}, u32[]{:S(2)}) collective-permute-start(bf16[2,512,1280]{2,1,0:T(8,128)(2,1)} %part_product.24), channel_id=1, source_target_pairs={{0,2},{2,0},{4,6},{6,4},{8,10},{10,8},{12,14},{14,12},{16,18},{18,... | collective-permute-start | bytes 7864328 | tf_op jit(solution)/shard_map/ppermute | solution.py:924
  730.6 298.2 %all-gather.18.cloned.1.call-start = ((), (), s32[]{:S(2)}) async-start(), calls=%async_computation.9 | async-start | bytes 2228224 | tf_op jit(solution)/shard_map/all_gather | solution.py:1000
  751.4 55.2 %collective-permute-start.27 = (bf16[512,1024]{1,0:T(8,128)(2,1)}, bf16[512,1024]{1,0:T(8,128)(2,1)}, u32[]{:S(2)}, u32[]{:S(2)}) collective-permute-start(bf16[512,1024]{1,0:T(8,128)(2,1)} %dynamic-slice_bitcast_fusion), channel_id=1, source_target_pairs={{0,1},{1,0},{2,3},{3,2},{4,5},{5,4},{6,7},{7,6},{8,9},{9,8},{10,11... | collective-permute-start | bytes 3145736 | tf_op jit(solution)/shard_map/ppermute | solution.py:922
  765.7 45.4 %collective-permute-start.28 = (bf16[2,256,1280]{2,1,0:T(8,128)(2,1)}, bf16[2,256,1280]{2,1,0:T(8,128)(2,1)S(1)}, u32[]{:S(2)}, u32[]{:S(2)}) collective-permute-start(bf16[2,256,1280]{2,1,0:T(8,128)(2,1)} %constant_dynamic-slice_fusion.14), channel_id=1, source_target_pairs={{0,4},{2,6},{4,0},{6,2},{8,12},{10,14},{12,8},{14,10},{16,20},{18,... | collective-permute-start | bytes 3932168 | tf_op jit(solution)/shard_map/ppermute | solution.py:924
  818.6 22.0 %collective-permute-start.29 = (bf16[2,512,1024]{2,1,0:T(8,128)(2,1)}, bf16[2,512,1024]{2,1,0:T(8,128)(2,1)S(1)}, u32[]{:S(2)}, u32[]{:S(2)}) collective-permute-start(bf16[2,512,1024]{2,1,0:T(8,128)(2,1)} %part_product.26), channel_id=1, source_target_pairs={{0,2},{2,0},{4,6},{6,4},{8,10},{10,8},{12,14},{14,12},{16,18},{18,... | collective-permute-start | bytes 6291464 | tf_op jit(solution)/shard_map/ppermute | solution.py:924
  840.0 26.3 %collective-permute-start.23 = (bf16[512,1024]{1,0:T(8,128)(2,1)}, bf16[512,1024]{1,0:T(8,128)(2,1)}, u32[]{:S(2)}, u32[]{:S(2)}) collective-permute-start(bf16[512,1024]{1,0:T(8,128)(2,1)} %dynamic-slice_convert_fusion), channel_id=1, source_target_pairs={{0,1},{1,0},{2,3},{3,2},{4,5},{5,4},{6,7},{7,6},{8,9},{9,8},{10,11... | collective-permute-start | bytes 3145736 | tf_op jit(solution)/shard_map/ppermute | solution.py:922
  849.8 39.9 %collective-permute-start.30 = (bf16[2,256,1024]{2,1,0:T(8,128)(2,1)S(1)}, bf16[2,256,1024]{2,1,0:T(8,128)(2,1)S(1)}, u32[]{:S(2)}, u32[]{:S(2)}) collective-permute-start(bf16[2,256,1024]{2,1,0:T(8,128)(2,1)S(1)} %constant_dynamic-slice_fusion.13), channel_id=1, source_target_pairs={{0,4},{2,6},{4,0},{6,2},{8,12},{10,14},{12,8},{14,10},{16,20},{18,... | collective-permute-start | bytes 3145736 | tf_op jit(solution)/shard_map/ppermute | solution.py:924
  852.4 39.9 %collective-permute-start.32 = (bf16[256,1280]{1,0:T(8,128)(2,1)}, bf16[256,1280]{1,0:T(8,128)(2,1)}, u32[]{:S(2)}, u32[]{:S(2)}) collective-permute-start(bf16[256,1280]{1,0:T(8,128)(2,1)} %dynamic-slice_bitcast_fusion.1), channel_id=1, source_target_pairs={{0,1},{1,0},{2,3},{3,2},{4,5},{5,4},{6,7},{7,6},{8,9},{9,8},{10,11... | collective-permute-start | bytes 1966088 | tf_op jit(solution)/shard_map/ppermute | solution.py:922
  887.6 17.7 %collective-permute-start.31 = (bf16[256,1024]{1,0:T(8,128)(2,1)S(1)}, bf16[256,1024]{1,0:T(8,128)(2,1)S(1)}, u32[]{:S(2)}, u32[]{:S(2)}) collective-permute-start(bf16[256,1024]{1,0:T(8,128)(2,1)S(1)} %constant_dynamic-slice_fusion.12), channel_id=1, source_target_pairs={{0,4},{2,6},{4,0},{6,2},{8,12},{10,14},{12,8},{14,10},{16,20},{18,... | collective-permute-start | bytes 1572872 | tf_op jit(solution)/shard_map/ppermute | solution.py:924
  890.7 18.9 %collective-permute-start.33 = (bf16[256,1024]{1,0:T(8,128)(2,1)S(1)}, bf16[256,1024]{1,0:T(8,128)(2,1)S(1)}, u32[]{:S(2)}, u32[]{:S(2)}) collective-permute-start(bf16[256,1024]{1,0:T(8,128)(2,1)S(1)} %dynamic-slice_bitcast_fusion.2), channel_id=1, source_target_pairs={{0,1},{1,0},{2,3},{3,2},{4,5},{5,4},{6,7},{7,6},{8,9},{9,8},{10,11... | collective-permute-start | bytes 1572872 | tf_op jit(solution)/shard_map/ppermute | solution.py:922
  907.4 17.0 %collective-permute-start.34 = (bf16[128,1024]{1,0:T(8,128)(2,1)S(1)}, bf16[128,1024]{1,0:T(8,128)(2,1)}, u32[]{:S(2)}, u32[]{:S(2)}) collective-permute-start(bf16[128,1024]{1,0:T(8,128)(2,1)S(1)} %constant_dynamic-slice_fusion.11), channel_id=1, source_target_pairs={{0,8},{2,10},{4,12},{6,14},{8,0},{10,2},{12,4},{14,6},{16,24},{18,... | collective-permute-start | bytes 786440 | tf_op jit(solution)/shard_map/ppermute | solution.py:924
  907.5 16.2 %collective-permute-start.35 = (bf16[128,1280]{1,0:T(8,128)(2,1)S(1)}, bf16[128,1280]{1,0:T(8,128)(2,1)S(1)}, u32[]{:S(2)}, u32[]{:S(2)}) collective-permute-start(bf16[128,1280]{1,0:T(8,128)(2,1)S(1)} %constant_dynamic-slice_fusion.10), channel_id=1, source_target_pairs={{0,8},{2,10},{4,12},{6,14},{8,0},{10,2},{12,4},{14,6},{16,24},{18,... | collective-permute-start | bytes 983048 | tf_op jit(solution)/shard_map/ppermute | solution.py:924
  910.3 17.4 %collective-permute-start.36 = (bf16[128,1024]{1,0:T(8,128)(2,1)S(1)}, bf16[128,1024]{1,0:T(8,128)(2,1)}, u32[]{:S(2)}, u32[]{:S(2)}) collective-permute-start(bf16[128,1024]{1,0:T(8,128)(2,1)S(1)} %constant_dynamic-slice_fusion.9), channel_id=1, source_target_pairs={{0,8},{2,10},{4,12},{6,14},{8,0},{10,2},{12,4},{14,6},{16,24},{18,... | collective-permute-start | bytes 786440 | tf_op jit(solution)/shard_map/ppermute | solution.py:924
  931.6 21.2 %collective-permute-start.39 = (bf16[64,1024]{1,0:T(8,128)(2,1)S(1)}, bf16[64,1024]{1,0:T(8,128)(2,1)S(1)}, u32[]{:S(2)}, u32[]{:S(2)}) collective-permute-start(bf16[64,1024]{1,0:T(8,128)(2,1)S(1)} %constant_dynamic-slice_fusion.6), channel_id=1, source_target_pairs={{0,16},{2,18},{4,20},{6,22},{8,24},{10,26},{12,28},{14,30},{16,0},... | collective-permute-start | bytes 393224 | tf_op jit(solution)/shard_map/ppermute | solution.py:924
  933.6 17.2 %collective-permute-start.38 = (bf16[64,1280]{1,0:T(8,128)(2,1)S(1)}, bf16[64,1280]{1,0:T(8,128)(2,1)S(1)}, u32[]{:S(2)}, u32[]{:S(2)}) collective-permute-start(bf16[64,1280]{1,0:T(8,128)(2,1)S(1)} %constant_dynamic-slice_fusion.7), channel_id=1, source_target_pairs={{0,16},{2,18},{4,20},{6,22},{8,24},{10,26},{12,28},{14,30},{16,0},... | collective-permute-start | bytes 491528 | tf_op jit(solution)/shard_map/ppermute | solution.py:924
  953.5 77.4 %all-gather.16.cloned.1.call-start = ((), (), s32[]{:S(2)}) async-start(), calls=%async_computation.8 | async-start | bytes 5013504 | tf_op jit(solution)/shard_map/all_gather | solution.py:1421
  1008.8 18.7 %collective-permute-start.49 = (f32[128,1024]{1,0:T(8,128)S(1)}, f32[128,1024]{1,0:T(8,128)S(1)}, u32[]{:S(2)}, u32[]{:S(2)}) collective-permute-start(f32[128,1024]{1,0:T(8,128)S(1)} %pad_maximum_fusion.16), channel_id=1, source_target_pairs={{0,2},{2,0},{4,6},{6,4},{8,10},{10,8},{12,14},{14,12},{16,18},{18,... | collective-permute-start | bytes 1572872 | tf_op jit(solution)/shard_map/ppermute | solution.py:924
  1031.9 18.6 %collective-permute-start.55 = (bf16[1024,128]{1,0:T(8,128)(2,1)S(1)}, bf16[1024,128]{1,0:T(8,128)(2,1)S(1)}, u32[]{:S(2)}, u32[]{:S(2)}) collective-permute-start(bf16[1024,128]{1,0:T(8,128)(2,1)S(1)} %slice.571), channel_id=1, source_target_pairs={{0,1},{1,0},{2,3},{3,2},{4,5},{5,4},{6,7},{7,6},{8,9},{9,8},{10,11... | collective-permute-start | bytes 786440 | tf_op jit(solution)/shard_map/ppermute | solution.py:922
  (143 other events, 2172.1 us)
Sparse Core Ops, SparseCore 0:
  59.9 132.2 all-gather.7
  195.1 175.8 all-gather.9
  467.1 138.3 reduce-scatter.2
  623.6 100.1 reduce-scatter.4
  725.2 98.7 all-gather.11
  825.4 72.4 all-gather.13
  953.6 32.3 all-gather.17
  988.1 36.5 all-gather.15
